TPU v7x, 512 devices: a whole 4x8x8 slice. The times are simulated.
512 devices in a mesh: ctx: 64 (over y, z), ch: 8 (over x, core).
Axes of the slice: x: 4, y: 8, z: 8, core: 2. Of those that a mesh axis runs over, the one named last changes fastest.
Arguments:
- query_field: bfloat16 [8192, 4096], P('ctx', 'ch'), may hold values from -6 to 6
- key_field: bfloat16 [8192, 4096], P('ctx', 'ch'), may hold values from -6 to 6
- value_field: bfloat16 [8192, 4096], P('ctx', 'ch'), may hold values from -6 to 6
- short_taps: float32 [3, 7, 4096], P(None, None, 'ch'), may hold values from -2 to 2
- filt_in: float32 [33, 64], replicated, may hold values from -1 to 1
- filt_mid: float32 [64, 64], replicated, may hold values from -0.75 to 0.75
- filt_out: float32 [64, 4096], P(None, 'ch'), may hold values from -0.75 to 0.75
- decay_rate: float32 [4096], P('ch'), may hold values from 3.0517578e-05 to 0.041666668
- skip_gain: float32 [4096], P('ch'), may hold values from -4 to 4
- out_weight: bfloat16 [4096, 2048], P('ch'), may hold values from -0.09375 to 0.09375
Outputs:
- projected: bfloat16 [8192, 2048], P(('ctx', 'ch'))
All inputs are finite; a program needn't handle non-finite values.
Results may differ from a plain program's by a relative error of at most 0.017.
Values may be sent and summed in bfloat16 or wider, within the bound.
No kernel may reach another device: no remote copies, remote signals or barrier semaphores. Data moves between devices by JAX's collectives and lax.ppermute only.
A program may use at most 64 MiB of HBM per device.

v0:
```python
import math

import jax
import jax.numpy as jnp
from jax import lax
from jax.sharding import PartitionSpec as P

RADIX = 128


highest = lax.Precision.HIGHEST


def shifted(value, axis, steps):
    count = lax.axis_size(axis)
    leading, last = (max(0, -steps), min(count, count - steps))
    return lax.ppermute(value, axis, [(source, source + steps) for source in range(leading, last)])


def position_features(tokens, band_count):
    steps_t = jnp.arange(tokens, dtype=jnp.int32)
    band_ids = jnp.arange(band_count, dtype=jnp.int32)
    frequency = 1 + band_ids * band_ids * (tokens // 4 - 1) // ((band_count - 1) * (band_count - 1))
    phase_idx = frequency[:, None] * steps_t[None, :] % tokens
    angles = phase_idx.astype(jnp.float32) * (2.0 * math.pi / tokens)
    ramp_time = (steps_t.astype(jnp.float32) / tokens)[None, :]
    return jnp.concatenate([ramp_time, jnp.cos(angles), jnp.sin(angles)], 0)


def short_mix(padded, taps_set, lead_rows):
    length = padded.shape[2] - lead_rows
    running = jnp.zeros(padded.shape[:2] + (length,), jnp.float32)
    for tap_pos in range(lead_rows + 1):
        window = padded[:, :, lead_rows - tap_pos : lead_rows - tap_pos + length].astype(
            jnp.float32
        )
        running = running + taps_set[:, tap_pos, :, None] * window
    return running.astype(jnp.bfloat16)


def angle_table(row_count, col_count, modulus):
    index_grid = (
        jnp.arange(row_count, dtype=jnp.int32)[:, None]
        * jnp.arange(col_count, dtype=jnp.int32)[None, :]
        % modulus
    )
    angles = index_grid.astype(jnp.float32) * (2.0 * math.pi / modulus)
    return (jnp.cos(angles), jnp.sin(angles))


def einsum_high(form, left_arr, right_arr):
    return jnp.einsum(
        form, left_arr, right_arr, precision=highest, preferred_element_type=jnp.float32
    )


def forward_dft(signal, tables):
    cos_long, sin_long, cos_short, sin_short, twiddle_cos, twiddle_sin = tables
    section_re = einsum_high("kn,cnp->ckp", cos_long, signal)
    section_im = -einsum_high("kn,cnp->ckp", sin_long, signal)
    turned_re = section_re * twiddle_cos + section_im * twiddle_sin
    turned_im = section_im * twiddle_cos - section_re * twiddle_sin
    spec_re = einsum_high("ckn,nm->ckm", turned_re, cos_short) + einsum_high(
        "ckn,nm->ckm", turned_im, sin_short
    )
    spec_im = einsum_high("ckn,nm->ckm", turned_im, cos_short) - einsum_high(
        "ckn,nm->ckm", turned_re, sin_short
    )
    return (spec_re, spec_im)


def inverse_dft(spec_re, spec_im, tables, points):
    cos_long, sin_long, cos_short, sin_short, twiddle_cos, twiddle_sin = tables
    back_re = einsum_high("ckn,nm->ckm", spec_re, cos_short) - einsum_high(
        "ckn,nm->ckm", spec_im, sin_short
    )
    back_im = einsum_high("ckn,nm->ckm", spec_im, cos_short) + einsum_high(
        "ckn,nm->ckm", spec_re, sin_short
    )
    turned_re = back_re * twiddle_cos - back_im * twiddle_sin
    turned_im = back_re * twiddle_sin + back_im * twiddle_cos
    signal = einsum_high("nk,ckp->cnp", cos_long, turned_re) - einsum_high(
        "nk,ckp->cnp", sin_long, turned_im
    )
    return signal / points


def regroup_forward(fields):
    return lax.all_to_all(fields, "ctx", split_axis=1, concat_axis=2, tiled=True)


def regroup_back(gated_out):
    return lax.all_to_all(gated_out, "ctx", split_axis=1, concat_axis=0, tiled=True)


def per_device(
    query_field,
    key_field,
    value_field,
    short_taps,
    filt_in,
    filt_mid,
    filt_out,
    decay_rate,
    skip_gain,
    out_weight,
):
    ctx_count = lax.axis_size("ctx")
    my_index = lax.axis_index("ctx")
    tok_local = query_field.shape[0]
    chan_local = query_field.shape[1]
    chan_mine = chan_local // ctx_count
    tokens = tok_local * ctx_count
    lead_rows = short_taps.shape[1] - 1
    offset = my_index * chan_mine
    stacked = jnp.transpose(jnp.stack([query_field, key_field, value_field], 0), (0, 2, 1))
    prior_rows = shifted(stacked[:, :, tok_local - lead_rows :], "ctx", 1)
    filtered = short_mix(jnp.concatenate([prior_rows, stacked], 2), short_taps, lead_rows)
    fields = regroup_forward(filtered)
    features = position_features(tokens, (filt_in.shape[0] - 1) // 2)
    layer_one = jnp.sin(
        jnp.dot(filt_in.T, features, precision=highest, preferred_element_type=jnp.float32)
    )
    layer_two = jnp.sin(
        jnp.dot(filt_mid.T, layer_one, precision=highest, preferred_element_type=jnp.float32)
    )
    out_mine = lax.dynamic_slice_in_dim(filt_out, offset, chan_mine, 1)
    shape_rows = jnp.dot(
        out_mine.T, layer_two, precision=highest, preferred_element_type=jnp.float32
    )
    rates_mine = lax.dynamic_slice_in_dim(decay_rate, offset, chan_mine, 0)
    ramp_time = jnp.arange(tokens, dtype=jnp.int32).astype(jnp.float32)
    long_filter = (
        jnp.sqrt(2.0 * rates_mine)[:, None]
        * jnp.exp(-rates_mine[:, None] * ramp_time[None, :])
        * shape_rows
    )
    product = fields[1].astype(jnp.float32) * fields[2].astype(jnp.float32)
    points = 2 * tokens
    long_len = points // RADIX
    cos_long, sin_long = angle_table(long_len, long_len, long_len)
    cos_short, sin_short = angle_table(RADIX, RADIX, RADIX)
    twiddle_cos, twiddle_sin = angle_table(long_len, RADIX, points)
    tables = (cos_long, sin_long, cos_short, sin_short, twiddle_cos, twiddle_sin)
    both_signals = jnp.concatenate([product, long_filter], 0)
    both_signals = jnp.pad(both_signals, ((0, 0), (0, points - tokens))).reshape(
        2 * chan_mine, long_len, RADIX
    )
    spec_re, spec_im = forward_dft(both_signals, tables)
    prod_re, filt_re = (spec_re[:chan_mine], spec_re[chan_mine:])
    prod_im, filt_im = (spec_im[:chan_mine], spec_im[chan_mine:])
    mixed_re = prod_re * filt_re - prod_im * filt_im
    mixed_im = prod_re * filt_im + prod_im * filt_re
    convolved = inverse_dft(mixed_re, mixed_im, tables, points).reshape(chan_mine, points)[
        :, :tokens
    ]
    skip_mine = lax.dynamic_slice_in_dim(skip_gain, offset, chan_mine, 0)
    gated_out = (fields[0].astype(jnp.float32) * (convolved + skip_mine[:, None] * product)).astype(
        jnp.bfloat16
    )
    returned = regroup_back(gated_out)
    return lax.psum_scatter(
        lax.dot_general(
            returned, out_weight, (((0,), (0,)), ((), ())), preferred_element_type=jnp.float32
        ).astype(jnp.bfloat16),
        "ch",
        scatter_dimension=0,
        tiled=True,
    )


def solution(mesh):
    return jax.shard_map(
        per_device,
        mesh=mesh,
        in_specs=(
            P("ctx", "ch"),
            P("ctx", "ch"),
            P("ctx", "ch"),
            P(None, None, "ch"),
            P(),
            P(),
            P(None, "ch"),
            P("ch"),
            P("ch"),
            P("ch", None),
        ),
        out_specs=P(("ctx", "ch"), None),
        check_vma=False,
    )
```

profile of v0, /device:TPU:1, one launch (start us, length us, event | category | flops | bytes accessed | tf_op | source)
XLA Modules:
  0.0 138.3 jit_solution(6888887935113325947)
XLA Ops:
  6.5 1.2 maximum_bitcast_fusion
  7.8 4.8 %collective-permute-start = (bf16[3,512,6]{1,2,0:T(8,128)(2,1)S(1)}, bf16[3,512,6]{1,2,0:T(8,128)(2,1)S(1)}, u32[]{:S(2)}, u32[]{:S(2)}) collective-permute-start(bf16[3,512,6]{1,2,0:T(8,128)(2,1)S(1)} %slice.91), channel_id=1, source_target_pairs={{0,8},{8,16},{16,24},{24,32},{32,40},{40,48},{48,56},{56,64},{64,7... | collective-permute-start | bytes 55304 | tf_op jit(solution)/shard_map/ppermute | solution.py:17
  12.7 2.1 %fusion.36 = (f32[16,8192]{1,0:T(8,128)S(1)}, f32[16,8192]{1,0:T(8,128)S(1)}) fusion(s32[16]{0:T(128)S(1)} %fusion.81), kind=kLoop, calls=%fused_computation.69 | loop fusion | flops 1835008 | bytes 1048640 | tf_op jit(solution)/shard_map/cos | solution.py:27
  14.8 1.2 fusion.132
  16.1 10.8 %convolution_sine_fusion.1 = f32[8192,64]{0,1:T(8,128)} fusion(f32[33,64]{1,0:T(8,128)S(1)} %copy-done.2, f32[16,8192]{1,0:T(8,128)S(1)} %get-tuple-element.17, f32[16,8192]{1,0:T(8,128)S(1)} %get-tuple-element.16, f32[1,8192]{1,0:T(1,128)S(1)} %convert_multiply_fusion), kind=kOutput, calls=%fused_computation.1 | convolution fusion | flops 208158720 | bytes 3186944 | tf_op jit(solution)/shard_map/dot_general | solution.py:122
  27.9 1.1 copy.59
  28.9 15.4 %all-to-all-start = ((bf16[3,512,128]{2,0,1:T(4,128)(2,1)}), bf16[3,512,128]{2,0,1:T(4,128)(2,1)S(1)}, u32[]{:S(2)}, u32[]{:S(2)}) async-start(bf16[3,512,128]{2,0,1:T(4,128)(2,1)} %copy.59), calls=%async_computation | async-start | bytes 1048576 | tf_op jit(solution)/shard_map/all_to_all | solution.py:89
  46.2 11.2 %convolution_sine_fusion = f32[8192,64]{0,1:T(8,128)S(1)} fusion(f32[8192,64]{0,1:T(8,128)} %convolution_sine_fusion.1, f32[64,64]{1,0:T(8,128)S(1)} %copy-done.1), kind=kOutput, calls=%fused_computation | convolution fusion | flops 402653184 | bytes 4210688 | tf_op jit(solution)/shard_map/dot_general | solution.py:125
  57.4 1.9 %convolution_multiply_fusion = f32[8,8192]{1,0:T(8,128)S(1)} fusion(f32[8192,64]{0,1:T(8,128)S(1)} %convolution_sine_fusion, f32[8192]{0:T(1024)S(1)} %iota_convert_fusion, f32[8]{0:T(128)S(1)} %get-tuple-element.15, f32[8]{0:T(128)S(1)} %get-tuple-element.14, f32[64,512]{1,0:T(8,128)} %param.16, s32[]{:T(128)S(6)} %select_n.80), kind=kOutput, calls=%fused_computation.2 | convolution fusion | flops 50528256 | bytes 2424900 | tf_op jit(solution)/shard_map/dot_general | solution.py:128
  59.3 1.4 all-to-all-done
  61.1 1.9 %convolution_bitcast_fusion = f32[16,128,128]{1,2,0:T(8,128)S(1)} fusion(f32[16,128,128]{2,1,0:T(8,128)S(1)} %bitcast.88), kind=kOutput, calls=%fused_computation.8 | convolution fusion | flops 402882560 | bytes 2097152 | tf_op jit(solution)/shard_map/kn,cnp->ckp/dot_general | solution.py:52
  63.0 1.9 %fusion = f32[16,128,128]{1,2,0:T(8,128)S(1)} fusion(f32[16,128,128]{2,1,0:T(8,128)S(1)} %bitcast.89), kind=kOutput, calls=%fused_computation.7 | convolution fusion | flops 403144704 | bytes 2097152 | tf_op jit(solution)/shard_map/kn,cnp->ckp/dot_general | solution.py:52
  64.9 2.0 %fusion.28 = f32[16,128,128]{2,1,0:T(8,128)S(1)} fusion(f32[16,128,128]{1,2,0:T(8,128)S(1)} %convolution_bitcast_fusion, f32[16,128,128]{1,2,0:T(8,128)S(1)} %fusion, f32[128,128]{0,1:T(8,128)S(1)} %copy.64, f32[128,128]{0,1:T(8,128)S(1)} %copy.62), kind=kOutput, calls=%fused_computation.60 | convolution fusion | flops 403668992 | bytes 3276800 | tf_op jit(solution)/shard_map/ckn,nm->ckm/dot_general | solution.py:52
  66.9 2.0 %fusion.27 = f32[16,128,128]{2,1,0:T(8,128)S(1)} fusion(f32[16,128,128]{1,2,0:T(8,128)S(1)} %fusion, f32[16,128,128]{1,2,0:T(8,128)S(1)} %convolution_bitcast_fusion, f32[128,128]{0,1:T(8,128)S(1)} %copy.64, f32[128,128]{0,1:T(8,128)S(1)} %copy.62), kind=kOutput, calls=%fused_computation.59 | convolution fusion | flops 403668992 | bytes 3276800 | tf_op jit(solution)/shard_map/ckn,nm->ckm/dot_general | solution.py:52
  68.9 2.0 %convolution_subtract_fusion = f32[16,128,128]{2,1,0:T(8,128)S(1)} fusion(f32[16,128,128]{2,1,0:T(8,128)S(1)} %fusion.28, f32[16,128,128]{1,2,0:T(8,128)S(1)} %fusion, f32[16,128,128]{1,2,0:T(8,128)S(1)} %convolution_bitcast_fusion, f32[128,128]{0,1:T(8,128)S(1)} %copy.64, f32[128,128]{0,1:T(8,128)S(1)} %copy.62), kind=kOutput, calls=%fused_computation.4 | convolution fusion | flops 403931136 | bytes 4325376 | tf_op jit(solution)/shard_map/ckn,nm->ckm/dot_general | solution.py:52
  71.0 2.2 %convolution_add_fusion = f32[16,128,128]{2,1,0:T(8,128)S(1)} fusion(f32[16,128,128]{2,1,0:T(8,128)S(1)} %fusion.27, f32[16,128,128]{1,2,0:T(8,128)S(1)} %convolution_bitcast_fusion, f32[16,128,128]{1,2,0:T(8,128)S(1)} %fusion, f32[128,128]{0,1:T(8,128)S(1)} %copy.64, f32[128,128]{0,1:T(8,128)S(1)} %copy.62), kind=kOutput, calls=%fused_computation.5 | convolution fusion | flops 403931136 | bytes 4325376 | tf_op jit(solution)/shard_map/ckn,nm->ckm/dot_general | solution.py:52
  74.2 0.8 fusion.52
  75.0 0.8 convolution_add_fusion.1
  75.8 0.8 convolution_subtract_fusion.2
  76.6 1.2 fusion.15
  77.9 1.2 fusion.7
  79.4 22.1 %all_to_all.34 = bf16[8,64,128]{2,0,1:T(8,128)(2,1)S(1)} all-to-all(bf16[8,64,128]{2,0,1:T(8,128)(2,1)S(1)} %fusion.37), channel_id=1, replica_groups=mesh['ctx'=64,'ch'=8] {'ctx'}, dimensions={1} | all-to-all | bytes 262144 | tf_op jit(solution)/shard_map/all_to_all | solution.py:93
  101.5 1.3 convolution_convert_fusion
  102.8 28.6 %reduce-scatter.2.cloned.1.call-done = bf16[16,2048]{1,0:T(8,128)(2,1)} async-done(((bf16[128,2048]{1,0:T(8,128)(2,1)}), bf16[16,2048]{1,0:T(8,128)(2,1)}) %reduce-scatter.2.cloned.1.call-update) | async-done | bytes 65552 | tf_op jit(solution)/shard_map/reduce_scatter | solution.py:162
  (31 shorter events, 4.5 us)
Async XLA Ops:
  6.5 95.0 %copy-start = (bf16[512,2048]{1,0:T(8,128)(2,1)S(1)}, bf16[512,2048]{1,0:T(8,128)(2,1)}, u32[]{:S(2)}) copy-start(bf16[512,2048]{1,0:T(8,128)(2,1)} %param.19) | copy-start | bytes 6291460
  6.5 9.5 %copy-start.2 = (f32[33,64]{1,0:T(8,128)S(1)}, f32[33,64]{1,0:T(8,128)}, u32[]{:S(2)}) copy-start(f32[33,64]{1,0:T(8,128)} %param.14) | copy-start | bytes 25348
  7.8 19.4 %collective-permute-start = (bf16[3,512,6]{1,2,0:T(8,128)(2,1)S(1)}, bf16[3,512,6]{1,2,0:T(8,128)(2,1)S(1)}, u32[]{:S(2)}, u32[]{:S(2)}) collective-permute-start(bf16[3,512,6]{1,2,0:T(8,128)(2,1)S(1)} %slice.91), channel_id=1, source_target_pairs={{0,8},{8,16},{16,24},{24,32},{32,40},{40,48},{48,56},{56,64},{64,7... | collective-permute-start | bytes 55304 | tf_op jit(solution)/shard_map/ppermute | solution.py:17
  26.9 19.3 %copy-start.1 = (f32[64,64]{1,0:T(8,128)S(1)}, f32[64,64]{1,0:T(8,128)}, u32[]{:S(2)}) copy-start(f32[64,64]{1,0:T(8,128)} %param.15) | copy-start | bytes 49156
  28.9 31.7 %all-to-all-start = ((bf16[3,512,128]{2,0,1:T(4,128)(2,1)}), bf16[3,512,128]{2,0,1:T(4,128)(2,1)S(1)}, u32[]{:S(2)}, u32[]{:S(2)}) async-start(bf16[3,512,128]{2,0,1:T(4,128)(2,1)} %copy.59), calls=%async_computation | async-start | bytes 1048576 | tf_op jit(solution)/shard_map/all_to_all | solution.py:89
  44.4 87.0 %reduce-scatter.2.cloned.1.call-start = ((), (), s32[]{:S(2)}) async-start(), calls=%async_computation.3 | async-start | bytes 589824 | tf_op jit(solution)/shard_map/reduce_scatter | solution.py:162
Sparse Core Ops, SparseCore 0:
  102.9 28.4 reduce-scatter.1
where the time goes:
time: 139 us; the launch traced here: 138 us
  matrix products  43 us (31%)
  waiting for transfers between devices  30 us (22%)
  blocking collectives  22.1 us (16%)
  starting transfers between devices  20.3 us (15%)
  between operations  13.7 us (10%)
  other arithmetic  5.52 us (4%)
  local copies, waits for them, and re-layouts  3.75 us (3%)
    reduce_scatter x1, waiting for transfers between devices, per_device(): lax.psum_scatter(lax.dot_general(returned, out_weight, (((0,), (0,)), (()...  28.6 us
    all_to_all x1, blocking collectives, regroup_back(): lax.all_to_all(gated_out, 'ctx', split_axis=1, concat_axis=0, tiled=True)  22.1 us
    dot_general x12, matrix products, einsum_high(): jnp.einsum(form, left_arr, right_arr, precision=highest, preferred_elemen...  17.8 us
    all_to_all x1, starting transfers between devices, regroup_forward(): lax.all_to_all(fields, 'ctx', split_axis=1, concat_axis=2, tiled=True)  15.4 us
    dot_general x1, matrix products, per_device(): jnp.dot(filt_mid.T, layer_one, precision=highest, preferred_element_type=...  11.2 us
    dot_general x1, matrix products, per_device(): jnp.dot(filt_in.T, features, precision=highest, preferred_element_type=jn...  10.8 us
    ppermute x1, starting transfers between devices, shifted(): lax.ppermute(value, axis, [(source, source + steps) for source in range(l...  4.83 us
  transfers between devices with their start and end apart: 3, of which 2 were waited for; matrix products, arithmetic and copies ran while one was open for 21% of the time, Pallas kernels for 0%

commit v1 on v0

v1 whole, which is shorter than its diff:
```python
import math

import jax
import jax.numpy as jnp
import numpy as np
from jax import lax
from jax.experimental import pallas as pl
from jax.experimental.pallas import tpu as pltpu
from jax.sharding import PartitionSpec as P

TOKENS = 8192
BLK = 128
NBLK = 64
CH = 8
BANDS = 16
FEAT = 33
FEAT_PAD = 48
TAPS = 7
UNITS = 64
CHUNK = 1024
bf16 = jnp.bfloat16
f32 = jnp.float32
highest = lax.Precision.HIGHEST


def split_np(table):
    table = np.asarray(table, np.float32)
    top = table.astype(jnp.bfloat16)
    low = (table - top.astype(np.float32)).astype(jnp.bfloat16)
    return top, low


def feature_table():
    steps = np.arange(TOKENS, dtype=np.int64)
    bands = np.arange(BANDS, dtype=np.int64)
    freq = 1 + bands * bands * (TOKENS // 4 - 1) // ((BANDS - 1) * (BANDS - 1))
    ang = (freq[:, None] * steps[None, :] % TOKENS) * (2.0 * math.pi / TOKENS)
    rows = np.concatenate([(steps / TOKENS)[None, :], np.cos(ang), np.sin(ang)], 0)
    rows = np.concatenate([rows, np.zeros((FEAT_PAD - FEAT, TOKENS))], 0)
    top, low = split_np(rows)
    return np.concatenate([top, low, top], 0)


def dft_tables():
    shifted = np.arange(NBLK) - 0.25
    block = np.arange(NBLK)
    inner = np.arange(BLK)
    outer_ang = 2.0 * math.pi * shifted[:, None] * block[None, :] / NBLK
    first = np.concatenate([np.cos(outer_ang), -np.sin(outer_ang)], 0)
    top, low = split_np(first)
    first_stack = np.concatenate([top, top, low], 1)
    last = np.concatenate([np.cos(outer_ang).T, -np.sin(outer_ang).T], 1) / TOKENS
    top, low = split_np(last)
    last_stack = np.concatenate([top, top, low], 1)
    tw_ang = 2.0 * math.pi * shifted[:, None] * inner[None, :] / TOKENS
    twiddle = np.stack([np.cos(tw_ang), -np.sin(tw_ang)], 0).astype(np.float32)
    in_ang = 2.0 * math.pi * (inner[:, None] * inner[None, :] % BLK) / BLK
    cos_in, sin_in = np.cos(in_ang), np.sin(in_ang)
    fwd = np.block([[cos_in, -sin_in], [sin_in, cos_in]])
    bwd = np.block([[cos_in, sin_in], [-sin_in, cos_in]])
    fwd_pair = np.stack(split_np(fwd), 0)
    bwd_pair = np.stack(split_np(bwd), 0)
    return first_stack, last_stack, twiddle, fwd_pair, bwd_pair


def sine_coefs():
    grid = 0.25 * np.cos((np.arange(400) + 0.5) * math.pi / 400)
    grid = np.concatenate([grid, 0.5 * np.cos((np.arange(800) + 0.5) * math.pi / 800)])
    grid = grid[np.abs(grid) > 1e-3]
    powers = np.stack([grid ** (2 * k + 1) for k in range(7)], 1)
    coef, *_ = np.linalg.lstsq(powers, np.sin(2.0 * math.pi * grid), rcond=None)
    return [float(c) for c in coef]


SINE = sine_coefs()


def sine_turns(turns):
    rest = turns - jnp.round(turns)
    sq = rest * rest
    acc = jnp.full_like(sq, SINE[-1])
    for c in SINE[-2::-1]:
        acc = acc * sq + c
    return acc * rest


def split(value):
    top = value.astype(bf16)
    return top, (value - top.astype(f32)).astype(bf16)


def mm(left, right):
    return jnp.dot(left, right, preferred_element_type=f32)


def mm_split(value, pair_ref):
    top, low = split(value)
    return mm(top, pair_ref[0]) + mm(low, pair_ref[0]) + mm(top, pair_ref[1])


def forward(rows_ref, first_ref, tw_ref, fwd_ref):
    cols = jnp.concatenate([rows_ref[pl.ds(c, NBLK, stride=CH), :] for c in range(CH)], 1)
    top, low = split(cols)
    outer = mm(first_ref[...], jnp.concatenate([top, low, top], 0))
    tw_re, tw_im = tw_ref[0], tw_ref[1]
    out = []
    for c in range(CH):
        lanes = slice(c * BLK, (c + 1) * BLK)
        re, im = outer[:NBLK, lanes], outer[NBLK:, lanes]
        out.append(jnp.concatenate([re * tw_re - im * tw_im, re * tw_im + im * tw_re], 1))
    return mm_split(jnp.concatenate(out, 0), fwd_ref)


def filter_kernel(feat_ref, w_in_ref, w_mid_ref, w_out_ref, taps_ref, rate_ref, skip_ref,
                  first_ref, tw_ref, fwd_ref, spec_ref, par_ref, rows_ref):
    first_chan = lax.axis_index("ctx") * CH
    chans = rate_ref.shape[1]
    pick = (lax.broadcasted_iota(jnp.int32, (CH, chans), 1)
            == lax.broadcasted_iota(jnp.int32, (CH, chans), 0) + first_chan).astype(f32)

    def mine(table):
        return lax.dot_general(pick, table, (((1,), (1,)), ((), ())), precision=highest,
                               preferred_element_type=f32)

    taps = mine(taps_ref[...])
    rate = mine(jnp.broadcast_to(rate_ref[...], (8, chans)))[:, :1]
    skip = mine(jnp.broadcast_to(skip_ref[...], (8, chans)))[:, :1]
    par_ref[...] = jnp.concatenate(
        [taps, skip, jnp.zeros((CH, 128 - 3 * TAPS - 1), f32)], 1)
    out_mine = mine(w_out_ref[...])

    def stack(weights):
        top, low = split(weights)
        return jnp.concatenate([top, top, low], 1)

    per_turn = 1.0 / (2.0 * math.pi)
    w_in = stack(w_in_ref[...] * per_turn)
    w_mid = stack(w_mid_ref[...] * per_turn)
    w_out = stack(out_mine)
    gain = jnp.sqrt(2.0 * rate)
    lane = lax.broadcasted_iota(jnp.int32, (CH, CHUNK), 1).astype(f32)
    for chunk in range(TOKENS // CHUNK):
        one = sine_turns(mm(w_in, feat_ref[:, chunk * CHUNK:(chunk + 1) * CHUNK]))
        top, low = split(one)
        two = sine_turns(mm(w_mid, jnp.concatenate([top, low, top], 0)))
        top, low = split(two)
        shape = mm(w_out, jnp.concatenate([top, low, top], 0))
        taper = gain * jnp.exp(-rate * (lane + float(chunk * CHUNK))) * shape
        for a in range(CHUNK // BLK):
            at = (chunk * (CHUNK // BLK) + a) * CH
            rows_ref[at:at + CH, :] = taper[:, a * BLK:(a + 1) * BLK]
    spec_ref[...] = forward(rows_ref, first_ref, tw_ref, fwd_ref)


def conv_kernel(field_ref, spec_ref, par_ref, first_ref, last_ref, tw_ref, fwd_ref, bwd_ref,
                out_ref, query_ref, prod_ref, conv_ref):
    par = par_ref[...]
    span = 8
    lane = lax.broadcasted_iota(jnp.int32, (span, CH, BLK), 2)
    for start in range(0, NBLK, span):
        if start == 0:
            block = field_ref[0:span].astype(f32)
            block = jnp.concatenate([jnp.zeros_like(block[:1]), block], 0)
        else:
            block = field_ref[start - 1:start + span].astype(f32)
        mixed = []
        for f in range(3):
            field = block[:, f * CH:(f + 1) * CH, :]
            total = par[:, f * TAPS:f * TAPS + 1][None] * field[1:]
            for j in range(1, TAPS):
                turned = pltpu.roll(field, j, 2)
                moved = jnp.where(lane < j, turned[:-1], turned[1:])
                total = total + par[:, f * TAPS + j:f * TAPS + j + 1][None] * moved
            mixed.append(total.astype(bf16).astype(f32).reshape(span * CH, BLK))
        at = slice(start * CH, (start + span) * CH)
        query_ref[at, :] = mixed[0]
        prod_ref[at, :] = mixed[1] * mixed[2]
    spec = forward(prod_ref, first_ref, tw_ref, fwd_ref)
    s_re, s_im = spec[:, :BLK], spec[:, BLK:]
    h_re, h_im = spec_ref[:, :BLK], spec_ref[:, BLK:]
    both = jnp.concatenate([s_re * h_re - s_im * h_im, s_re * h_im + s_im * h_re], 1)
    back = mm_split(both, bwd_ref)
    tw_re, tw_im = tw_ref[0], tw_ref[1]
    cols = []
    for c in range(CH):
        re, im = back[c * NBLK:(c + 1) * NBLK, :BLK], back[c * NBLK:(c + 1) * NBLK, BLK:]
        cols.append(jnp.concatenate([re * tw_re + im * tw_im, im * tw_re - re * tw_im], 0))
    top, low = split(jnp.concatenate(cols, 1))
    conv = mm(last_ref[...], jnp.concatenate([top, low, top], 0))
    for c in range(CH):
        conv_ref[pl.ds(c, NBLK, stride=CH), :] = conv[:, c * BLK:(c + 1) * BLK]
    skip = par[:, 3 * TAPS:3 * TAPS + 1][None]
    prod = prod_ref[...].reshape(NBLK, CH, BLK)
    total = conv_ref[...].reshape(NBLK, CH, BLK) + skip * prod
    gated = query_ref[...].reshape(NBLK, CH, BLK) * total
    out_ref[...] = gated.reshape(NBLK * CH, BLK).astype(bf16)


def per_device(query_field, key_field, value_field, short_taps, filt_in, filt_mid, filt_out,
               decay_rate, skip_gain, out_weight):
    tok, chans = query_field.shape
    groups = lax.axis_size("ch")
    first, last, twiddle, fwd, bwd = (jnp.asarray(t) for t in dft_tables())
    stacked = jnp.stack([query_field, key_field, value_field], 0)
    parts = jnp.transpose(stacked.reshape(3, tok, NBLK, CH), (2, 0, 3, 1)).reshape(NBLK, 3 * CH, tok)
    fields = lax.all_to_all(parts, "ctx", 0, 0, tiled=True)
    w_in = jnp.pad(filt_in.T, ((0, 0), (0, FEAT_PAD - FEAT)))
    params = pltpu.CompilerParams(vmem_limit_bytes=48 * 1024 * 1024)
    spec, par = pl.pallas_call(
        filter_kernel,
        out_shape=(jax.ShapeDtypeStruct((CH * NBLK, 2 * BLK), f32),
                   jax.ShapeDtypeStruct((CH, 128), f32)),
        scratch_shapes=[pltpu.VMEM((NBLK * CH, BLK), f32)],
        compiler_params=params,
        cost_estimate=pl.CostEstimate(flops=2 * 10**9, bytes_accessed=5 * 10**6, transcendentals=10**6),
        name="filter",
    )(jnp.asarray(feature_table()), w_in, filt_mid.T, filt_out, short_taps.reshape(3 * TAPS, chans),
      decay_rate.reshape(1, chans), skip_gain.reshape(1, chans), first, twiddle, fwd)
    gated = pl.pallas_call(
        conv_kernel,
        out_shape=jax.ShapeDtypeStruct((NBLK * CH, BLK), bf16),
        scratch_shapes=[pltpu.VMEM((NBLK * CH, BLK), f32)] * 3,
        compiler_params=params,
        name="convolve",
    )(fields, spec, par, first, last, twiddle, fwd, bwd)
    returned = lax.all_to_all(gated.reshape(NBLK, CH, BLK), "ctx", 0, 0, tiled=True)
    partial = lax.dot_general(returned.reshape(chans, tok), out_weight, (((0,), (0,)), ((), ())),
                              preferred_element_type=f32).astype(bf16)
    shares = lax.all_to_all(partial.reshape(groups, tok // groups, -1), "ch", 0, 0, tiled=True)
    return jnp.sum(shares.astype(f32), 0).astype(bf16)


def solution(mesh):
    return jax.shard_map(
        per_device,
        mesh=mesh,
        in_specs=(
            P("ctx", "ch"),
            P("ctx", "ch"),
            P("ctx", "ch"),
            P(None, None, "ch"),
            P(),
            P(),
            P(None, "ch"),
            P("ch"),
            P("ch"),
            P("ch", None),
        ),
        out_specs=P(("ctx", "ch"), None),
        check_vma=False,
    )
```

time: 139 us -> 80.2 us (0.58)
  matrix products: 43 us -> 0.46 us
  waiting for transfers between devices: 30 us -> 1.84 us
  blocking collectives: 22.1 us -> 37.7 us
  between operations: 13.7 us -> 0.14 us
  local copies, waits for them, and re-layouts: 3.75 us -> 12.9 us
  Pallas kernels: 0 us -> 7.67 us
  other arithmetic: 5.52 us -> 1.53 us
  starting transfers between devices: 20.3 us -> 17.1 us
    dot_general x16 -> x1, matrix products: 43 us -> 0.46 us  [per_device(): lax.dot_general(returned.reshape(chans, tok), out_weight, (((0,), (0,)),...]
    reduce_scatter x1 -> x0, waiting for transfers between devices: 28.6 us -> none  [per_device(): lax.psum_scatter(lax.dot_general(returned, out_weight, (((0,), (0,)), (()...]
    all_to_all x1 -> x2, blocking collectives: 22.1 us -> 37.7 us  [the longest x1 21.6 us: per_device(): lax.all_to_all(gated.reshape(NBLK, CH, BLK), 'ctx', 0, 0, tiled=True)]
    unnamed x11 -> x39, local copies, waits for them, and re-layouts: 0.24 us -> 12.3 us
    pallas_call x0 -> x2, Pallas kernels: none -> 7.67 us  [the longest x1 5.54 us: per_device(): pl.pallas_call(filter_kernel, out_shape=(jax.ShapeDtypeStruct((CH * NBLK,...]
    ppermute x1 -> x0, starting transfers between devices: 4.83 us -> none  [shifted(): lax.ppermute(value, axis, [(source, source + steps) for source in range(l...]
    cos x1 -> x0, other arithmetic: 2.12 us -> none  [position_features(): return jnp.concatenate([ramp_time, jnp.cos(angles), jnp.sin(angles)], 0)]
    all_to_all x1, starting transfers between devices: 15.4 us -> 17.1 us  [per_device(): fields = lax.all_to_all(parts, 'ctx', 0, 0, tiled=True)]
  transfers between devices with their start and end apart: 3 -> 1, of which waited for: 2 -> 1; matrix products, arithmetic and copies ran while one was open for 21% -> 2% of each run, Pallas kernels for 0% -> 7%
where the time goes in v1:
time: 80.2 us; the launch traced here: 79.5 us
  blocking collectives  37.7 us (47%)
  starting transfers between devices  17.1 us (21%)
  local copies, waits for them, and re-layouts  12.9 us (16%)
  Pallas kernels  7.67 us (10%)
  waiting for transfers between devices  1.84 us (2%)
  other arithmetic  1.53 us (2%)
    all_to_all x1, blocking collectives, per_device(): lax.all_to_all(gated.reshape(NBLK, CH, BLK), 'ctx', 0, 0, tiled=True)  21.6 us
    all_to_all x1, starting transfers between devices, per_device(): fields = lax.all_to_all(parts, 'ctx', 0, 0, tiled=True)  17.1 us
    all_to_all x1, blocking collectives, per_device(): lax.all_to_all(partial.reshape(groups, tok // groups, -1), 'ch', 0, 0, ti...  16.1 us
    unnamed x39, local copies, waits for them, and re-layouts  12.3 us
    pallas_call x1, Pallas kernels, per_device(): pl.pallas_call(filter_kernel, out_shape=(jax.ShapeDtypeStruct((CH * NBLK,...  5.54 us
    pallas_call x1, Pallas kernels, per_device(): pl.pallas_call(conv_kernel, out_shape=jax.ShapeDtypeStruct((NBLK * CH, BL...  2.13 us
    all_to_all x1, waiting for transfers between devices, per_device(): fields = lax.all_to_all(parts, 'ctx', 0, 0, tiled=True)  1.84 us
  transfers between devices with their start and end apart: 1, of which 1 were waited for; matrix products, arithmetic and copies ran while one was open for 2% of the time, Pallas kernels for 7%

profile of v1, /device:TPU:1, one launch (start us, length us, event | category | flops | bytes accessed | tf_op | source)
XLA Modules:
  0.0 79.5 jit_solution(2500720489106987705)
XLA Ops:
  0.1 1.2 %copy.22 = bf16[128,512]{0,1:T(8,128)(2,1)S(1)} copy(bf16[128,512]{1,0:T(8,128)(2,1)} %param.16) | data formatting | bytes 262144 | tf_op args[0]
  1.2 1.0 %copy.23 = bf16[128,512]{0,1:T(8,128)(2,1)S(1)} copy(bf16[128,512]{1,0:T(8,128)(2,1)} %param.17) | data formatting | bytes 262144 | tf_op args[1]
  2.3 1.0 %copy.24 = bf16[128,512]{0,1:T(8,128)(2,1)S(1)} copy(bf16[128,512]{1,0:T(8,128)(2,1)} %param.18) | data formatting | bytes 262144 | tf_op args[2]
  3.3 0.8 %copy_bitcast_fusion = bf16[64,24,128]{2,1,0:T(8,128)(2,1)} fusion(bf16[1,128,64,8]{1,3,2,0:T(8,128)(2,1)S(1)} %bitcast.25, bf16[1,128,64,8]{1,3,2,0:T(8,128)(2,1)S(1)} %bitcast.24, bf16[1,128,64,8]{1,3,2,0:T(8,128)(2,1)S(1)} %bitcast.23), kind=kLoop, calls=%fused_computation.2 | loop fusion | flops 393216 | bytes 786432 | tf_op jit(solution)/shard_map/reshape | solution.py:205
  4.1 17.1 %all-to-all-start = ((bf16[64,24,128]{2,1,0:T(8,128)(2,1)}), bf16[64,24,128]{2,1,0:T(8,128)(2,1)S(1)}, u32[]{:S(2)}, u32[]{:S(2)}) async-start(bf16[64,24,128]{2,1,0:T(8,128)(2,1)} %copy_bitcast_fusion), calls=%async_computation | async-start | bytes 786432 | tf_op jit(solution)/shard_map/all_to_all | solution.py:206
  21.3 0.1 copy.26
  21.4 0.7 copy.27
  22.1 0.6 reshape.29.taps_ref
  22.7 0.8 %copy-done.3 = f32[2,64,128]{2,1,0:T(8,128)S(1)} copy-done((f32[2,64,128]{2,1,0:T(8,128)S(1)}, f32[2,64,128]{2,1,0:T(8,128)}, u32[]{:S(2)}) %copy-start.3) | copy-done | bytes 65560
  23.6 0.8 %copy-done.5 = bf16[128,192]{1,0:T(8,128)(2,1)S(1)} copy-done((bf16[128,192]{1,0:T(8,128)(2,1)S(1)}, bf16[128,192]{1,0:T(8,128)(2,1)}, u32[]{:S(2)}) %copy-start.5) | copy-done | bytes 49176
  24.4 0.8 %copy-done.8 = f32[21,512]{1,0:T(8,128)S(1)} copy-done((f32[21,512]{1,0:T(8,128)S(1)}, f32[21,512]{1,0:T(8,128)}, u32[]{:S(2)}) %copy-start.8) | copy-done | bytes 43032
  25.2 0.8 copy-done.9
  26.0 0.9 %copy-done.10 = f32[64,512]{1,0:T(8,128)S(1)} copy-done((f32[64,512]{1,0:T(8,128)S(1)}, f32[64,512]{1,0:T(8,128)}, u32[]{:S(2)}) %copy-start.10) | copy-done | bytes 131096
  26.9 1.7 %copy-done.13 = bf16[144,8192]{1,0:T(8,128)(2,1)S(1)} copy-done((bf16[144,8192]{1,0:T(8,128)(2,1)S(1)}, bf16[144,8192]{1,0:T(8,128)(2,1)}, u32[]{:S(2)}) %copy-start.13) | copy-done | bytes 2359320
  28.5 5.5 %filter.1 = (f32[512,256]{1,0:T(8,128)S(1)}, f32[8,128]{1,0:T(8,128)S(1)}) custom-call(bf16[144,8192]{1,0:T(8,128)(2,1)S(1)} %copy-done.13, f32[64,48]{1,0:T(8,128)S(1)} %pad.4.w_in_ref, f32[64,64]{1,0:T(8,128)S(1)} %bitcast.19, f32[64,512]{1,0:T(8,128)S(1)} %copy-done.10, f32[21,512]{1,0:T(8,128)S(1)} %copy-done.8, f32[1,512]{1,0:T(1,128)S(1)} %bitcast.20, ...), custom_call_target="tpu_custom_call" | custom-call | flops 2000000000 | bytes 5000000 | tf_op jit(solution)/shard_map/filter/pallas_call | solution.py:209
  34.1 1.8 %all-to-all-done.field_ref = bf16[64,24,128]{2,1,0:T(8,128)(2,1)S(1)} async-done(((bf16[64,24,128]{2,1,0:T(8,128)(2,1)}), bf16[64,24,128]{2,1,0:T(8,128)(2,1)S(1)}, u32[]{:S(2)}, u32[]{:S(2)}) %all-to-all-start) | async-done | bytes 393248 | tf_op jit(solution)/shard_map/all_to_all | solution.py:206
  35.9 0.8 %copy-done.4 = f32[2,64,128]{2,1,0:T(8,128)S(1)} copy-done((f32[2,64,128]{2,1,0:T(8,128)S(1)}, f32[2,64,128]{2,1,0:T(8,128)}, u32[]{:S(2)}) %copy-start.4) | copy-done | bytes 65560
  36.8 0.8 %copy-done.6 = bf16[128,192]{1,0:T(8,128)(2,1)S(1)} copy-done((bf16[128,192]{1,0:T(8,128)(2,1)S(1)}, bf16[128,192]{1,0:T(8,128)(2,1)}, u32[]{:S(2)}) %copy-start.6) | copy-done | bytes 49176
  37.6 0.8 %copy-done.7 = bf16[64,384]{1,0:T(8,128)(2,1)S(1)} copy-done((bf16[64,384]{1,0:T(8,128)(2,1)S(1)}, bf16[64,384]{1,0:T(8,128)(2,1)}, u32[]{:S(2)}) %copy-start.7) | copy-done | bytes 49176
  38.4 2.1 %convolve.1 = bf16[512,128]{1,0:T(8,128)(2,1)S(1)} custom-call(bf16[64,24,128]{2,1,0:T(8,128)(2,1)S(1)} %all-to-all-done.field_ref, f32[512,256]{1,0:T(8,128)S(1)} %get-tuple-element.7.spec_ref, f32[8,128]{1,0:T(8,128)S(1)} %get-tuple-element.8.par_ref, bf16[128,192]{1,0:T(8,128)(2,1)S(1)} %copy-done.6, bf16[64,384]{1,0:T(8,128)(2,1)S(1)} %copy-done.7, ...), custom_call_target="tpu_custom_call" | custom-call | tf_op jit(solution)/shard_map/convolve/pallas_call | solution.py:219
  40.5 21.6 %all_to_all.15 = bf16[64,8,128]{2,1,0:T(8,128)(2,1)S(1)} all-to-all(bf16[64,8,128]{2,1,0:T(8,128)(2,1)S(1)} %bitcast.18), channel_id=1, replica_groups=mesh['ctx'=64,'ch'=8] {'ctx'}, dimensions={0} | all-to-all | bytes 262144 | tf_op jit(solution)/shard_map/all_to_all | solution.py:226
  62.2 0.5 convolution_convert_fusion
  62.6 16.1 %all_to_all.16 = bf16[8,16,2048]{2,1,0:T(8,128)(2,1)S(1)} all-to-all(bf16[8,16,2048]{2,1,0:T(8,128)(2,1)S(1)} %bitcast.22), channel_id=1, replica_groups=mesh['ctx'=64,'ch'=8] {'ch'}, dimensions={0} | all-to-all | bytes 1048576 | tf_op jit(solution)/shard_map/all_to_all | solution.py:229
  78.7 0.7 reduce_sum.12
  (26 shorter events, 0.1 us)
Async XLA Ops:
  0.0 62.2 %copy-start = (bf16[512,2048]{1,0:T(8,128)(2,1)S(1)}, bf16[512,2048]{1,0:T(8,128)(2,1)}, u32[]{:S(2)}) copy-start(bf16[512,2048]{1,0:T(8,128)(2,1)} %param.25) | copy-start | bytes 6291460
  0.0 22.7 %copy-start.1 = (bf16[2,256,256]{2,1,0:T(8,128)(2,1)S(1)}, bf16[2,256,256]{2,1,0:T(8,128)(2,1)}, u32[]{:S(2)}) copy-start(bf16[2,256,256]{2,1,0:T(8,128)(2,1)} %constant.21.clone.fwd_ref) | copy-start | bytes 786436
  0.0 21.3 %copy-start.16 = (f32[33,64]{1,0:T(8,128)S(1)}, f32[33,64]{1,0:T(8,128)}, u32[]{:S(2)}) copy-start(f32[33,64]{1,0:T(8,128)} %param.20) | copy-start | bytes 25348
  0.0 21.4 %copy-start.15 = (f32[64,64]{1,0:T(8,128)S(1)}, f32[64,64]{1,0:T(8,128)}, u32[]{:S(2)}) copy-start(f32[64,64]{1,0:T(8,128)} %param.21) | copy-start | bytes 49156
  0.0 22.0 %copy-start.14 = (f32[3,7,512]{2,1,0:T(8,128)S(1)}, f32[3,7,512]{2,1,0:T(8,128)}, u32[]{:S(2)}) copy-start(f32[3,7,512]{2,1,0:T(8,128)} %param.19) | copy-start | bytes 129028
  0.0 22.7 %copy-start.12 = (f32[512]{0:T(512)S(1)}, f32[512]{0:T(512)}, u32[]{:S(2)}) copy-start(f32[512]{0:T(512)} %param.24) | copy-start | bytes 6148
  0.0 22.7 %copy-start.11 = (f32[512]{0:T(512)S(1)}, f32[512]{0:T(512)}, u32[]{:S(2)}) copy-start(f32[512]{0:T(512)} %param.23) | copy-start | bytes 6148
  4.1 31.8 %all-to-all-start = ((bf16[64,24,128]{2,1,0:T(8,128)(2,1)}), bf16[64,24,128]{2,1,0:T(8,128)(2,1)S(1)}, u32[]{:S(2)}, u32[]{:S(2)}) async-start(bf16[64,24,128]{2,1,0:T(8,128)(2,1)} %copy_bitcast_fusion), calls=%async_computation | async-start | bytes 786432 | tf_op jit(solution)/shard_map/all_to_all | solution.py:206
  22.7 0.8 %copy-start.3 = (f32[2,64,128]{2,1,0:T(8,128)S(1)}, f32[2,64,128]{2,1,0:T(8,128)}, u32[]{:S(2)}) copy-start(f32[2,64,128]{2,1,0:T(8,128)} %constant.20.clone.tw_ref) | copy-start | bytes 196612
  23.6 0.8 %copy-start.5 = (bf16[128,192]{1,0:T(8,128)(2,1)S(1)}, bf16[128,192]{1,0:T(8,128)(2,1)}, u32[]{:S(2)}) copy-start(bf16[128,192]{1,0:T(8,128)(2,1)} %constant.18.clone.first_ref) | copy-start | bytes 147460
  24.4 0.8 %copy-start.8 = (f32[21,512]{1,0:T(8,128)S(1)}, f32[21,512]{1,0:T(8,128)}, u32[]{:S(2)}) copy-start(f32[21,512]{1,0:T(8,128)} %reshape.29.taps_ref) | copy-start | bytes 129028
  25.2 0.8 copy-start.9
  26.0 0.9 %copy-start.10 = (f32[64,512]{1,0:T(8,128)S(1)}, f32[64,512]{1,0:T(8,128)}, u32[]{:S(2)}) copy-start(f32[64,512]{1,0:T(8,128)} %w_out_ref.1) | copy-start | bytes 393220
  26.9 1.7 %copy-start.13 = (bf16[144,8192]{1,0:T(8,128)(2,1)S(1)}, bf16[144,8192]{1,0:T(8,128)(2,1)}, u32[]{:S(2)}) copy-start(bf16[144,8192]{1,0:T(8,128)(2,1)} %constant.23.clone.feat_ref) | copy-start | bytes 7077892
  28.5 7.4 %copy-start.2 = (bf16[2,256,256]{2,1,0:T(8,128)(2,1)S(1)}, bf16[2,256,256]{2,1,0:T(8,128)(2,1)}, u32[]{:S(2)}) copy-start(bf16[2,256,256]{2,1,0:T(8,128)(2,1)} %constant.22.clone.bwd_ref) | copy-start | bytes 786436
  35.9 0.8 %copy-start.4 = (f32[2,64,128]{2,1,0:T(8,128)S(1)}, f32[2,64,128]{2,1,0:T(8,128)}, u32[]{:S(2)}) copy-start(f32[2,64,128]{2,1,0:T(8,128)} %constant.20.clone.tw_ref) | copy-start | bytes 196612
  36.8 0.8 %copy-start.6 = (bf16[128,192]{1,0:T(8,128)(2,1)S(1)}, bf16[128,192]{1,0:T(8,128)(2,1)}, u32[]{:S(2)}) copy-start(bf16[128,192]{1,0:T(8,128)(2,1)} %constant.18.clone.first_ref) | copy-start | bytes 147460
  37.6 0.8 %copy-start.7 = (bf16[64,384]{1,0:T(8,128)(2,1)S(1)}, bf16[64,384]{1,0:T(8,128)(2,1)}, u32[]{:S(2)}) copy-start(bf16[64,384]{1,0:T(8,128)(2,1)} %constant.19.clone.last_ref) | copy-start | bytes 147460

commit v2 on v1

v2 whole, which is shorter than its diff:
```python
import math

import jax
import jax.numpy as jnp
import numpy as np
from jax import lax
from jax.experimental import pallas as pl
from jax.experimental.pallas import tpu as pltpu
from jax.sharding import PartitionSpec as P

TOKENS = 8192
BLK = 128
NBLK = 64
CH = 8
BANDS = 16
FEAT = 33
FEAT_PAD = 48
HALF = 64
SHARE = 16
TAPS = 7
UNITS = 64
CHUNK = 1024
bf16 = jnp.bfloat16
f32 = jnp.float32
highest = lax.Precision.HIGHEST


def split_np(table):
    table = np.asarray(table, np.float32)
    top = table.astype(jnp.bfloat16)
    low = (table - top.astype(np.float32)).astype(jnp.bfloat16)
    return top, low


def feature_table():
    steps = np.arange(TOKENS, dtype=np.int64)
    bands = np.arange(BANDS, dtype=np.int64)
    freq = 1 + bands * bands * (TOKENS // 4 - 1) // ((BANDS - 1) * (BANDS - 1))
    ang = (freq[:, None] * steps[None, :] % TOKENS) * (2.0 * math.pi / TOKENS)
    rows = np.concatenate([(steps / TOKENS)[None, :], np.cos(ang), np.sin(ang)], 0)
    rows = np.concatenate([rows, np.zeros((FEAT_PAD - FEAT, TOKENS))], 0)
    return np.concatenate(split_np(rows), 0)


def token_order(cores):
    at = np.arange(BLK).reshape(BLK // SHARE // cores, cores, SHARE)
    return at.transpose(1, 0, 2).reshape(-1)


def dft_tables(cores):
    shifted = np.arange(NBLK) - 0.25
    block = np.arange(NBLK)
    inner = np.arange(BLK)
    order = token_order(cores)
    outer_ang = 2.0 * math.pi * shifted[:, None] * block[None, :] / NBLK
    first = np.concatenate([np.cos(outer_ang), -np.sin(outer_ang)], 0)
    top, low = split_np(first)
    first_stack = np.concatenate([top, top, low], 1)
    last = np.concatenate([np.cos(outer_ang).T, -np.sin(outer_ang).T], 1) / TOKENS
    top, low = split_np(last)
    last_stack = np.concatenate([top, top, low], 1)
    tw_ang = 2.0 * math.pi * shifted[:, None] * inner[None, :] / TOKENS
    back_ang = tw_ang[:, order]
    twiddle = np.stack([np.cos(tw_ang), -np.sin(tw_ang), np.cos(back_ang), np.sin(back_ang)], 0)
    in_ang = 2.0 * math.pi * (inner[:, None] * inner[None, :] % BLK) / BLK
    cos_in, sin_in = np.cos(in_ang), np.sin(in_ang)
    fwd = np.block([[cos_in, -sin_in], [sin_in, cos_in]])
    cos_back, sin_back = cos_in[:, order], sin_in[:, order]
    bwd = np.block([[cos_back, sin_back], [-sin_back, cos_back]])
    mats = np.stack(split_np(fwd) + split_np(bwd), 0)
    reorder = np.zeros((BLK, BLK), np.float32)
    reorder[order, inner] = 1.0
    return first_stack, last_stack, twiddle.astype(np.float32), mats, reorder.astype(jnp.bfloat16)


def sine_coefs():
    grid = 0.25 * np.cos((np.arange(400) + 0.5) * math.pi / 400)
    grid = np.concatenate([grid, 0.5 * np.cos((np.arange(800) + 0.5) * math.pi / 800)])
    grid = grid[np.abs(grid) > 1e-3]
    powers = np.stack([grid ** (2 * k + 1) for k in range(7)], 1)
    coef, *_ = np.linalg.lstsq(powers, np.sin(2.0 * math.pi * grid), rcond=None)
    return [float(c) for c in coef]


SINE = sine_coefs()


def sine_turns(turns):
    rest = turns - jnp.round(turns)
    sq = rest * rest
    acc = jnp.full_like(sq, SINE[-1])
    for c in SINE[-2::-1]:
        acc = acc * sq + c
    return acc * rest


def split(value):
    top = value.astype(bf16)
    return top, (value - top.astype(f32)).astype(bf16)


def mm(left, right):
    return jnp.dot(left, right, preferred_element_type=f32)


def mm_split(value, top_mat, low_mat):
    top, low = split(value)
    return mm(top, top_mat) + mm(low, top_mat) + mm(top, low_mat)


def lift(rows, low_half):
    return jnp.where(low_half, rows[0], pltpu.roll(rows[1], 4, 1))


def drop(rows, low_half):
    return jnp.where(low_half, pltpu.roll(rows[0], 4, 1), rows[1])


def prep_kernel(query_hbm, key_hbm, value_hbm, out_ref, held, sems):
    copies = [pltpu.make_async_copy(src, held.at[f], sems.at[f])
              for f, src in enumerate((query_hbm, key_hbm, value_hbm))]
    for copy in copies:
        copy.start()
    low_half = lax.broadcasted_iota(jnp.int32, (NBLK // 2, CH, BLK), 1) < 4
    sets = []
    for f in range(3):
        copies[f].wait()
        turned = held[f].astype(f32).T.reshape(2, NBLK // 2, CH, BLK)
        pairs = jnp.stack([lift(turned, low_half), drop(turned, low_half)], 1)
        sets.append(pairs.reshape(NBLK, CH, BLK))
    out_ref[...] = jnp.concatenate(sets, 1).astype(bf16)


def forward(rows_ref, first_ref, tw_ref, mats_ref):
    cols = jnp.concatenate([rows_ref[pl.ds(c, NBLK, stride=CH), :] for c in range(CH)], 1)
    top, low = split(cols)
    outer = mm(first_ref[...], jnp.concatenate([top, low, top], 0))
    tw_re, tw_im = tw_ref[0], tw_ref[1]
    out = []
    for c in range(CH):
        lanes = slice(c * BLK, (c + 1) * BLK)
        re, im = outer[:NBLK, lanes], outer[NBLK:, lanes]
        out.append(jnp.concatenate([re * tw_re - im * tw_im, re * tw_im + im * tw_re], 1))
    return mm_split(jnp.concatenate(out, 0), mats_ref[0], mats_ref[1])


def filter_kernel(feat_hbm, w_in_hbm, w_mid_hbm, w_out_hbm, taps_hbm, rate_hbm, skip_hbm,
                  first_hbm, last_hbm, tw_hbm, mats_hbm, reorder_hbm,
                  spec_ref, par_ref, first_ref, last_ref, tw_ref, mats_ref, reorder_ref,
                  rows_ref, feat_ref, w_in_ref, w_mid_ref, w_out_ref, taps_ref, rate_ref, skip_ref,
                  sems):
    sources = (w_in_hbm, w_mid_hbm, rate_hbm, w_out_hbm, skip_hbm, taps_hbm, feat_hbm,
               first_hbm, tw_hbm, mats_hbm, last_hbm, reorder_hbm)
    targets = (w_in_ref, w_mid_ref, rate_ref, w_out_ref, skip_ref, taps_ref, feat_ref,
               first_ref, tw_ref, mats_ref, last_ref, reorder_ref)
    copies = [pltpu.make_async_copy(src, dst, sems.at[n])
              for n, (src, dst) in enumerate(zip(sources, targets))]
    for copy in copies:
        copy.start()
    chans = rate_ref.shape[1]
    row = lax.broadcasted_iota(jnp.int32, (CH, chans), 0)
    wanted = lax.axis_index("ctx") * 4 + row % 4 + row // 4 * (chans // 2)
    pick = (lax.broadcasted_iota(jnp.int32, (CH, chans), 1) == wanted).astype(f32)

    def mine(table):
        return lax.dot_general(pick, table, (((1,), (1,)), ((), ())), precision=highest,
                               preferred_element_type=f32)

    def stack(weights):
        top, low = split(weights)
        return jnp.concatenate([top, top, low], 1)

    for copy in copies[:7]:
        copy.wait()
    taps = jnp.concatenate([mine(taps_ref[f]) for f in range(3)], 1)
    rate = mine(jnp.broadcast_to(rate_ref[...], (8, chans)))[:, :1]
    skip = mine(jnp.broadcast_to(skip_ref[...], (8, chans)))[:, :1]
    par_ref[...] = jnp.concatenate([taps, jnp.zeros((CH, 128 - 3 * TAPS), f32)], 1)
    per_turn = 1.0 / (2.0 * math.pi)
    padded = jnp.concatenate([w_in_ref[...], jnp.zeros((FEAT_PAD - FEAT, UNITS), f32)], 0)
    w_in = stack(padded.T * per_turn)
    w_mid = stack(w_mid_ref[...].T * per_turn)
    w_out = stack(mine(w_out_ref[...]))
    gain = jnp.sqrt(2.0 * rate)
    lane = lax.broadcasted_iota(jnp.int32, (CH, CHUNK), 1).astype(f32)
    for chunk in range(TOKENS // CHUNK):
        feat = feat_ref[:, chunk * CHUNK:(chunk + 1) * CHUNK]
        one = sine_turns(mm(w_in, jnp.concatenate([feat, feat[:FEAT_PAD]], 0)))
        top, low = split(one)
        two = sine_turns(mm(w_mid, jnp.concatenate([top, low, top], 0)))
        top, low = split(two)
        shape = mm(w_out, jnp.concatenate([top, low, top], 0))
        taper = gain * jnp.exp(-rate * (lane + float(chunk * CHUNK))) * shape
        for a in range(CHUNK // BLK):
            at = (chunk * (CHUNK // BLK) + a) * CH
            rows_ref[at:at + CH, :] = taper[:, a * BLK:(a + 1) * BLK]
    for copy in copies[7:]:
        copy.wait()
    spec = forward(rows_ref, first_ref, tw_ref, mats_ref)
    direct = jnp.concatenate([jnp.broadcast_to(skip[c:c + 1], (NBLK, BLK)) for c in range(CH)], 0)
    spec_ref[:, :BLK] = spec[:, :BLK] + direct
    spec_ref[:, BLK:] = spec[:, BLK:]


def conv_kernel(field_ref, spec_ref, par_ref, first_ref, last_ref, tw_ref, mats_ref, reorder_ref,
                out_ref, query_ref, prod_ref, conv_ref):
    par = par_ref[...]
    span = 8
    lane = lax.broadcasted_iota(jnp.int32, (span, CH, BLK), 2)
    for start in range(0, NBLK, span):
        if start == 0:
            block = field_ref[0:span].astype(f32)
            block = jnp.concatenate([jnp.zeros_like(block[:1]), block], 0)
        else:
            block = field_ref[start - 1:start + span].astype(f32)
        mixed = []
        for f in range(3):
            field = block[:, f * CH:(f + 1) * CH, :]
            total = par[:, f * TAPS:f * TAPS + 1][None] * field[1:]
            for j in range(1, TAPS):
                turned = pltpu.roll(field, j, 2)
                moved = jnp.where(lane < j, turned[:-1], turned[1:])
                total = total + par[:, f * TAPS + j:f * TAPS + j + 1][None] * moved
            mixed.append(total.astype(bf16).reshape(span * CH, BLK))
        at = slice(start * CH, (start + span) * CH)
        prod_ref[at, :] = mixed[1].astype(f32) * mixed[2].astype(f32)
        query_ref[at, :] = mm(mixed[0], reorder_ref[...])
    spec = forward(prod_ref, first_ref, tw_ref, mats_ref)
    s_re, s_im = spec[:, :BLK], spec[:, BLK:]
    h_re, h_im = spec_ref[:, :BLK], spec_ref[:, BLK:]
    both = jnp.concatenate([s_re * h_re - s_im * h_im, s_re * h_im + s_im * h_re], 1)
    back = mm_split(both, mats_ref[2], mats_ref[3])
    tw_re, tw_im = tw_ref[2], tw_ref[3]
    cols = []
    for c in range(CH):
        re, im = back[c * NBLK:(c + 1) * NBLK, :BLK], back[c * NBLK:(c + 1) * NBLK, BLK:]
        cols.append(jnp.concatenate([re * tw_re - im * tw_im, im * tw_re + re * tw_im], 0))
    top, low = split(jnp.concatenate(cols, 1))
    conv = mm(last_ref[...], jnp.concatenate([top, low, top], 0))
    for c in range(CH):
        conv_ref[pl.ds(c, NBLK, stride=CH), :] = conv[:, c * BLK:(c + 1) * BLK]
    gated = (query_ref[...] * conv_ref[...]).reshape(NBLK, CH, BLK)
    sub = lax.broadcasted_iota(jnp.int32, (NBLK, CH, BLK), 1) < 4
    left = lax.broadcasted_iota(jnp.int32, (NBLK, CH, BLK), 2) < HALF
    crossed = pltpu.roll(pltpu.roll(gated, 4, 1), HALF, 2)
    sorted_rows = jnp.where(sub == left, gated, crossed).reshape(NBLK // 2, 2, CH, BLK)
    pairs = (sorted_rows[:, 0], sorted_rows[:, 1])
    half = sub[:NBLK // 2]
    both = jnp.concatenate([lift(pairs, half), drop(pairs, half)], 0)
    out_ref[...] = both.reshape(NBLK * CH, BLK).astype(bf16)


def project_kernel(rows_ref, own_ref, other_ref, out_ref):
    core = lax.axis_index("ch") % 2
    depth = rows_ref.shape[0] // 2
    total = None
    for weight_ref, part in ((own_ref, core), (other_ref, 1 - core)):
        rows = rows_ref[pl.ds(pl.multiple_of(part * depth, depth), depth), :]
        turned = rows.astype(f32).T.astype(bf16)
        for half in range(2):
            term = mm(turned[half * HALF:(half + 1) * HALF], weight_ref[half * depth:(half + 1) * depth, :])
            total = term if total is None else total + term
    out_ref[...] = total.astype(bf16)


def per_device(query_field, key_field, value_field, short_taps, filt_in, filt_mid, filt_out,
               decay_rate, skip_gain, out_weight):
    chans = query_field.shape[1]
    cores = 2
    groups = lax.axis_size("ch")
    chips = groups // cores
    dout = out_weight.shape[1]
    first, last, twiddle, mats, reorder = (jnp.asarray(t) for t in dft_tables(cores))
    params = pltpu.CompilerParams(vmem_limit_bytes=48 * 1024 * 1024)
    far = pl.BlockSpec(memory_space=pltpu.HBM)
    parts = pl.pallas_call(
        prep_kernel,
        out_shape=jax.ShapeDtypeStruct((NBLK, 3 * CH, BLK), bf16),
        in_specs=[far] * 3,
        scratch_shapes=[pltpu.VMEM((3,) + query_field.shape, bf16), pltpu.SemaphoreType.DMA((3,))],
        compiler_params=params,
        name="prep",
    )(query_field, key_field, value_field)
    fields = lax.all_to_all(parts, "ctx", 0, 0, tiled=True)
    sources = (jnp.asarray(feature_table()), filt_in, filt_mid, filt_out, short_taps,
               decay_rate.reshape(1, chans), skip_gain.reshape(1, chans),
               first, last, twiddle, mats, reorder)
    passed = [jax.ShapeDtypeStruct(t.shape, t.dtype) for t in sources[7:]]
    spec, par, *tables = pl.pallas_call(
        filter_kernel,
        out_shape=[jax.ShapeDtypeStruct((CH * NBLK, 2 * BLK), f32),
                   jax.ShapeDtypeStruct((CH, 128), f32)] + passed,
        in_specs=[far] * len(sources),
        scratch_shapes=[pltpu.VMEM((NBLK * CH, BLK), f32)]
        + [pltpu.VMEM(t.shape, t.dtype) for t in sources[:7]]
        + [pltpu.SemaphoreType.DMA((len(sources),))],
        compiler_params=params,
        cost_estimate=pl.CostEstimate(flops=2 * 10**9, bytes_accessed=5 * 10**6, transcendentals=10**6),
        name="filter",
    )(*sources)
    own_weight, par = lax.optimization_barrier((out_weight, par))
    other_weight = lax.ppermute(own_weight, "ch", [(d, d ^ 1) for d in range(groups)])
    gated = pl.pallas_call(
        conv_kernel,
        out_shape=jax.ShapeDtypeStruct((NBLK * CH, BLK), bf16),
        scratch_shapes=[pltpu.VMEM((NBLK * CH, BLK), f32)] * 3,
        compiler_params=params,
        name="convolve",
    )(fields, spec, par, *tables)
    on_chip = [[c * groups + x * cores + k for k in range(cores) for c in range(NBLK)] for x in range(chips)]
    returned = lax.all_to_all(gated.reshape(NBLK * cores, CH // cores, BLK), ("ctx", "ch"), 0, 0,
                              tiled=True, axis_index_groups=on_chip)
    partial = pl.pallas_call(
        project_kernel,
        out_shape=jax.ShapeDtypeStruct((BLK // cores, dout), bf16),
        compiler_params=params,
        name="project",
    )(returned.reshape(NBLK * CH, BLK), own_weight, other_weight)
    along_x = [[x * cores + k for x in range(chips)] for k in range(cores)]
    shares = lax.all_to_all(partial.reshape(chips, SHARE, dout), "ch", 0, 0, tiled=True,
                            axis_index_groups=along_x)
    return jnp.sum(shares.astype(f32), 0).astype(bf16)


def solution(mesh):
    return jax.shard_map(
        per_device,
        mesh=mesh,
        in_specs=(
            P("ctx", "ch"),
            P("ctx", "ch"),
            P("ctx", "ch"),
            P(None, None, "ch"),
            P(),
            P(),
            P(None, "ch"),
            P("ch"),
            P("ch"),
            P("ch", None),
        ),
        out_specs=P(("ctx", "ch"), None),
        check_vma=False,
    )
```

time: 80.2 us -> 87.6 us (1.092)
  blocking collectives: 37.7 us -> 56.6 us
  starting transfers between devices: 17.1 us -> 8.78 us
  Pallas kernels: 7.67 us -> 10.4 us
  local copies, waits for them, and re-layouts: 12.9 us -> 10.3 us
  waiting for transfers between devices: 1.84 us -> 0.01 us
    all_to_all x2 -> x3, blocking collectives: 37.7 us -> 56.6 us  [the longest x1 26.2 us: per_device(): fields = lax.all_to_all(parts, 'ctx', 0, 0, tiled=True)]
    all_to_all x1 -> x0, starting transfers between devices: 17.1 us -> none  [per_device(): fields = lax.all_to_all(parts, 'ctx', 0, 0, tiled=True)]
    ppermute x0 -> x1, starting transfers between devices: none -> 8.78 us  [per_device(): lax.ppermute(own_weight, 'ch', [(d, d ^ 1) for d in range(groups)])]
    pallas_call x1 -> x3, Pallas kernels: 5.54 us -> 8.04 us  [the longest x1 6.27 us: per_device(): pl.pallas_call(filter_kernel, out_shape=[jax.ShapeDtypeStruct((CH * NBLK,...]
    unnamed x39 -> x32, local copies, waits for them, and re-layouts: 12.3 us -> 10.3 us
    all_to_all x1 -> x0, waiting for transfers between devices: 1.84 us -> none  [per_device(): fields = lax.all_to_all(parts, 'ctx', 0, 0, tiled=True)]
  transfers between devices with their start and end apart: 1 -> 1, of which waited for: 1 -> 0; matrix products, arithmetic and copies ran while one was open for 2% -> 0% of each run, Pallas kernels for 7% -> 4%
where the time goes in v2:
time: 87.6 us; the launch traced here: 86.8 us
  blocking collectives  56.6 us (65%)
  Pallas kernels  10.4 us (12%)
  local copies, waits for them, and re-layouts  10.3 us (12%)
  starting transfers between devices  8.78 us (10%)
    all_to_all x1, blocking collectives, per_device(): fields = lax.all_to_all(parts, 'ctx', 0, 0, tiled=True)  26.2 us
    all_to_all x1, blocking collectives, per_device(): lax.all_to_all(gated.reshape(NBLK * cores, CH // cores, BLK), ('ctx', 'ch...  21.1 us
    unnamed x32, local copies, waits for them, and re-layouts  10.3 us
    all_to_all x1, blocking collectives, per_device(): lax.all_to_all(partial.reshape(chips, SHARE, dout), 'ch', 0, 0, tiled=Tru...  9.36 us
    ppermute x1, starting transfers between devices, per_device(): lax.ppermute(own_weight, 'ch', [(d, d ^ 1) for d in range(groups)])  8.78 us
    pallas_call x1, Pallas kernels, per_device(): pl.pallas_call(filter_kernel, out_shape=[jax.ShapeDtypeStruct((CH * NBLK,...  6.27 us
    pallas_call x1, Pallas kernels, per_device(): pl.pallas_call(conv_kernel, out_shape=jax.ShapeDtypeStruct((NBLK * CH, BL...  2.32 us
  transfers between devices with their start and end apart: 1, of which 0 were waited for; matrix products, arithmetic and copies ran while one was open for 0% of the time, Pallas kernels for 4%

profile of v2, /device:TPU:1, one launch (start us, length us, event | category | flops | bytes accessed | tf_op | source)
XLA Modules:
  0.0 86.8 jit_solution(10847750094042973468)
XLA Ops:
  0.0 0.9 %copy-done.4 = f32[64,512]{1,0:T(8,128)S(1)} copy-done((f32[64,512]{1,0:T(8,128)S(1)}, f32[64,512]{1,0:T(8,128)}, u32[]{:S(2)}) %copy-start.4) | copy-done | bytes 131096
  0.9 0.8 copy-done.5
  1.7 0.8 copy-done.6
  2.5 0.7 copy-done.7
  3.2 0.7 copy-done.8
  3.9 0.7 copy-done.9
  4.6 1.4 %copy-done.10 = bf16[96,8192]{1,0:T(8,128)(2,1)S(1)} copy-done((bf16[96,8192]{1,0:T(8,128)(2,1)S(1)}, bf16[96,8192]{1,0:T(8,128)(2,1)}, u32[]{:S(2)}) %copy-start.10) | copy-done | bytes 1572888
  6.0 1.0 %copy-done.11 = bf16[4,256,256]{2,1,0:T(8,128)(2,1)S(1)} copy-done((bf16[4,256,256]{2,1,0:T(8,128)(2,1)S(1)}, bf16[4,256,256]{2,1,0:T(8,128)(2,1)}, u32[]{:S(2)}) %copy-start.11) | copy-done | bytes 524312
  7.0 0.9 %copy-done.12 = f32[4,64,128]{2,1,0:T(8,128)S(1)} copy-done((f32[4,64,128]{2,1,0:T(8,128)S(1)}, f32[4,64,128]{2,1,0:T(8,128)}, u32[]{:S(2)}) %copy-start.12) | copy-done | bytes 131096
  7.9 0.8 copy-done.13
  8.8 0.8 copy-done.14
  9.6 0.8 copy-done.15
  10.3 6.3 %filter.1 = (f32[512,256]{1,0:T(8,128)S(1)}, f32[8,128]{1,0:T(8,128)S(1)}, bf16[128,192]{1,0:T(8,128)(2,1)S(1)}, bf16[64,384]{1,0:T(8,128)(2,1)S(1)}, f32[4,64,1...) custom-call(bf16[96,8192]{1,0:T(8,128)(2,1)S(1)} %copy-done.10, ...), custom_call_target="tpu_custom_call" | custom-call | flops 2000000000 | bytes 5000000 | tf_op jit(solution)/shard_map/filter/pallas_call | solution.py:289
  16.6 8.8 %collective-permute-start = (bf16[512,2048]{1,0:T(8,128)(2,1)S(1)}, bf16[512,2048]{1,0:T(8,128)(2,1)S(1)}, u32[]{:S(2)}, u32[]{:S(2)}) collective-permute-start(bf16[512,2048]{1,0:T(8,128)(2,1)S(1)} %copy-done), channel_id=1, source_target_pairs={{0,1},{1,0},{2,3},{3,2},{4,5},{5,4},{6,7},{7,6},{8,9},{9,8},{10,11... | collective-permute-start | bytes 6291464 | tf_op jit(solution)/shard_map/ppermute | solution.py:302
  25.4 0.0 copy-done.1
  25.4 0.0 copy-done.2
  25.4 0.9 prep.1
  26.3 26.2 %all_to_all.15.field_ref = bf16[64,24,128]{2,1,0:T(8,128)(2,1)S(1)} all-to-all(bf16[64,24,128]{2,1,0:T(8,128)(2,1)S(1)} %prep.1), channel_id=1, replica_groups=mesh['ctx'=64,'ch'=8] {'ctx'}, dimensions={0} | all-to-all | bytes 786432 | tf_op jit(solution)/shard_map/all_to_all | solution.py:284
  52.5 2.3 %convolve.1 = bf16[512,128]{1,0:T(8,128)(2,1)S(1)} custom-call(bf16[64,24,128]{2,1,0:T(8,128)(2,1)S(1)} %all_to_all.15.field_ref, f32[512,256]{1,0:T(8,128)S(1)} %get-tuple-element.14.spec_ref, f32[8,128]{1,0:T(8,128)S(1)} %get-tuple-element.16.par_ref, bf16[128,192]{1,0:T(8,128)(2,1)S(1)} %get-tuple-element.17.first_ref, ...), custom_call_target="tpu_custom_call" | custom-call | tf_op jit(solution)/shard_map/convolve/pallas_call | solution.py:303
  54.8 21.1 %all_to_all.16 = bf16[128,4,128]{2,1,0:T(4,128)(2,1)S(1)} all-to-all(bf16[128,4,128]{2,1,0:T(4,128)(2,1)S(1)} %bitcast.6), channel_id=1, replica_groups={{0,8,16,24,32,40,48,56,64,72,80,88,96,104,112,120,128,136,144,152,160,1..., dimensions={0} | all-to-all | bytes 262144 | tf_op jit(solution)/shard_map/all_to_all | solution.py:311
  75.9 0.0 collective-permute-done.other_ref
  75.9 0.9 %project.1 = bf16[64,2048]{1,0:T(8,128)(2,1)S(1)} custom-call(bf16[512,128]{1,0:T(8,128)(2,1)S(1)} %bitcast.7, bf16[512,2048]{1,0:T(8,128)(2,1)S(1)} %copy-done, bf16[512,2048]{1,0:T(8,128)(2,1)S(1)} %collective-permute-done.other_ref), custom_call_target="tpu_custom_call" | custom-call | tf_op jit(solution)/shard_map/project/pallas_call | solution.py:313
  76.8 9.4 %all_to_all.17 = bf16[4,16,2048]{2,1,0:T(8,128)(2,1)S(1)} all-to-all(bf16[4,16,2048]{2,1,0:T(8,128)(2,1)S(1)} %bitcast.5), channel_id=1, replica_groups={{0,2,4,6},{1,3,5,7},{8,10,12,14},{9,11,13,15},{16,18,20,22},{17,19,21,2..., dimensions={0} | all-to-all | bytes 524288 | tf_op jit(solution)/shard_map/all_to_all | solution.py:320
  86.2 0.7 reduce_sum.12
  (18 shorter events, 0.0 us)
Async XLA Ops:
  0.0 0.9 %copy-start.4 = (f32[64,512]{1,0:T(8,128)S(1)}, f32[64,512]{1,0:T(8,128)}, u32[]{:S(2)}) copy-start(f32[64,512]{1,0:T(8,128)} %w_out_hbm.1) | copy-start | bytes 393220
  0.9 0.8 copy-start.5
  1.7 0.8 copy-start.6
  2.5 0.7 copy-start.7
  3.2 0.7 copy-start.8
  3.9 0.7 copy-start.9
  4.6 1.4 %copy-start.10 = (bf16[96,8192]{1,0:T(8,128)(2,1)S(1)}, bf16[96,8192]{1,0:T(8,128)(2,1)}, u32[]{:S(2)}) copy-start(bf16[96,8192]{1,0:T(8,128)(2,1)} %constant.20.clone.feat_hbm) | copy-start | bytes 4718596
  6.0 1.0 %copy-start.11 = (bf16[4,256,256]{2,1,0:T(8,128)(2,1)S(1)}, bf16[4,256,256]{2,1,0:T(8,128)(2,1)}, u32[]{:S(2)}) copy-start(bf16[4,256,256]{2,1,0:T(8,128)(2,1)} %constant.18.clone.mats_hbm) | copy-start | bytes 1572868
  7.0 0.9 %copy-start.12 = (f32[4,64,128]{2,1,0:T(8,128)S(1)}, f32[4,64,128]{2,1,0:T(8,128)}, u32[]{:S(2)}) copy-start(f32[4,64,128]{2,1,0:T(8,128)} %constant.17.clone.tw_hbm) | copy-start | bytes 393220
  7.9 0.8 copy-start.13
  8.8 0.8 copy-start.14
  9.5 0.8 copy-start.15
  10.3 6.3 %copy-start = (bf16[512,2048]{1,0:T(8,128)(2,1)S(1)}, bf16[512,2048]{1,0:T(8,128)(2,1)}, u32[]{:S(2)}) copy-start(bf16[512,2048]{1,0:T(8,128)(2,1)} %own_ref) | copy-start | bytes 6291460
  10.3 15.1 %copy-start.1 = (bf16[128,512]{1,0:T(8,128)(2,1)S(1)}, bf16[128,512]{1,0:T(8,128)(2,1)}, u32[]{:S(2)}) copy-start(bf16[128,512]{1,0:T(8,128)(2,1)} %query_hbm.1) | copy-start | bytes 393220
  10.3 15.1 %copy-start.2 = (bf16[128,512]{1,0:T(8,128)(2,1)S(1)}, bf16[128,512]{1,0:T(8,128)(2,1)}, u32[]{:S(2)}) copy-start(bf16[128,512]{1,0:T(8,128)(2,1)} %key_hbm.1) | copy-start | bytes 393220
  10.3 15.1 %copy-start.3 = (bf16[128,512]{1,0:T(8,128)(2,1)S(1)}, bf16[128,512]{1,0:T(8,128)(2,1)}, u32[]{:S(2)}) copy-start(bf16[128,512]{1,0:T(8,128)(2,1)} %value_hbm.1) | copy-start | bytes 393220
  16.6 59.3 %collective-permute-start = (bf16[512,2048]{1,0:T(8,128)(2,1)S(1)}, bf16[512,2048]{1,0:T(8,128)(2,1)S(1)}, u32[]{:S(2)}, u32[]{:S(2)}) collective-permute-start(bf16[512,2048]{1,0:T(8,128)(2,1)S(1)} %copy-done), channel_id=1, source_target_pairs={{0,1},{1,0},{2,3},{3,2},{4,5},{5,4},{6,7},{7,6},{8,9},{9,8},{10,11... | collective-permute-start | bytes 6291464 | tf_op jit(solution)/shard_map/ppermute | solution.py:302

commit v3 on v1

v3 whole, which is shorter than its diff:
```python
import math

import jax
import jax.numpy as jnp
import numpy as np
from jax import lax
from jax.experimental import pallas as pl
from jax.experimental.pallas import tpu as pltpu
from jax.sharding import PartitionSpec as P

TOKENS = 8192
BLK = 128
NBLK = 64
CH = 8
BANDS = 16
FEAT = 33
FEAT_PAD = 48
TAPS = 7
UNITS = 64
CHUNK = 2048
STEP = 27
BACK = 19
PACK = (0, 64, 88, 96, 104, 168)
PACK_ROWS = 208
bf16 = jnp.bfloat16
f32 = jnp.float32
highest = lax.Precision.HIGHEST


def first_order():
    return [STEP * n % NBLK for n in range(NBLK)]


def second_place(ctx):
    return BACK * ctx % NBLK


def sine_coefs():
    grid = 0.25 * np.cos((np.arange(400) + 0.5) * math.pi / 400)
    grid = np.concatenate([grid, 0.5 * np.cos((np.arange(800) + 0.5) * math.pi / 800)])
    grid = grid[np.abs(grid) > 1e-3]
    powers = np.stack([grid ** (2 * k + 1) for k in range(7)], 1)
    coef, *_ = np.linalg.lstsq(powers, np.sin(2.0 * math.pi * grid), rcond=None)
    return [float(c) for c in coef]


SINE = sine_coefs()
NEAREST = 1.5 * 2.0**23


def sine_turns(turns):
    rest = turns - ((turns + NEAREST) - NEAREST)
    sq = rest * rest
    acc = sq * SINE[-1] + SINE[-2]
    for c in SINE[-3::-1]:
        acc = acc * sq + c
    return acc * rest


def split(value):
    top = value.astype(bf16)
    return top, (value - top.astype(f32)).astype(bf16)


def mm(left, right):
    return jnp.dot(left, right, preferred_element_type=f32)


def mm_split(value, top_mat, low_mat):
    top, low = split(value)
    return mm(top, top_mat) + mm(low, top_mat) + mm(top, low_mat)


def prep_kernel(query_hbm, key_hbm, value_hbm, w_in_hbm, w_mid_hbm, w_out_hbm, taps_hbm, rate_hbm,
                skip_hbm, out_ref, pack_ref, held, w_in_ref, w_mid_ref, w_out_ref, taps_ref, rate_ref,
                skip_ref, sems):
    sources = (query_hbm, key_hbm, value_hbm, w_out_hbm, taps_hbm, w_mid_hbm, w_in_hbm, rate_hbm, skip_hbm)
    targets = (held.at[0], held.at[1], held.at[2], w_out_ref, taps_ref, w_mid_ref, w_in_ref, rate_ref, skip_ref)
    copies = [pltpu.make_async_copy(src, dst, sems.at[n])
              for n, (src, dst) in enumerate(zip(sources, targets))]
    for copy in copies:
        copy.start()
    sets = []
    for f in range(3):
        copies[f].wait()
        sets.append(held[f].astype(f32).T)
    for slot, ctx in enumerate(first_order()):
        place = second_place(ctx)
        rows = slice(place * CH, (place + 1) * CH)
        out_ref[slot] = jnp.concatenate([turned[rows] for turned in sets], 0).astype(bf16)
    for copy in copies[3:]:
        copy.wait()
    chans = rate_ref.shape[1]
    at_out, at_taps, at_rate, at_skip, at_mid, at_in = PACK
    pack_ref[at_out:at_out + UNITS, :] = w_out_ref[...]
    for f in range(3):
        pack_ref[at_taps + f * 8:at_taps + f * 8 + TAPS, :] = taps_ref[f]
    pack_ref[at_rate:at_rate + 8, :] = jnp.broadcast_to(rate_ref[...], (8, chans))
    pack_ref[at_skip:at_skip + 8, :] = jnp.broadcast_to(skip_ref[...], (8, chans))
    pack_ref[at_mid:at_mid + UNITS, 0:UNITS] = w_mid_ref[...]
    pack_ref[at_in:at_in + FEAT, 0:UNITS] = w_in_ref[...]


def forward(rows_ref, first_ref, tw_ref, mats_ref):
    cols = jnp.concatenate([rows_ref[pl.ds(c, NBLK, stride=CH), :] for c in range(CH)], 1)
    top, low = split(cols)
    outer = mm(first_ref[...], jnp.concatenate([top, low, top], 0))
    tw_re, tw_im = tw_ref[0][...], tw_ref[1][...]
    out = []
    for c in range(CH):
        lanes = slice(c * BLK, (c + 1) * BLK)
        re, im = outer[:NBLK, lanes], outer[NBLK:, lanes]
        out.append(jnp.concatenate([re * tw_re - im * tw_im, re * tw_im + im * tw_re], 1))
    return mm_split(jnp.concatenate(out, 0), mats_ref[0][...], mats_ref[1][...])


def views(wide_ref, table_ref):
    half = 2 * BLK
    spec = wide_ref.at[0:CH * NBLK]
    tw = [wide_ref.at[CH * NBLK:CH * NBLK + NBLK, n * BLK:(n + 1) * BLK] for n in range(2)]
    par = wide_ref.at[CH * NBLK + NBLK:CH * NBLK + NBLK + CH, 0:BLK]
    mats = [table_ref.at[n * half:(n + 1) * half] for n in range(4)]
    first = table_ref.at[4 * half:4 * half + BLK, 0:3 * NBLK]
    last = [table_ref.at[4 * half + BLK + n * NBLK:4 * half + BLK + (n + 1) * NBLK, 0:3 * NBLK]
            for n in range(2)]
    return spec, tw, par, mats, first, last


def fill_tables(first_ref, last_ref, tw_ref, mats_ref):
    def grid(shape, axis):
        return lax.broadcasted_iota(jnp.int32, shape, axis)

    def wave(turns):
        turns = turns - jnp.round(turns)
        return sine_turns(turns + 0.25), sine_turns(turns)

    shape = (NBLK, NBLK)
    cos, sin = wave((grid(shape, 0).astype(f32) - 0.25) * grid(shape, 1).astype(f32) / NBLK)
    top, low = split(jnp.concatenate([cos, -sin], 0))
    first_ref[...] = jnp.concatenate([top, top, low], 1)
    cos, sin = wave((grid(shape, 1).astype(f32) - 0.25) * grid(shape, 0).astype(f32) / NBLK)
    top, low = split(jnp.concatenate([cos, -sin], 1) / TOKENS)
    wide = jnp.concatenate([top, top, low], 1)
    last_ref[0][...], last_ref[1][...] = wide[:, :3 * NBLK], wide[:, 3 * NBLK:]
    shape = (NBLK, BLK)
    shifted = grid(shape, 0).astype(f32) - 0.25
    cos, sin = wave(shifted * grid(shape, 1).astype(f32) / TOKENS)
    tw_ref[0][...], tw_ref[1][...] = cos, -sin
    shape = (BLK, BLK)
    cos, sin = wave((grid(shape, 0) * grid(shape, 1)).astype(f32) / BLK)
    mats = jnp.concatenate([jnp.concatenate([cos, -sin], 1), jnp.concatenate([sin, cos], 1)], 0)
    mats_ref[0][...], mats_ref[1][...] = split(mats)
    mats = jnp.concatenate([jnp.concatenate([cos, sin], 1), jnp.concatenate([-sin, cos], 1)], 0)
    mats_ref[2][...], mats_ref[3][...] = split(mats)


def filter_kernel(pack_ref, wide_ref, table_ref, rows_ref):
    at_out, at_taps, at_rate, at_skip, at_mid, at_in = PACK
    spec_ref, tw_ref, par_ref, mats_ref, first_ref, last_ref = views(wide_ref, table_ref)
    fill_tables(first_ref, last_ref, tw_ref, mats_ref)
    chans = pack_ref.shape[1]
    wanted = second_place(lax.axis_index("ctx")) * CH + lax.broadcasted_iota(jnp.int32, (CH, chans), 0)
    pick = (lax.broadcasted_iota(jnp.int32, (CH, chans), 1) == wanted).astype(f32)

    def mine(table):
        return lax.dot_general(pick, table, (((1,), (1,)), ((), ())), precision=highest,
                               preferred_element_type=f32)

    def stack(weights):
        top, low = split(weights)
        return jnp.concatenate([top, top, low], 1)

    taps = jnp.concatenate([mine(pack_ref[at_taps + f * 8:at_taps + (f + 1) * 8, :])[:, :TAPS]
                            for f in range(3)], 1)
    rate = mine(pack_ref[at_rate:at_rate + 8, :])[:, :1]
    skip = mine(pack_ref[at_skip:at_skip + 8, :])[:, :1]
    par_ref[...] = jnp.concatenate([taps, jnp.zeros((CH, 128 - 3 * TAPS), f32)], 1)
    per_turn = 1.0 / (2.0 * math.pi)
    padded = jnp.concatenate([pack_ref[at_in + 1:at_in + FEAT, 0:UNITS], pack_ref[at_in:at_in + 1, 0:UNITS],
                              jnp.zeros((FEAT_PAD - FEAT, UNITS), f32)], 0)
    w_in = stack(padded.T * per_turn)
    w_mid = stack(pack_ref[at_mid:at_mid + UNITS, 0:UNITS].T * per_turn)
    w_out = stack(mine(pack_ref[at_out:at_out + UNITS, :]))
    gain = jnp.sqrt(2.0 * rate)

    band = lax.broadcasted_iota(jnp.int32, (BANDS, BLK), 0).astype(f32)
    at = lax.broadcasted_iota(jnp.int32, (BANDS, BLK), 1).astype(f32)
    span = float((BANDS - 1) * (BANDS - 1))
    freq = 1.0 + jnp.floor((band * band * (TOKENS // 4 - 1) + 0.5) * (1.0 / span))
    inner = freq * at * (1.0 / TOKENS)
    inner = inner - jnp.round(inner)
    inner_cos, inner_sin = sine_turns(inner + 0.25), sine_turns(inner)
    outer = freq * at * (1.0 / NBLK)
    outer = outer - jnp.round(outer)
    outer_cos, outer_sin = sine_turns(outer + 0.25), sine_turns(outer)
    ramp_row = lax.broadcasted_iota(jnp.int32, (FEAT_PAD - 2 * BANDS, BLK), 0) == 0
    ramp_at = lax.broadcasted_iota(jnp.int32, (FEAT_PAD - 2 * BANDS, BLK), 1).astype(f32)

    def features(a):
        turn_cos, turn_sin = outer_cos[:, a:a + 1], outer_sin[:, a:a + 1]
        ramp = jnp.where(ramp_row, (ramp_at + float(a * BLK)) * (1.0 / TOKENS), 0.0)
        return jnp.concatenate([inner_cos * turn_cos - inner_sin * turn_sin,
                                inner_sin * turn_cos + inner_cos * turn_sin, ramp], 0)

    lane = lax.broadcasted_iota(jnp.int32, (CH, CHUNK), 1).astype(f32)
    per_chunk = CHUNK // BLK
    for chunk in range(TOKENS // CHUNK):
        feat = jnp.concatenate([features(chunk * per_chunk + n) for n in range(per_chunk)], 1)
        top, low = split(feat)
        one = sine_turns(mm(w_in, jnp.concatenate([top, low, top], 0)))
        top, low = split(one)
        two = sine_turns(mm(w_mid, jnp.concatenate([top, low, top], 0)))
        top, low = split(two)
        shape = mm(w_out, jnp.concatenate([top, low, top], 0))
        taper = gain * jnp.exp(-rate * (lane + float(chunk * CHUNK))) * shape
        for n in range(per_chunk):
            first_row = (chunk * per_chunk + n) * CH
            rows_ref[first_row:first_row + CH, :] = taper[:, n * BLK:(n + 1) * BLK]
    spec = forward(rows_ref, first_ref, tw_ref, mats_ref)
    direct = jnp.concatenate([jnp.broadcast_to(skip[c:c + 1], (NBLK, BLK)) for c in range(CH)], 0)
    spec_ref[:, :BLK] = spec[:, :BLK] + direct
    spec_ref[:, BLK:] = spec[:, BLK:]


def conv_kernel(field_ref, wide_ref, table_ref, out_ref, query_ref, prod_ref, conv_ref):
    spec_ref, tw_ref, par_ref, mats_ref, first_ref, last_ref = views(wide_ref, table_ref)
    par = par_ref[...]
    taps = [jnp.broadcast_to(par[:, n:n + 1], (CH, BLK))[None] for n in range(3 * TAPS)]
    span = 8
    lane = lax.broadcasted_iota(jnp.int32, (span + 1, CH, BLK), 2)

    def later(value, steps):
        turned = pltpu.roll(value, steps, 2)
        return jnp.where(lane < steps, jnp.concatenate([turned[:1], turned[:-1]], 0), turned)

    for start in range(0, NBLK, span):
        block = [field_ref[BACK * n % NBLK].astype(f32) for n in range(max(start - 1, 0), start + span)]
        if start == 0:
            block = [jnp.zeros_like(block[0])] + block
        block = jnp.stack(block, 0)
        mixed = []
        for f in range(3):
            now = block[:, f * CH:(f + 1) * CH, :]
            past = later(now, 1)
            t = taps[f * TAPS:(f + 1) * TAPS]
            total = later(t[6] * now, 2) + (t[4] * now + t[5] * past)
            total = later(total, 2) + (t[2] * now + t[3] * past)
            total = later(total, 2) + (t[0] * now + t[1] * past)
            mixed.append(total[1:].astype(bf16).reshape(span * CH, BLK))
        at = slice(start * CH, (start + span) * CH)
        prod_ref[at, :] = mixed[1].astype(f32) * mixed[2].astype(f32)
        query_ref[at, :] = mixed[0].astype(f32)
    spec = forward(prod_ref, first_ref, tw_ref, mats_ref)
    s_re, s_im = spec[:, :BLK], spec[:, BLK:]
    h_re, h_im = spec_ref[:, :BLK], spec_ref[:, BLK:]
    both = jnp.concatenate([s_re * h_re - s_im * h_im, s_re * h_im + s_im * h_re], 1)
    back = mm_split(both, mats_ref[2][...], mats_ref[3][...])
    tw_re, tw_im = tw_ref[0][...], tw_ref[1][...]
    cols = []
    for c in range(CH):
        re, im = back[c * NBLK:(c + 1) * NBLK, :BLK], back[c * NBLK:(c + 1) * NBLK, BLK:]
        cols.append(jnp.concatenate([re * tw_re + im * tw_im, im * tw_re - re * tw_im], 0))
    top, low = split(jnp.concatenate(cols, 1))
    last = jnp.concatenate([last_ref[0][...], last_ref[1][...]], 1)
    conv = mm(last, jnp.concatenate([top, low, top], 0))
    for c in range(CH):
        conv_ref[pl.ds(c, NBLK, stride=CH), :] = conv[:, c * BLK:(c + 1) * BLK]
    order = first_order()
    for slot in range(0, NBLK, 2):
        gated = []
        for ctx in order[slot:slot + 2]:
            rows = slice(ctx * CH, (ctx + 1) * CH)
            gated.append(query_ref[rows, :] * conv_ref[rows, :])
        out_ref[slot * CH:(slot + 2) * CH, :] = jnp.concatenate(gated, 0).astype(bf16)


def per_device(query_field, key_field, value_field, short_taps, filt_in, filt_mid, filt_out,
               decay_rate, skip_gain, out_weight):
    chans = query_field.shape[1]
    groups = lax.axis_size("ch")
    params = pltpu.CompilerParams(vmem_limit_bytes=32 * 1024 * 1024)
    far = pl.BlockSpec(memory_space=pltpu.HBM)
    operands = (query_field, key_field, value_field, filt_in, filt_mid, filt_out, short_taps,
                decay_rate.reshape(1, chans), skip_gain.reshape(1, chans))
    parts, pack = pl.pallas_call(
        prep_kernel,
        out_shape=[jax.ShapeDtypeStruct((NBLK, 3 * CH, BLK), bf16),
                   jax.ShapeDtypeStruct((PACK_ROWS, chans), f32)],
        in_specs=[far] * len(operands),
        scratch_shapes=[pltpu.VMEM((3,) + query_field.shape, bf16)]
        + [pltpu.VMEM(t.shape, t.dtype) for t in operands[3:]]
        + [pltpu.SemaphoreType.DMA((len(operands),))],
        compiler_params=pltpu.CompilerParams(vmem_limit_bytes=62 * 1024 * 1024),
        name="prep",
    )(*operands)
    fields = lax.all_to_all(parts, "ctx", 0, 0, tiled=True, axis_index_groups=[first_order()])
    wide, table = pl.pallas_call(
        filter_kernel,
        out_shape=[jax.ShapeDtypeStruct((CH * NBLK + NBLK + CH, 2 * BLK), f32),
                   jax.ShapeDtypeStruct((8 * BLK + 2 * BLK, 2 * BLK), bf16)],
        scratch_shapes=[pltpu.VMEM((NBLK * CH, BLK), f32)],
        compiler_params=params,
        cost_estimate=pl.CostEstimate(flops=2 * 10**9, bytes_accessed=5 * 10**6, transcendentals=10**6),
        name="filter",
    )(pack)
    gated = pl.pallas_call(
        conv_kernel,
        out_shape=jax.ShapeDtypeStruct((NBLK * CH, BLK), bf16),
        scratch_shapes=[pltpu.VMEM((NBLK * CH, BLK), f32)] * 3,
        compiler_params=params,
        cost_estimate=pl.CostEstimate(flops=10**11, bytes_accessed=10**9, transcendentals=0),
        name="convolve",
    )(fields, wide, table)
    returned = lax.all_to_all(gated.reshape(NBLK, CH, BLK), "ctx", 0, 0, tiled=True,
                              axis_index_groups=[first_order()])
    partial = lax.dot_general(returned.reshape(chans, BLK), out_weight, (((0,), (0,)), ((), ())),
                              preferred_element_type=f32).astype(bf16)
    shares = lax.all_to_all(partial.reshape(groups, BLK // groups, -1), "ch", 0, 0, tiled=True,
                            axis_index_groups=None)
    return jnp.sum(shares.astype(f32), 0).astype(bf16)


def solution(mesh):
    return jax.shard_map(
        per_device,
        mesh=mesh,
        in_specs=(
            P("ctx", "ch"),
            P("ctx", "ch"),
            P("ctx", "ch"),
            P(None, None, "ch"),
            P(),
            P(),
            P(None, "ch"),
            P("ch"),
            P("ch"),
            P("ch", None),
        ),
        out_specs=P(("ctx", "ch"), None),
        check_vma=False,
    )
```

time: 80.2 us -> 70.8 us (0.88)
  local copies, waits for them, and re-layouts: 12.9 us -> 1 us
  waiting for transfers between devices: 1.84 us -> 7.77 us
  blocking collectives: 37.7 us -> 34.7 us
  Pallas kernels: 7.67 us -> 8.68 us
  other arithmetic: 1.53 us -> 0.7 us
    unnamed x39 -> x4, local copies, waits for them, and re-layouts: 12.3 us -> 1 us
    all_to_all x1, waiting for transfers between devices: 1.84 us -> 7.77 us  [per_device(): lax.all_to_all(parts, 'ctx', 0, 0, tiled=True, axis_index_groups=[first_o...]
    all_to_all x2, blocking collectives: 37.7 us -> 34.7 us  [the longest x1 18.8 us: per_device(): lax.all_to_all(gated.reshape(NBLK, CH, BLK), 'ctx', 0, 0, tiled=True, axi...]
    pallas_call x1 -> x2, Pallas kernels: 5.54 us -> 6.68 us  [the longest x1 4.47 us: per_device(): pl.pallas_call(filter_kernel, out_shape=[jax.ShapeDtypeStruct((CH * NBLK...]
    reshape x1 -> x0, other arithmetic: 0.83 us -> none  [per_device(): jnp.transpose(stacked.reshape(3, tok, NBLK, CH), (2, 0, 3, 1))]
  transfers between devices with their start and end apart: 1 -> 1, of which waited for: 1 -> 1; matrix products, arithmetic and copies ran while one was open for 2% -> 0% of each run, Pallas kernels for 7% -> 6%
where the time goes in v3:
time: 70.8 us; the launch traced here: 70.5 us
  blocking collectives  34.7 us (49%)
  starting transfers between devices  17.1 us (24%)
  Pallas kernels  8.68 us (12%)
  waiting for transfers between devices  7.77 us (11%)
  local copies, waits for them, and re-layouts  1 us (1%)
    all_to_all x1, blocking collectives, per_device(): lax.all_to_all(gated.reshape(NBLK, CH, BLK), 'ctx', 0, 0, tiled=True, axi...  18.8 us
    all_to_all x1, starting transfers between devices, per_device(): lax.all_to_all(parts, 'ctx', 0, 0, tiled=True, axis_index_groups=[first_o...  17.1 us
    all_to_all x1, blocking collectives, per_device(): lax.all_to_all(partial.reshape(groups, BLK // groups, -1), 'ch', 0, 0, ti...  15.8 us
    all_to_all x1, waiting for transfers between devices, per_device(): lax.all_to_all(parts, 'ctx', 0, 0, tiled=True, axis_index_groups=[first_o...  7.77 us
    pallas_call x1, Pallas kernels, per_device(): pl.pallas_call(filter_kernel, out_shape=[jax.ShapeDtypeStruct((CH * NBLK...  4.47 us
    pallas_call x1, Pallas kernels, per_device(): pl.pallas_call(prep_kernel, out_shape=[jax.ShapeDtypeStruct((NBLK, 3 * CH...  2.21 us
    pallas_call x1, Pallas kernels, per_device(): pl.pallas_call(conv_kernel, out_shape=jax.ShapeDtypeStruct((NBLK * CH, BL...  2 us
  transfers between devices with their start and end apart: 1, of which 1 were waited for; matrix products, arithmetic and copies ran while one was open for 0% of the time, Pallas kernels for 6%

profile of v3, /device:TPU:1, one launch (start us, length us, event | category | flops | bytes accessed | tf_op | source)
XLA Modules:
  0.0 70.5 jit_solution(15809095700576884903)
XLA Ops:
  0.0 2.2 %prep.1 = (bf16[64,24,128]{2,1,0:T(8,128)(2,1)}, f32[208,512]{1,0:T(8,128)}) custom-call(bf16[128,512]{1,0:T(8,128)(2,1)} %query_hbm.1, bf16[128,512]{1,0:T(8,128)(2,1)} %key_hbm.1, bf16[128,512]{1,0:T(8,128)(2,1)} %value_hbm.1, f32[33,64]{1,0:T(8,128)} %w_in_hbm.1, f32[64,64]{1,0:T(8,128)} %w_mid_hbm.1, f32[64,512]{1,0:T(8,128)} %w_out_hbm.1, ...), custom_call_target="tpu_custom_call" | custom-call | tf_op jit(solution)/shard_map/prep/pallas_call | solution.py:285
  2.2 17.1 %all-to-all-start = ((bf16[64,24,128]{2,1,0:T(8,128)(2,1)}), bf16[64,24,128]{2,1,0:T(8,128)(2,1)S(1)}, u32[]{:S(2)}, u32[]{:S(2)}) async-start(bf16[64,24,128]{2,1,0:T(8,128)(2,1)} %get-tuple-element.9), calls=%async_computation | async-start | bytes 786432 | tf_op jit(solution)/shard_map/all_to_all | solution.py:296
  19.4 0.0 copy-start
  19.4 1.0 %copy-done = f32[208,512]{1,0:T(8,128)S(1)} copy-done((f32[208,512]{1,0:T(8,128)S(1)}, f32[208,512]{1,0:T(8,128)}, u32[]{:S(2)}) %copy-start) | copy-done | bytes 426008
  20.4 4.5 %filter.1 = (f32[584,256]{1,0:T(8,128)S(1)}, bf16[1280,256]{1,0:T(8,128)(2,1)S(1)}) custom-call(f32[208,512]{1,0:T(8,128)S(1)} %copy-done), custom_call_target="tpu_custom_call" | custom-call | flops 2000000000 | bytes 5000000 | tf_op jit(solution)/shard_map/filter/pallas_call | solution.py:297
  24.9 7.8 %all-to-all-done.field_ref = bf16[64,24,128]{2,1,0:T(8,128)(2,1)S(1)} async-done(((bf16[64,24,128]{2,1,0:T(8,128)(2,1)}), bf16[64,24,128]{2,1,0:T(8,128)(2,1)S(1)}, u32[]{:S(2)}, u32[]{:S(2)}) %all-to-all-start) | async-done | bytes 393248 | tf_op jit(solution)/shard_map/all_to_all | solution.py:296
  32.6 0.0 copy-start.1
  32.6 2.0 %convolve.1 = bf16[512,128]{1,0:T(8,128)(2,1)S(1)} custom-call(bf16[64,24,128]{2,1,0:T(8,128)(2,1)S(1)} %all-to-all-done.field_ref, f32[584,256]{1,0:T(8,128)S(1)} %get-tuple-element.11.wide_ref, bf16[1280,256]{1,0:T(8,128)(2,1)S(1)} %get-tuple-element.12.table_ref), custom_call_target="tpu_custom_call" | custom-call | flops 99999997952 | bytes 1000000000 | tf_op jit(solution)/shard_map/convolve/pallas_call | solution.py:306
  34.6 18.8 %all_to_all.15 = bf16[64,8,128]{2,1,0:T(8,128)(2,1)S(1)} all-to-all(bf16[64,8,128]{2,1,0:T(8,128)(2,1)S(1)} %bitcast.8), channel_id=1, replica_groups={{0,216,432,136,352,56,272,488,192,408,112,328,32,248,464,168,384,88,304..., dimensions={0} | all-to-all | bytes 262144 | tf_op jit(solution)/shard_map/all_to_all | solution.py:314
  53.5 0.0 copy-done.1
  53.5 0.5 convolution_convert_fusion
  54.0 15.8 %all_to_all.16 = bf16[8,16,2048]{2,1,0:T(8,128)(2,1)S(1)} all-to-all(bf16[8,16,2048]{2,1,0:T(8,128)(2,1)S(1)} %bitcast.9), channel_id=1, replica_groups=mesh['ctx'=64,'ch'=8] {'ch'}, dimensions={0} | all-to-all | bytes 1048576 | tf_op jit(solution)/shard_map/all_to_all | solution.py:318
  69.8 0.7 reduce_sum.12
Async XLA Ops:
  2.2 30.4 %all-to-all-start = ((bf16[64,24,128]{2,1,0:T(8,128)(2,1)}), bf16[64,24,128]{2,1,0:T(8,128)(2,1)S(1)}, u32[]{:S(2)}, u32[]{:S(2)}) async-start(bf16[64,24,128]{2,1,0:T(8,128)(2,1)} %get-tuple-element.9), calls=%async_computation | async-start | bytes 786432 | tf_op jit(solution)/shard_map/all_to_all | solution.py:296
  19.4 1.0 %copy-start = (f32[208,512]{1,0:T(8,128)S(1)}, f32[208,512]{1,0:T(8,128)}, u32[]{:S(2)}) copy-start(f32[208,512]{1,0:T(8,128)} %get-tuple-element.10.pack_ref) | copy-start | bytes 1277956
  32.6 20.9 %copy-start.1 = (bf16[512,2048]{1,0:T(8,128)(2,1)S(1)}, bf16[512,2048]{1,0:T(8,128)(2,1)}, u32[]{:S(2)}) copy-start(bf16[512,2048]{1,0:T(8,128)(2,1)} %param.19) | copy-start | bytes 6291460

commit v4 on v3

--- a/solution.py
+++ b/solution.py
@@ -15,6 +15,8 @@
 BANDS = 16
 FEAT = 33
 FEAT_PAD = 48
+HALF = 64
+SHARE = 16
 TAPS = 7
 UNITS = 64
 CHUNK = 2048
@@ -31,8 +33,16 @@
     return [STEP * n % NBLK for n in range(NBLK)]
 
 
+def second_order():
+    order = []
+    for n in range(NBLK):
+        turned = int(format(n, "06b")[::-1], 2)
+        order.append(turned % 8 * 8 + turned // 8)
+    return order
+
+
 def second_place(ctx):
-    return BACK * ctx % NBLK
+    return sum((ctx // 2 ** src % 2) * 2 ** dst for src, dst in enumerate((2, 1, 0, 5, 4, 3)))
 
 
 def sine_coefs():
@@ -69,6 +79,14 @@
 def mm_split(value, top_mat, low_mat):
     top, low = split(value)
     return mm(top, top_mat) + mm(low, top_mat) + mm(top, low_mat)
+
+
+def lift(rows, low_half):
+    return jnp.where(low_half, rows[0], pltpu.roll(rows[1], 4, 1))
+
+
+def drop(rows, low_half):
+    return jnp.where(low_half, pltpu.roll(rows[0], 4, 1), rows[1])
 
 
 def prep_kernel(query_hbm, key_hbm, value_hbm, w_in_hbm, w_mid_hbm, w_out_hbm, taps_hbm, rate_hbm,
@@ -80,14 +98,15 @@
               for n, (src, dst) in enumerate(zip(sources, targets))]
     for copy in copies:
         copy.start()
+    low_half = lax.broadcasted_iota(jnp.int32, (NBLK // 2, CH, BLK), 1) < 4
     sets = []
     for f in range(3):
         copies[f].wait()
-        sets.append(held[f].astype(f32).T)
+        turned = held[f].astype(f32).T.reshape(2, NBLK // 2, CH, BLK)
+        sets.append((lift(turned, low_half), drop(turned, low_half)))
     for slot, ctx in enumerate(first_order()):
         place = second_place(ctx)
-        rows = slice(place * CH, (place + 1) * CH)
-        out_ref[slot] = jnp.concatenate([turned[rows] for turned in sets], 0).astype(bf16)
+        out_ref[slot] = jnp.concatenate([pair[place % 2][place // 2] for pair in sets], 0).astype(bf16)
     for copy in copies[3:]:
         copy.wait()
     chans = rate_ref.shape[1]
@@ -119,9 +138,9 @@
     spec = wide_ref.at[0:CH * NBLK]
     tw = [wide_ref.at[CH * NBLK:CH * NBLK + NBLK, n * BLK:(n + 1) * BLK] for n in range(2)]
     par = wide_ref.at[CH * NBLK + NBLK:CH * NBLK + NBLK + CH, 0:BLK]
-    mats = [table_ref.at[n * half:(n + 1) * half] for n in range(4)]
-    first = table_ref.at[4 * half:4 * half + BLK, 0:3 * NBLK]
-    last = [table_ref.at[4 * half + BLK + n * NBLK:4 * half + BLK + (n + 1) * NBLK, 0:3 * NBLK]
+    mats = [table_ref.at[n * half:(n + 1) * half] for n in range(2)]
+    first = table_ref.at[2 * half:2 * half + BLK, 0:3 * NBLK]
+    last = [table_ref.at[2 * half + BLK + n * NBLK:2 * half + BLK + (n + 1) * NBLK, 0:3 * NBLK]
             for n in range(2)]
     return spec, tw, par, mats, first, last
 
@@ -150,37 +169,42 @@
     cos, sin = wave((grid(shape, 0) * grid(shape, 1)).astype(f32) / BLK)
     mats = jnp.concatenate([jnp.concatenate([cos, -sin], 1), jnp.concatenate([sin, cos], 1)], 0)
     mats_ref[0][...], mats_ref[1][...] = split(mats)
-    mats = jnp.concatenate([jnp.concatenate([cos, sin], 1), jnp.concatenate([-sin, cos], 1)], 0)
-    mats_ref[2][...], mats_ref[3][...] = split(mats)
-
-
-def filter_kernel(pack_ref, wide_ref, table_ref, rows_ref):
+
+
+def weights_kernel(pack_ref, small_ref, stack_ref):
+    at_out, at_taps, at_rate, at_skip, at_mid, at_in = PACK
+    chans = pack_ref.shape[1]
+    row = lax.broadcasted_iota(jnp.int32, (CH, chans), 0)
+    wanted = second_place(lax.axis_index("ctx")) * 4 + row % 4 + row // 4 * (chans // 2)
+    pick = (lax.broadcasted_iota(jnp.int32, (CH, chans), 1) == wanted).astype(f32)
+
+    def stack(weights):
+        top, low = split(weights)
+        return jnp.concatenate([top, top, low], 1)
+
+    mine = lax.dot_general(pick, pack_ref[:at_mid, :], (((1,), (1,)), ((), ())), precision=highest,
+                           preferred_element_type=f32)
+    per_turn = 1.0 / (2.0 * math.pi)
+    padded = jnp.concatenate([pack_ref[at_in + 1:at_in + FEAT, 0:UNITS], pack_ref[at_in:at_in + 1, 0:UNITS],
+                              jnp.zeros((FEAT_PAD - FEAT, UNITS), f32)], 0)
+    small_ref[:, 0:at_mid] = mine
+    stack_ref[0:UNITS, 0:3 * FEAT_PAD] = stack(padded.T * per_turn)
+    stack_ref[UNITS:2 * UNITS, 0:3 * UNITS] = stack(pack_ref[at_mid:at_mid + UNITS, 0:UNITS].T * per_turn)
+    wide = stack(mine[:, at_out:at_out + UNITS])
+    stack_ref[2 * UNITS:2 * UNITS + 2 * CH, 0:3 * UNITS] = jnp.concatenate([wide, wide], 0)
+
+
+def filter_kernel(small_ref, stack_ref, wide_ref, table_ref, rows_ref):
     at_out, at_taps, at_rate, at_skip, at_mid, at_in = PACK
     spec_ref, tw_ref, par_ref, mats_ref, first_ref, last_ref = views(wide_ref, table_ref)
     fill_tables(first_ref, last_ref, tw_ref, mats_ref)
-    chans = pack_ref.shape[1]
-    wanted = second_place(lax.axis_index("ctx")) * CH + lax.broadcasted_iota(jnp.int32, (CH, chans), 0)
-    pick = (lax.broadcasted_iota(jnp.int32, (CH, chans), 1) == wanted).astype(f32)
-
-    def mine(table):
-        return lax.dot_general(pick, table, (((1,), (1,)), ((), ())), precision=highest,
-                               preferred_element_type=f32)
-
-    def stack(weights):
-        top, low = split(weights)
-        return jnp.concatenate([top, top, low], 1)
-
-    taps = jnp.concatenate([mine(pack_ref[at_taps + f * 8:at_taps + (f + 1) * 8, :])[:, :TAPS]
-                            for f in range(3)], 1)
-    rate = mine(pack_ref[at_rate:at_rate + 8, :])[:, :1]
-    skip = mine(pack_ref[at_skip:at_skip + 8, :])[:, :1]
-    par_ref[...] = jnp.concatenate([taps, jnp.zeros((CH, 128 - 3 * TAPS), f32)], 1)
-    per_turn = 1.0 / (2.0 * math.pi)
-    padded = jnp.concatenate([pack_ref[at_in + 1:at_in + FEAT, 0:UNITS], pack_ref[at_in:at_in + 1, 0:UNITS],
-                              jnp.zeros((FEAT_PAD - FEAT, UNITS), f32)], 0)
-    w_in = stack(padded.T * per_turn)
-    w_mid = stack(pack_ref[at_mid:at_mid + UNITS, 0:UNITS].T * per_turn)
-    w_out = stack(mine(pack_ref[at_out:at_out + UNITS, :]))
+    w_in = stack_ref[0:UNITS, 0:3 * FEAT_PAD]
+    w_mid = stack_ref[UNITS:2 * UNITS, 0:3 * UNITS]
+    w_out = stack_ref[2 * UNITS:2 * UNITS + 2 * CH, 0:3 * UNITS]
+    taps = [small_ref[:, at_taps + f * 8:at_taps + f * 8 + TAPS] for f in range(3)]
+    rate = small_ref[:, at_rate:at_rate + 1]
+    skip = small_ref[:, at_skip:at_skip + 1]
+    par_ref[...] = jnp.concatenate(taps + [jnp.zeros((CH, 128 - 3 * TAPS), f32)], 1)
     gain = jnp.sqrt(2.0 * rate)
 
     band = lax.broadcasted_iota(jnp.int32, (BANDS, BLK), 0).astype(f32)
@@ -211,7 +235,7 @@
         top, low = split(one)
         two = sine_turns(mm(w_mid, jnp.concatenate([top, low, top], 0)))
         top, low = split(two)
-        shape = mm(w_out, jnp.concatenate([top, low, top], 0))
+        shape = mm(w_out, jnp.concatenate([top, low, top], 0))[:CH]
         taper = gain * jnp.exp(-rate * (lane + float(chunk * CHUNK))) * shape
         for n in range(per_chunk):
             first_row = (chunk * per_chunk + n) * CH
@@ -222,7 +246,9 @@
     spec_ref[:, BLK:] = spec[:, BLK:]
 
 
-def conv_kernel(field_ref, wide_ref, table_ref, out_ref, query_ref, prod_ref, conv_ref):
+def conv_kernel(field_ref, wide_ref, table_ref, other_hbm, out_ref, other_ref, query_ref, prod_ref, conv_ref, sem):
+    swap = pltpu.make_async_copy(other_hbm, other_ref, sem)
+    swap.start()
     spec_ref, tw_ref, par_ref, mats_ref, first_ref, last_ref = views(wide_ref, table_ref)
     par = par_ref[...]
     taps = [jnp.broadcast_to(par[:, n:n + 1], (CH, BLK))[None] for n in range(3 * TAPS)]
@@ -253,31 +279,66 @@
     spec = forward(prod_ref, first_ref, tw_ref, mats_ref)
     s_re, s_im = spec[:, :BLK], spec[:, BLK:]
     h_re, h_im = spec_ref[:, :BLK], spec_ref[:, BLK:]
-    both = jnp.concatenate([s_re * h_re - s_im * h_im, s_re * h_im + s_im * h_re], 1)
-    back = mm_split(both, mats_ref[2][...], mats_ref[3][...])
+    both = jnp.concatenate([s_re * h_re - s_im * h_im, -(s_re * h_im + s_im * h_re)], 1)
+    back = mm_split(both, mats_ref[0][...], mats_ref[1][...])
     tw_re, tw_im = tw_ref[0][...], tw_ref[1][...]
     cols = []
     for c in range(CH):
         re, im = back[c * NBLK:(c + 1) * NBLK, :BLK], back[c * NBLK:(c + 1) * NBLK, BLK:]
-        cols.append(jnp.concatenate([re * tw_re + im * tw_im, im * tw_re - re * tw_im], 0))
+        cols.append(jnp.concatenate([re * tw_re - im * tw_im, -(re * tw_im + im * tw_re)], 0))
     top, low = split(jnp.concatenate(cols, 1))
     last = jnp.concatenate([last_ref[0][...], last_ref[1][...]], 1)
     conv = mm(last, jnp.concatenate([top, low, top], 0))
     for c in range(CH):
         conv_ref[pl.ds(c, NBLK, stride=CH), :] = conv[:, c * BLK:(c + 1) * BLK]
-    order = first_order()
-    for slot in range(0, NBLK, 2):
+    sub = lax.broadcasted_iota(jnp.int32, (CH, BLK), 0) < 4
+    same = sub == (lax.broadcasted_iota(jnp.int32, (CH, BLK), 1) < HALF)
+    order = second_order()
+    lane = lax.broadcasted_iota(jnp.int32, (BLK, BLK), 1)
+    token = lane // HALF * SHARE + lane % HALF // SHARE * (2 * SHARE) + lane % SHARE
+    reorder = (lax.broadcasted_iota(jnp.int32, (BLK, BLK), 0) == token).astype(f32).astype(bf16)
+
+    for slot in range(0, NBLK, 8):
         gated = []
-        for ctx in order[slot:slot + 2]:
+        for ctx in order[slot:slot + 8]:
             rows = slice(ctx * CH, (ctx + 1) * CH)
             gated.append(query_ref[rows, :] * conv_ref[rows, :])
-        out_ref[slot * CH:(slot + 2) * CH, :] = jnp.concatenate(gated, 0).astype(bf16)
+        gated = mm(jnp.concatenate(gated, 0).astype(bf16), reorder)
+        tops, lows = [], []
+        for n in range(0, 8, 2):
+            pair = []
+            for at in (n * CH, (n + 1) * CH):
+                rows = gated[at:at + CH]
+                pair.append(jnp.where(same, rows, pltpu.roll(pltpu.roll(rows, 4, 0), HALF, 1)))
+            tops.append(jnp.where(sub, pair[0], pltpu.roll(pair[1], 4, 0)))
+            lows.append(jnp.where(sub, pltpu.roll(pair[0], 4, 0), pair[1]))
+        at = slot * 4
+        out_ref[at:at + 32, :] = jnp.concatenate(tops, 0).astype(bf16)
+        out_ref[at + NBLK * 4:at + NBLK * 4 + 32, :] = jnp.concatenate(lows, 0).astype(bf16)
+    swap.wait()
+
+
+def project_kernel(rows_ref, own_ref, other_ref, out_ref):
+    core = lax.axis_index("ch") % 2
+    depth = rows_ref.shape[0] // 2
+
+    def turned(part):
+        rows = rows_ref[pl.ds(pl.multiple_of(part * depth, depth), depth), :]
+        return rows.astype(f32).T.astype(bf16)
+
+    own, other = turned(core), turned(1 - core)
+    total = mm(own[:HALF], own_ref[:depth, :]) + mm(own[HALF:], own_ref[depth:, :])
+    total = total + mm(other[:HALF], other_ref[:depth, :]) + mm(other[HALF:], other_ref[depth:, :])
+    out_ref[...] = total.astype(bf16)
 
 
 def per_device(query_field, key_field, value_field, short_taps, filt_in, filt_mid, filt_out,
                decay_rate, skip_gain, out_weight):
     chans = query_field.shape[1]
+    cores = 2
     groups = lax.axis_size("ch")
+    chips = groups // cores
+    dout = out_weight.shape[1]
     params = pltpu.CompilerParams(vmem_limit_bytes=32 * 1024 * 1024)
     far = pl.BlockSpec(memory_space=pltpu.HBM)
     operands = (query_field, key_field, value_field, filt_in, filt_mid, filt_out, short_taps,
@@ -294,29 +355,45 @@
         name="prep",
     )(*operands)
     fields = lax.all_to_all(parts, "ctx", 0, 0, tiled=True, axis_index_groups=[first_order()])
+    small, stack = pl.pallas_call(
+        weights_kernel,
+        out_shape=[jax.ShapeDtypeStruct((CH, 128), f32),
+                   jax.ShapeDtypeStruct((2 * UNITS + 2 * CH, 2 * BLK), bf16)],
+        compiler_params=params,
+        name="weights",
+    )(pack)
+    own_weight, small = lax.optimization_barrier((out_weight, small))
+    other_weight = lax.ppermute(own_weight, "ch", [(d, d ^ 1) for d in range(groups)])
     wide, table = pl.pallas_call(
         filter_kernel,
         out_shape=[jax.ShapeDtypeStruct((CH * NBLK + NBLK + CH, 2 * BLK), f32),
-                   jax.ShapeDtypeStruct((8 * BLK + 2 * BLK, 2 * BLK), bf16)],
+                   jax.ShapeDtypeStruct((4 * BLK + 2 * BLK, 2 * BLK), bf16)],
         scratch_shapes=[pltpu.VMEM((NBLK * CH, BLK), f32)],
         compiler_params=params,
-        cost_estimate=pl.CostEstimate(flops=2 * 10**9, bytes_accessed=5 * 10**6, transcendentals=10**6),
+        cost_estimate=pl.CostEstimate(flops=10**11, bytes_accessed=10**9, transcendentals=10**6),
         name="filter",
-    )(pack)
-    gated = pl.pallas_call(
+    )(small, stack)
+    gated, other_weight = pl.pallas_call(
         conv_kernel,
-        out_shape=jax.ShapeDtypeStruct((NBLK * CH, BLK), bf16),
-        scratch_shapes=[pltpu.VMEM((NBLK * CH, BLK), f32)] * 3,
+        out_shape=[jax.ShapeDtypeStruct((NBLK * CH, BLK), bf16),
+                   jax.ShapeDtypeStruct(out_weight.shape, bf16)],
+        in_specs=[pl.BlockSpec(memory_space=pltpu.VMEM)] * 3 + [far],
+        scratch_shapes=[pltpu.VMEM((NBLK * CH, BLK), f32)] * 3 + [pltpu.SemaphoreType.DMA],
         compiler_params=params,
-        cost_estimate=pl.CostEstimate(flops=10**11, bytes_accessed=10**9, transcendentals=0),
         name="convolve",
-    )(fields, wide, table)
-    returned = lax.all_to_all(gated.reshape(NBLK, CH, BLK), "ctx", 0, 0, tiled=True,
-                              axis_index_groups=[first_order()])
-    partial = lax.dot_general(returned.reshape(chans, BLK), out_weight, (((0,), (0,)), ((), ())),
-                              preferred_element_type=f32).astype(bf16)
-    shares = lax.all_to_all(partial.reshape(groups, BLK // groups, -1), "ch", 0, 0, tiled=True,
-                            axis_index_groups=None)
+    )(fields, wide, table, other_weight)
+    on_chip = [[c * groups + x * cores + k for k in range(cores) for c in second_order()] for x in range(chips)]
+    returned = lax.all_to_all(gated.reshape(NBLK * cores, CH // cores, BLK), ("ctx", "ch"), 0, 0,
+                              tiled=True, axis_index_groups=on_chip)
+    partial = pl.pallas_call(
+        project_kernel,
+        out_shape=jax.ShapeDtypeStruct((BLK // cores, dout), bf16),
+        compiler_params=params,
+        name="project",
+    )(returned.reshape(NBLK * CH, BLK), own_weight, other_weight)
+    along_x = [[x * cores + k for x in range(chips)] for k in range(cores)]
+    shares = lax.all_to_all(partial.reshape(chips, SHARE, dout), "ch", 0, 0, tiled=True,
+                            axis_index_groups=along_x)
     return jnp.sum(shares.astype(f32), 0).astype(bf16)
 
 

time: 70.8 us -> 68 us (0.960)
  blocking collectives: 34.7 us -> 30.6 us
  waiting for transfers between devices: 7.77 us -> 4.64 us
  starting transfers between devices: 17.1 us -> 20 us
  Pallas kernels: 8.68 us -> 10.1 us
    all_to_all x2, blocking collectives: 34.7 us -> 30.6 us  [the longest x1 21.2 us: per_device(): lax.all_to_all(gated.reshape(NBLK * cores, CH // cores, BLK), ('ctx', 'ch...]
    all_to_all x1, waiting for transfers between devices: 7.77 us -> 4.64 us  [per_device(): lax.all_to_all(parts, 'ctx', 0, 0, tiled=True, axis_index_groups=[first_o...]
    ppermute x0 -> x1, starting transfers between devices: none -> 2.86 us  [per_device(): lax.ppermute(own_weight, 'ch', [(d, d ^ 1) for d in range(groups)])]
    pallas_call x1 -> x3, Pallas kernels: 2 us -> 3.55 us  [the longest x1 2.27 us: per_device(): pl.pallas_call(conv_kernel, out_shape=[jax.ShapeDtypeStruct((NBLK * CH, B...]
  transfers between devices with their start and end apart: 1 -> 2, of which waited for: 1 -> 1; matrix products, arithmetic and copies ran while one was open for 0% -> 0% of each run, Pallas kernels for 6% -> 7%
where the time goes in v4:
time: 68 us; the launch traced here: 67.1 us
  blocking collectives  30.6 us (45%)
  starting transfers between devices  20 us (29%)
  Pallas kernels  10.1 us (15%)
  waiting for transfers between devices  4.64 us (7%)
  local copies, waits for them, and re-layouts  1.01 us (1%)
    all_to_all x1, blocking collectives, per_device(): lax.all_to_all(gated.reshape(NBLK * cores, CH // cores, BLK), ('ctx', 'ch...  21.2 us
    all_to_all x1, starting transfers between devices, per_device(): lax.all_to_all(parts, 'ctx', 0, 0, tiled=True, axis_index_groups=[first_o...  17.1 us
    all_to_all x1, blocking collectives, per_device(): lax.all_to_all(partial.reshape(chips, SHARE, dout), 'ch', 0, 0, tiled=Tru...  9.36 us
    all_to_all x1, waiting for transfers between devices, per_device(): lax.all_to_all(parts, 'ctx', 0, 0, tiled=True, axis_index_groups=[first_o...  4.64 us
    pallas_call x1, Pallas kernels, per_device(): pl.pallas_call(filter_kernel, out_shape=[jax.ShapeDtypeStruct((CH * NBLK...  4.35 us
    ppermute x1, starting transfers between devices, per_device(): lax.ppermute(own_weight, 'ch', [(d, d ^ 1) for d in range(groups)])  2.86 us
    pallas_call x1, Pallas kernels, per_device(): pl.pallas_call(conv_kernel, out_shape=[jax.ShapeDtypeStruct((NBLK * CH, B...  2.27 us
    pallas_call x1, Pallas kernels, per_device(): pl.pallas_call(prep_kernel, out_shape=[jax.ShapeDtypeStruct((NBLK, 3 * CH...  2.2 us
  transfers between devices with their start and end apart: 2, of which 1 were waited for; matrix products, arithmetic and copies ran while one was open for 0% of the time, Pallas kernels for 7%

profile of v4, /device:TPU:1, one launch (start us, length us, event | category | flops | bytes accessed | tf_op | source)
XLA Modules:
  0.0 67.1 jit_solution(3073046875697583415)
XLA Ops:
  0.0 2.2 %prep.1 = (bf16[64,24,128]{2,1,0:T(8,128)(2,1)}, f32[208,512]{1,0:T(8,128)}) custom-call(bf16[128,512]{1,0:T(8,128)(2,1)} %query_hbm.1, bf16[128,512]{1,0:T(8,128)(2,1)} %key_hbm.1, bf16[128,512]{1,0:T(8,128)(2,1)} %value_hbm.1, f32[33,64]{1,0:T(8,128)} %w_in_hbm.1, f32[64,64]{1,0:T(8,128)} %w_mid_hbm.1, f32[64,512]{1,0:T(8,128)} %w_out_hbm.1, ...), custom_call_target="tpu_custom_call" | custom-call | tf_op jit(solution)/shard_map/prep/pallas_call | solution.py:346
  2.2 17.1 %all-to-all-start = ((bf16[64,24,128]{2,1,0:T(8,128)(2,1)}), bf16[64,24,128]{2,1,0:T(8,128)(2,1)S(1)}, u32[]{:S(2)}, u32[]{:S(2)}) async-start(bf16[64,24,128]{2,1,0:T(8,128)(2,1)} %get-tuple-element.15), calls=%async_computation | async-start | bytes 786432 | tf_op jit(solution)/shard_map/all_to_all | solution.py:357
  19.4 0.0 copy-start.1
  19.4 1.0 %copy-done.1 = f32[208,512]{1,0:T(8,128)S(1)} copy-done((f32[208,512]{1,0:T(8,128)S(1)}, f32[208,512]{1,0:T(8,128)}, u32[]{:S(2)}) %copy-start.1) | copy-done | bytes 426008
  20.4 0.4 weights.1
  20.7 2.9 %collective-permute-start = (bf16[512,2048]{1,0:T(8,128)(2,1)}, bf16[512,2048]{1,0:T(8,128)(2,1)}, u32[]{:S(2)}, u32[]{:S(2)}) collective-permute-start(bf16[512,2048]{1,0:T(8,128)(2,1)} %own_ref), channel_id=1, source_target_pairs={{0,1},{1,0},{2,3},{3,2},{4,5},{5,4},{6,7},{7,6},{8,9},{9,8},{10,11... | collective-permute-start | bytes 6291464 | tf_op jit(solution)/shard_map/ppermute | solution.py:366
  23.6 4.3 %filter.1 = (f32[584,256]{1,0:T(8,128)S(1)}, bf16[768,256]{1,0:T(8,128)(2,1)S(1)}) custom-call(f32[8,128]{1,0:T(8,128)S(1)} %get-tuple-element.18.small_ref, bf16[144,256]{1,0:T(8,128)(2,1)S(1)} %get-tuple-element.19.stack_ref), custom_call_target="tpu_custom_call" | custom-call | flops 99999997952 | bytes 1000000000 | tf_op jit(solution)/shard_map/filter/pallas_call | solution.py:367
  28.0 0.0 copy-start
  28.0 4.6 %all-to-all-done.field_ref = bf16[64,24,128]{2,1,0:T(8,128)(2,1)S(1)} async-done(((bf16[64,24,128]{2,1,0:T(8,128)(2,1)}), bf16[64,24,128]{2,1,0:T(8,128)(2,1)S(1)}, u32[]{:S(2)}, u32[]{:S(2)}) %all-to-all-start) | async-done | bytes 393248 | tf_op jit(solution)/shard_map/all_to_all | solution.py:357
  32.6 0.0 collective-permute-done.other_hbm
  32.6 2.3 %convolve.1 = (bf16[512,128]{1,0:T(8,128)(2,1)S(1)}, bf16[512,2048]{1,0:T(8,128)(2,1)S(1)}) custom-call(bf16[64,24,128]{2,1,0:T(8,128)(2,1)S(1)} %all-to-all-done.field_ref, f32[584,256]{1,0:T(8,128)S(1)} %get-tuple-element.20.wide_ref, bf16[768,256]{1,0:T(8,128)(2,1)S(1)} %get-tuple-element.21.table_ref, bf16[512,2048]{1,0:T(8,128)(2,1)} %collective-permute-done.other_hbm), custom_call_target="tpu_custom_call" | custom-call | tf_op jit(solution)/shard_map/convolve/pallas_call | solution.py:376
  34.9 21.2 %all_to_all.15 = bf16[128,4,128]{2,1,0:T(4,128)(2,1)S(1)} all-to-all(bf16[128,4,128]{2,1,0:T(4,128)(2,1)S(1)} %bitcast.7), channel_id=1, replica_groups={{0,32,16,48,8,40,24,56,256,288,272,304,264,296,280,312,128,160,144,176,..., dimensions={0} | all-to-all | bytes 262144 | tf_op jit(solution)/shard_map/all_to_all | solution.py:386
  56.1 0.0 copy-done
  56.2 0.9 %project.1 = bf16[64,2048]{1,0:T(8,128)(2,1)S(1)} custom-call(bf16[512,128]{1,0:T(8,128)(2,1)S(1)} %bitcast.6, bf16[512,2048]{1,0:T(8,128)(2,1)S(1)} %copy-done, bf16[512,2048]{1,0:T(8,128)(2,1)S(1)} %get-tuple-element.24.other_ref), custom_call_target="tpu_custom_call" | custom-call | tf_op jit(solution)/shard_map/project/pallas_call | solution.py:388
  57.1 9.4 %all_to_all.16 = bf16[4,16,2048]{2,1,0:T(8,128)(2,1)S(1)} all-to-all(bf16[4,16,2048]{2,1,0:T(8,128)(2,1)S(1)} %bitcast.5), channel_id=1, replica_groups={{0,2,4,6},{1,3,5,7},{8,10,12,14},{9,11,13,15},{16,18,20,22},{17,19,21,2..., dimensions={0} | all-to-all | bytes 524288 | tf_op jit(solution)/shard_map/all_to_all | solution.py:395
  66.4 0.7 reduce_sum.12
Async XLA Ops:
  2.2 30.4 %all-to-all-start = ((bf16[64,24,128]{2,1,0:T(8,128)(2,1)}), bf16[64,24,128]{2,1,0:T(8,128)(2,1)S(1)}, u32[]{:S(2)}, u32[]{:S(2)}) async-start(bf16[64,24,128]{2,1,0:T(8,128)(2,1)} %get-tuple-element.15), calls=%async_computation | async-start | bytes 786432 | tf_op jit(solution)/shard_map/all_to_all | solution.py:357
  19.4 1.0 %copy-start.1 = (f32[208,512]{1,0:T(8,128)S(1)}, f32[208,512]{1,0:T(8,128)}, u32[]{:S(2)}) copy-start(f32[208,512]{1,0:T(8,128)} %get-tuple-element.16.pack_ref) | copy-start | bytes 1277956
  20.7 11.9 %collective-permute-start = (bf16[512,2048]{1,0:T(8,128)(2,1)}, bf16[512,2048]{1,0:T(8,128)(2,1)}, u32[]{:S(2)}, u32[]{:S(2)}) collective-permute-start(bf16[512,2048]{1,0:T(8,128)(2,1)} %own_ref), channel_id=1, source_target_pairs={{0,1},{1,0},{2,3},{3,2},{4,5},{5,4},{6,7},{7,6},{8,9},{9,8},{10,11... | collective-permute-start | bytes 6291464 | tf_op jit(solution)/shard_map/ppermute | solution.py:366
  28.0 28.2 %copy-start = (bf16[512,2048]{1,0:T(8,128)(2,1)S(1)}, bf16[512,2048]{1,0:T(8,128)(2,1)}, u32[]{:S(2)}) copy-start(bf16[512,2048]{1,0:T(8,128)(2,1)} %own_ref) | copy-start | bytes 6291460

commit v5 on v4

--- a/solution.py
+++ b/solution.py
@@ -22,8 +22,8 @@
 CHUNK = 2048
 STEP = 27
 BACK = 19
-PACK = (0, 64, 88, 96, 104, 168)
-PACK_ROWS = 208
+PACK = (0, 64, 88, 96, 104, 112)
+PACK_ROWS = 120
 bf16 = jnp.bfloat16
 f32 = jnp.float32
 highest = lax.Precision.HIGHEST
@@ -77,8 +77,8 @@
 
 
 def mm_split(value, top_mat, low_mat):
-    top, low = split(value)
-    return mm(top, top_mat) + mm(low, top_mat) + mm(top, low_mat)
+    top = value.astype(bf16)
+    return mm(top, top_mat) + mm(top, low_mat)
 
 
 def lift(rows, low_half):
@@ -116,8 +116,11 @@
         pack_ref[at_taps + f * 8:at_taps + f * 8 + TAPS, :] = taps_ref[f]
     pack_ref[at_rate:at_rate + 8, :] = jnp.broadcast_to(rate_ref[...], (8, chans))
     pack_ref[at_skip:at_skip + 8, :] = jnp.broadcast_to(skip_ref[...], (8, chans))
-    pack_ref[at_mid:at_mid + UNITS, 0:UNITS] = w_mid_ref[...]
-    pack_ref[at_in:at_in + FEAT, 0:UNITS] = w_in_ref[...]
+    for n in range(8):
+        pack_ref[at_mid:at_mid + 8, n * UNITS:(n + 1) * UNITS] = w_mid_ref[n * 8:(n + 1) * 8, :]
+    for n in range(4):
+        pack_ref[at_in:at_in + 8, n * UNITS:(n + 1) * UNITS] = w_in_ref[n * 8:(n + 1) * 8, :]
+    pack_ref[at_in:at_in + 1, 4 * UNITS:5 * UNITS] = w_in_ref[FEAT - 1:FEAT, :]
 
 
 def forward(rows_ref, first_ref, tw_ref, mats_ref):
@@ -185,11 +188,13 @@
     mine = lax.dot_general(pick, pack_ref[:at_mid, :], (((1,), (1,)), ((), ())), precision=highest,
                            preferred_element_type=f32)
     per_turn = 1.0 / (2.0 * math.pi)
-    padded = jnp.concatenate([pack_ref[at_in + 1:at_in + FEAT, 0:UNITS], pack_ref[at_in:at_in + 1, 0:UNITS],
-                              jnp.zeros((FEAT_PAD - FEAT, UNITS), f32)], 0)
+    w_in = jnp.concatenate([pack_ref[at_in:at_in + 8, n * UNITS:(n + 1) * UNITS] for n in range(4)]
+                           + [pack_ref[at_in:at_in + 1, 4 * UNITS:5 * UNITS]], 0)
+    padded = jnp.concatenate([w_in[1:FEAT], w_in[0:1], jnp.zeros((FEAT_PAD - FEAT, UNITS), f32)], 0)
+    w_mid = jnp.concatenate([pack_ref[at_mid:at_mid + 8, n * UNITS:(n + 1) * UNITS] for n in range(8)], 0)
     small_ref[:, 0:at_mid] = mine
     stack_ref[0:UNITS, 0:3 * FEAT_PAD] = stack(padded.T * per_turn)
-    stack_ref[UNITS:2 * UNITS, 0:3 * UNITS] = stack(pack_ref[at_mid:at_mid + UNITS, 0:UNITS].T * per_turn)
+    stack_ref[UNITS:2 * UNITS, 0:3 * UNITS] = stack(w_mid.T * per_turn)
     wide = stack(mine[:, at_out:at_out + UNITS])
     stack_ref[2 * UNITS:2 * UNITS + 2 * CH, 0:3 * UNITS] = jnp.concatenate([wide, wide], 0)
 
@@ -295,7 +300,8 @@
     same = sub == (lax.broadcasted_iota(jnp.int32, (CH, BLK), 1) < HALF)
     order = second_order()
     lane = lax.broadcasted_iota(jnp.int32, (BLK, BLK), 1)
-    token = lane // HALF * SHARE + lane % HALF // SHARE * (2 * SHARE) + lane % SHARE
+    slot = lane % HALF // SHARE
+    token = lane // HALF * SHARE + (slot ^ slot // 2) * (2 * SHARE) + lane % SHARE
     reorder = (lax.broadcasted_iota(jnp.int32, (BLK, BLK), 0) == token).astype(f32).astype(bf16)
 
     for slot in range(0, NBLK, 8):
@@ -391,7 +397,7 @@
         compiler_params=params,
         name="project",
     )(returned.reshape(NBLK * CH, BLK), own_weight, other_weight)
-    along_x = [[x * cores + k for x in range(chips)] for k in range(cores)]
+    along_x = [[(x ^ x // 2) * cores + k for x in range(chips)] for k in range(cores)]
     shares = lax.all_to_all(partial.reshape(chips, SHARE, dout), "ch", 0, 0, tiled=True,
                             axis_index_groups=along_x)
     return jnp.sum(shares.astype(f32), 0).astype(bf16)

time: 68 us -> 67.4 us (level)
  no operation moved by 1% of the time
where the time goes in v5:
time: 67.4 us; the launch traced here: 66.5 us
  blocking collectives  30.3 us (45%)
  starting transfers between devices  20 us (30%)
  Pallas kernels  9.72 us (14%)
  waiting for transfers between devices  4.75 us (7%)
  local copies, waits for them, and re-layouts  0.94 us (1%)
    all_to_all x1, blocking collectives, per_device(): lax.all_to_all(gated.reshape(NBLK * cores, CH // cores, BLK), ('ctx', 'ch...  21.2 us
    all_to_all x1, starting transfers between devices, per_device(): lax.all_to_all(parts, 'ctx', 0, 0, tiled=True, axis_index_groups=[first_o...  17.1 us
    all_to_all x1, blocking collectives, per_device(): lax.all_to_all(partial.reshape(chips, SHARE, dout), 'ch', 0, 0, tiled=Tru...  9.05 us
    all_to_all x1, waiting for transfers between devices, per_device(): lax.all_to_all(parts, 'ctx', 0, 0, tiled=True, axis_index_groups=[first_o...  4.75 us
    pallas_call x1, Pallas kernels, per_device(): pl.pallas_call(filter_kernel, out_shape=[jax.ShapeDtypeStruct((CH * NBLK...  4.29 us
    ppermute x1, starting transfers between devices, per_device(): lax.ppermute(own_weight, 'ch', [(d, d ^ 1) for d in range(groups)])  2.86 us
    pallas_call x1, Pallas kernels, per_device(): pl.pallas_call(prep_kernel, out_shape=[jax.ShapeDtypeStruct((NBLK, 3 * CH...  2.16 us
    pallas_call x1, Pallas kernels, per_device(): pl.pallas_call(conv_kernel, out_shape=[jax.ShapeDtypeStruct((NBLK * CH, B...  1.98 us
  transfers between devices with their start and end apart: 2, of which 1 were waited for; matrix products, arithmetic and copies ran while one was open for 0% of the time, Pallas kernels for 7%

profile of v5, /device:TPU:1, one launch (start us, length us, event | category | flops | bytes accessed | tf_op | source)
XLA Modules:
  0.0 66.5 jit_solution(6510022437527373740)
XLA Ops:
  0.0 2.2 %prep.1 = (bf16[64,24,128]{2,1,0:T(8,128)(2,1)}, f32[120,512]{1,0:T(8,128)}) custom-call(bf16[128,512]{1,0:T(8,128)(2,1)} %query_hbm.1, bf16[128,512]{1,0:T(8,128)(2,1)} %key_hbm.1, bf16[128,512]{1,0:T(8,128)(2,1)} %value_hbm.1, f32[33,64]{1,0:T(8,128)} %w_in_hbm.1, f32[64,64]{1,0:T(8,128)} %w_mid_hbm.1, f32[64,512]{1,0:T(8,128)} %w_out_hbm.1, ...), custom_call_target="tpu_custom_call" | custom-call | tf_op jit(solution)/shard_map/prep/pallas_call | solution.py:352
  2.2 17.1 %all-to-all-start = ((bf16[64,24,128]{2,1,0:T(8,128)(2,1)}), bf16[64,24,128]{2,1,0:T(8,128)(2,1)S(1)}, u32[]{:S(2)}, u32[]{:S(2)}) async-start(bf16[64,24,128]{2,1,0:T(8,128)(2,1)} %get-tuple-element.15), calls=%async_computation | async-start | bytes 786432 | tf_op jit(solution)/shard_map/all_to_all | solution.py:363
  19.3 0.0 copy-start.1
  19.3 0.9 %copy-done.1 = f32[120,512]{1,0:T(8,128)S(1)} copy-done((f32[120,512]{1,0:T(8,128)S(1)}, f32[120,512]{1,0:T(8,128)}, u32[]{:S(2)}) %copy-start.1) | copy-done | bytes 245784
  20.3 0.4 weights.1
  20.7 2.9 %collective-permute-start = (bf16[512,2048]{1,0:T(8,128)(2,1)}, bf16[512,2048]{1,0:T(8,128)(2,1)}, u32[]{:S(2)}, u32[]{:S(2)}) collective-permute-start(bf16[512,2048]{1,0:T(8,128)(2,1)} %own_ref), channel_id=1, source_target_pairs={{0,1},{1,0},{2,3},{3,2},{4,5},{5,4},{6,7},{7,6},{8,9},{9,8},{10,11... | collective-permute-start | bytes 6291464 | tf_op jit(solution)/shard_map/ppermute | solution.py:372
  23.5 4.3 %filter.1 = (f32[584,256]{1,0:T(8,128)S(1)}, bf16[768,256]{1,0:T(8,128)(2,1)S(1)}) custom-call(f32[8,128]{1,0:T(8,128)S(1)} %get-tuple-element.18.small_ref, bf16[144,256]{1,0:T(8,128)(2,1)S(1)} %get-tuple-element.19.stack_ref), custom_call_target="tpu_custom_call" | custom-call | flops 99999997952 | bytes 1000000000 | tf_op jit(solution)/shard_map/filter/pallas_call | solution.py:373
  27.8 0.0 copy-start
  27.8 4.7 %all-to-all-done.field_ref = bf16[64,24,128]{2,1,0:T(8,128)(2,1)S(1)} async-done(((bf16[64,24,128]{2,1,0:T(8,128)(2,1)}), bf16[64,24,128]{2,1,0:T(8,128)(2,1)S(1)}, u32[]{:S(2)}, u32[]{:S(2)}) %all-to-all-start) | async-done | bytes 393248 | tf_op jit(solution)/shard_map/all_to_all | solution.py:363
  32.6 0.0 collective-permute-done.other_hbm
  32.6 2.0 %convolve.1 = (bf16[512,128]{1,0:T(8,128)(2,1)S(1)}, bf16[512,2048]{1,0:T(8,128)(2,1)S(1)}) custom-call(bf16[64,24,128]{2,1,0:T(8,128)(2,1)S(1)} %all-to-all-done.field_ref, f32[584,256]{1,0:T(8,128)S(1)} %get-tuple-element.20.wide_ref, bf16[768,256]{1,0:T(8,128)(2,1)S(1)} %get-tuple-element.21.table_ref, bf16[512,2048]{1,0:T(8,128)(2,1)} %collective-permute-done.other_hbm), custom_call_target="tpu_custom_call" | custom-call | tf_op jit(solution)/shard_map/convolve/pallas_call | solution.py:382
  34.6 21.2 %all_to_all.15 = bf16[128,4,128]{2,1,0:T(4,128)(2,1)S(1)} all-to-all(bf16[128,4,128]{2,1,0:T(4,128)(2,1)S(1)} %bitcast.7), channel_id=1, replica_groups={{0,32,16,48,8,40,24,56,256,288,272,304,264,296,280,312,128,160,144,176,..., dimensions={0} | all-to-all | bytes 262144 | tf_op jit(solution)/shard_map/all_to_all | solution.py:392
  55.8 0.0 copy-done
  55.8 0.9 %project.1 = bf16[64,2048]{1,0:T(8,128)(2,1)S(1)} custom-call(bf16[512,128]{1,0:T(8,128)(2,1)S(1)} %bitcast.6, bf16[512,2048]{1,0:T(8,128)(2,1)S(1)} %copy-done, bf16[512,2048]{1,0:T(8,128)(2,1)S(1)} %get-tuple-element.24.other_ref), custom_call_target="tpu_custom_call" | custom-call | tf_op jit(solution)/shard_map/project/pallas_call | solution.py:394
  56.7 9.1 %all_to_all.16 = bf16[4,16,2048]{2,1,0:T(8,128)(2,1)S(1)} all-to-all(bf16[4,16,2048]{2,1,0:T(8,128)(2,1)S(1)} %bitcast.5), channel_id=1, replica_groups={{0,2,6,4},{1,3,7,5},{8,10,14,12},{9,11,15,13},{16,18,22,20},{17,19,23,2..., dimensions={0} | all-to-all | bytes 524288 | tf_op jit(solution)/shard_map/all_to_all | solution.py:401
  65.8 0.7 %reduce_sum.12 = bf16[16,2048]{1,0:T(8,128)(2,1)} reduce(bf16[4,16,2048]{2,1,0:T(8,128)(2,1)S(1)} %all_to_all.16, bf16[]{:T(256)} %constant.2.clone.1), dimensions={0}, to_apply=%region_0.0 | reduce | flops 98304 | bytes 327682 | tf_op jit(solution)/shard_map/reduce_sum | solution.py:403
Async XLA Ops:
  2.2 30.4 %all-to-all-start = ((bf16[64,24,128]{2,1,0:T(8,128)(2,1)}), bf16[64,24,128]{2,1,0:T(8,128)(2,1)S(1)}, u32[]{:S(2)}, u32[]{:S(2)}) async-start(bf16[64,24,128]{2,1,0:T(8,128)(2,1)} %get-tuple-element.15), calls=%async_computation | async-start | bytes 786432 | tf_op jit(solution)/shard_map/all_to_all | solution.py:363
  19.3 0.9 %copy-start.1 = (f32[120,512]{1,0:T(8,128)S(1)}, f32[120,512]{1,0:T(8,128)}, u32[]{:S(2)}) copy-start(f32[120,512]{1,0:T(8,128)} %get-tuple-element.16.pack_ref) | copy-start | bytes 737284
  20.7 11.9 %collective-permute-start = (bf16[512,2048]{1,0:T(8,128)(2,1)}, bf16[512,2048]{1,0:T(8,128)(2,1)}, u32[]{:S(2)}, u32[]{:S(2)}) collective-permute-start(bf16[512,2048]{1,0:T(8,128)(2,1)} %own_ref), channel_id=1, source_target_pairs={{0,1},{1,0},{2,3},{3,2},{4,5},{5,4},{6,7},{7,6},{8,9},{9,8},{10,11... | collective-permute-start | bytes 6291464 | tf_op jit(solution)/shard_map/ppermute | solution.py:372
  27.8 28.0 %copy-start = (bf16[512,2048]{1,0:T(8,128)(2,1)S(1)}, bf16[512,2048]{1,0:T(8,128)(2,1)}, u32[]{:S(2)}) copy-start(bf16[512,2048]{1,0:T(8,128)(2,1)} %own_ref) | copy-start | bytes 6291460

commit v6 on v5

--- a/solution.py
+++ b/solution.py
@@ -18,19 +18,15 @@
 HALF = 64
 SHARE = 16
 TAPS = 7
+EDGE = TAPS - 1
+PIECE = 20
 UNITS = 64
 CHUNK = 2048
-STEP = 27
-BACK = 19
 PACK = (0, 64, 88, 96, 104, 112)
 PACK_ROWS = 120
 bf16 = jnp.bfloat16
 f32 = jnp.float32
 highest = lax.Precision.HIGHEST
-
-
-def first_order():
-    return [STEP * n % NBLK for n in range(NBLK)]
 
 
 def second_order():
@@ -81,33 +77,53 @@
     return mm(top, top_mat) + mm(top, low_mat)
 
 
-def lift(rows, low_half):
-    return jnp.where(low_half, rows[0], pltpu.roll(rows[1], 4, 1))
-
-
-def drop(rows, low_half):
-    return jnp.where(low_half, pltpu.roll(rows[0], 4, 1), rows[1])
-
-
 def prep_kernel(query_hbm, key_hbm, value_hbm, w_in_hbm, w_mid_hbm, w_out_hbm, taps_hbm, rate_hbm,
                 skip_hbm, out_ref, pack_ref, held, w_in_ref, w_mid_ref, w_out_ref, taps_ref, rate_ref,
-                skip_ref, sems):
-    sources = (query_hbm, key_hbm, value_hbm, w_out_hbm, taps_hbm, w_mid_hbm, w_in_hbm, rate_hbm, skip_hbm)
-    targets = (held.at[0], held.at[1], held.at[2], w_out_ref, taps_ref, w_mid_ref, w_in_ref, rate_ref, skip_ref)
+                skip_ref, lead_ref, edge_ref, sems):
+    sources = (taps_hbm, key_hbm, value_hbm, query_hbm, w_out_hbm, w_mid_hbm, w_in_hbm, rate_hbm, skip_hbm)
+    targets = (taps_ref, held.at[1], held.at[2], held.at[0], w_out_ref, w_mid_ref, w_in_ref, rate_ref, skip_ref)
     copies = [pltpu.make_async_copy(src, dst, sems.at[n])
               for n, (src, dst) in enumerate(zip(sources, targets))]
     for copy in copies:
         copy.start()
     low_half = lax.broadcasted_iota(jnp.int32, (NBLK // 2, CH, BLK), 1) < 4
-    sets = []
-    for f in range(3):
+    half = edge_ref.shape[1]
+    edge_ref[...] = jnp.zeros_like(edge_ref)
+    copies[0].wait()
+    mixed = []
+    blocks = range(2 * half // BLK)
+    for f in (1, 2):
         copies[f].wait()
-        turned = held[f].astype(f32).T.reshape(2, NBLK // 2, CH, BLK)
-        sets.append((lift(turned, low_half), drop(turned, low_half)))
-    for slot, ctx in enumerate(first_order()):
-        place = second_place(ctx)
-        out_ref[slot] = jnp.concatenate([pair[place % 2][place // 2] for pair in sets], 0).astype(bf16)
-    for copy in copies[3:]:
+        parts = []
+        for n in blocks:
+            lead = lead_ref.at[(f - 1) * len(blocks) + n]
+            lanes = slice(n * BLK, (n + 1) * BLK)
+            lead[0:8, :] = jnp.zeros((8, BLK), f32)
+            lead[8:8 + BLK, :] = held[f, :, lanes].astype(f32)
+            total = taps_ref[f, 0:1, lanes] * lead[8:8 + BLK, :]
+            for j in range(1, TAPS):
+                total = total + taps_ref[f, j:j + 1, lanes] * lead[8 - j:8 - j + BLK, :]
+            parts.append(total.astype(bf16).astype(f32))
+            at = n * BLK // half * HALF + (f - 1) * (HALF // 2)
+            lanes = slice(n * BLK % half, n * BLK % half + BLK)
+            edge_ref[at:at + EDGE, lanes] = lead[8 + BLK - EDGE:8 + BLK, :]
+            edge_ref[at + EDGE:at + 2 * EDGE, lanes] = lead[8:8 + EDGE, :]
+        mixed.append(jnp.concatenate(parts, 1))
+
+    def pairs(field):
+        rows = field.T.reshape(2, NBLK // 2, CH, BLK)
+        up = pltpu.roll(rows[1], 4, 1)
+        return jnp.where(low_half, rows[0], up), jnp.where(low_half, up, rows[0])
+
+    prod_even, prod_odd = pairs(mixed[0] * mixed[1])
+    copies[3].wait()
+    query_even, query_odd = pairs(held[0].astype(f32))
+    edges = edge_ref[...].T.reshape(NBLK // 2, CH, BLK)
+    rows = jnp.concatenate([prod_even, query_even, jnp.where(low_half, edges, prod_odd),
+                            jnp.where(low_half, prod_odd, query_odd),
+                            jnp.where(low_half, query_odd, edges)], 1)
+    out_ref[...] = rows.reshape(NBLK * PIECE, BLK).astype(bf16)
+    for copy in copies[4:]:
         copy.wait()
     chans = rate_ref.shape[1]
     at_out, at_taps, at_rate, at_skip, at_mid, at_in = PACK
@@ -251,12 +267,51 @@
     spec_ref[:, BLK:] = spec[:, BLK:]
 
 
-def conv_kernel(field_ref, wide_ref, table_ref, other_hbm, out_ref, other_ref, query_ref, prod_ref, conv_ref, sem):
+def conv_kernel(field_ref, wide_ref, table_ref, other_hbm, out_ref, other_ref, query_ref, prod_ref,
+                conv_ref, raw_ref, edge_ref, sem):
     swap = pltpu.make_async_copy(other_hbm, other_ref, sem)
     swap.start()
     spec_ref, tw_ref, par_ref, mats_ref, first_ref, last_ref = views(wide_ref, table_ref)
     par = par_ref[...]
-    taps = [jnp.broadcast_to(par[:, n:n + 1], (CH, BLK))[None] for n in range(3 * TAPS)]
+    order = second_order()
+    sub = lax.broadcasted_iota(jnp.int32, (CH, BLK), 0) < 4
+    at_lane = lax.broadcasted_iota(jnp.int32, (CH, BLK), 1)
+    raw_ref[0:CH, :] = jnp.zeros((CH, BLK), f32)
+    edge_ref[0:CH, :] = jnp.zeros((CH, BLK), f32)
+    for quad in range(0, NBLK, 4):
+        rows = field_ref[quad * PIECE:(quad + 4) * PIECE, :].astype(f32)
+        for pair in range(2):
+            five = [rows[pair * 2 * PIECE + n * CH:pair * 2 * PIECE + (n + 1) * CH] for n in range(5)]
+            even, odd = order[quad + pair * 2], order[quad + pair * 2 + 1]
+            prod_ref[even * CH:(even + 1) * CH, :] = five[0]
+            prod_ref[odd * CH:(odd + 1) * CH, :] = pltpu.roll(jnp.where(sub, five[3], five[2]), 4, 0)
+            raw_ref[(even + 1) * CH:(even + 2) * CH, :] = five[1]
+            raw_ref[(odd + 1) * CH:(odd + 2) * CH, :] = pltpu.roll(jnp.where(sub, five[4], five[3]), 4, 0)
+            edge_ref[4 + even * 4:8 + even * 4, :] = five[2][0:4]
+            edge_ref[4 + odd * 4:8 + odd * 4, :] = five[4][4:8]
+
+    both_taps = []
+    for j in range(TAPS):
+        mine = jnp.where(at_lane % HALF < HALF // 2, par[:, TAPS + j:TAPS + j + 1],
+                         par[:, 2 * TAPS + j:2 * TAPS + j + 1])
+        both_taps.append(jnp.where(sub == (at_lane < HALF), mine, pltpu.roll(mine, 4, 0))[None])
+    shape = (NBLK // 2, CH, BLK)
+    from_past = lax.broadcasted_iota(jnp.int32, shape, 2) % (HALF // 2) < EDGE
+    now = jnp.where(from_past, edge_ref[0:4 * NBLK, :].reshape(shape), edge_ref[4:4 + 4 * NBLK, :].reshape(shape))
+    past = pltpu.roll(now, 1, 2)
+    total = pltpu.roll(both_taps[6] * now, 2, 2) + (both_taps[4] * now + both_taps[5] * past)
+    total = pltpu.roll(total, 2, 2) + (both_taps[2] * now + both_taps[3] * past)
+    total = pltpu.roll(total, 2, 2) + (both_taps[0] * now + both_taps[1] * past)
+    total = total.astype(bf16).astype(f32)
+    total = total * pltpu.roll(total, BLK - HALF // 2, 2)
+    left, right = pltpu.roll(total, BLK - EDGE, 2), pltpu.roll(total, BLK - HALF - EDGE, 2)
+    subs = lax.broadcasted_iota(jnp.int32, shape, 1) < 4
+    fixed = jnp.stack([jnp.where(subs, left, pltpu.roll(right, 4, 1)),
+                       jnp.where(subs, pltpu.roll(left, 4, 1), right)], 1).reshape(NBLK * CH, BLK)
+    head = lax.broadcasted_iota(jnp.int32, (NBLK * CH, BLK), 1) < EDGE
+    prod_ref[...] = jnp.where(head, fixed, prod_ref[...])
+
+    taps = [jnp.broadcast_to(par[:, n:n + 1], (CH, BLK))[None] for n in range(TAPS)]
     span = 8
     lane = lax.broadcasted_iota(jnp.int32, (span + 1, CH, BLK), 2)
 
@@ -265,22 +320,13 @@
         return jnp.where(lane < steps, jnp.concatenate([turned[:1], turned[:-1]], 0), turned)
 
     for start in range(0, NBLK, span):
-        block = [field_ref[BACK * n % NBLK].astype(f32) for n in range(max(start - 1, 0), start + span)]
-        if start == 0:
-            block = [jnp.zeros_like(block[0])] + block
-        block = jnp.stack(block, 0)
-        mixed = []
-        for f in range(3):
-            now = block[:, f * CH:(f + 1) * CH, :]
-            past = later(now, 1)
-            t = taps[f * TAPS:(f + 1) * TAPS]
-            total = later(t[6] * now, 2) + (t[4] * now + t[5] * past)
-            total = later(total, 2) + (t[2] * now + t[3] * past)
-            total = later(total, 2) + (t[0] * now + t[1] * past)
-            mixed.append(total[1:].astype(bf16).reshape(span * CH, BLK))
-        at = slice(start * CH, (start + span) * CH)
-        prod_ref[at, :] = mixed[1].astype(f32) * mixed[2].astype(f32)
-        query_ref[at, :] = mixed[0].astype(f32)
+        now = raw_ref[start * CH:(start + span + 1) * CH, :].reshape(span + 1, CH, BLK)
+        past = later(now, 1)
+        total = later(taps[6] * now, 2) + (taps[4] * now + taps[5] * past)
+        total = later(total, 2) + (taps[2] * now + taps[3] * past)
+        total = later(total, 2) + (taps[0] * now + taps[1] * past)
+        total = total[1:].astype(bf16).astype(f32)
+        query_ref[start * CH:(start + span) * CH, :] = total.reshape(span * CH, BLK)
     spec = forward(prod_ref, first_ref, tw_ref, mats_ref)
     s_re, s_im = spec[:, :BLK], spec[:, BLK:]
     h_re, h_im = spec_ref[:, :BLK], spec_ref[:, BLK:]
@@ -296,9 +342,7 @@
     conv = mm(last, jnp.concatenate([top, low, top], 0))
     for c in range(CH):
         conv_ref[pl.ds(c, NBLK, stride=CH), :] = conv[:, c * BLK:(c + 1) * BLK]
-    sub = lax.broadcasted_iota(jnp.int32, (CH, BLK), 0) < 4
-    same = sub == (lax.broadcasted_iota(jnp.int32, (CH, BLK), 1) < HALF)
-    order = second_order()
+    same = sub == (at_lane < HALF)
     lane = lax.broadcasted_iota(jnp.int32, (BLK, BLK), 1)
     slot = lane % HALF // SHARE
     token = lane // HALF * SHARE + (slot ^ slot // 2) * (2 * SHARE) + lane % SHARE
@@ -351,16 +395,18 @@
                 decay_rate.reshape(1, chans), skip_gain.reshape(1, chans))
     parts, pack = pl.pallas_call(
         prep_kernel,
-        out_shape=[jax.ShapeDtypeStruct((NBLK, 3 * CH, BLK), bf16),
+        out_shape=[jax.ShapeDtypeStruct((NBLK * PIECE, BLK), bf16),
                    jax.ShapeDtypeStruct((PACK_ROWS, chans), f32)],
         in_specs=[far] * len(operands),
         scratch_shapes=[pltpu.VMEM((3,) + query_field.shape, bf16)]
         + [pltpu.VMEM(t.shape, t.dtype) for t in operands[3:]]
-        + [pltpu.SemaphoreType.DMA((len(operands),))],
+        + [pltpu.VMEM((2 * chans // BLK, 8 + BLK, BLK), f32), pltpu.VMEM((BLK, chans // 2), f32),
+           pltpu.SemaphoreType.DMA((len(operands),))],
         compiler_params=pltpu.CompilerParams(vmem_limit_bytes=62 * 1024 * 1024),
         name="prep",
     )(*operands)
-    fields = lax.all_to_all(parts, "ctx", 0, 0, tiled=True, axis_index_groups=[first_order()])
+    fields = lax.all_to_all(parts.reshape(NBLK, PIECE // 4, 4, BLK), "ctx", 0, 0, tiled=True,
+                            axis_index_groups=[second_order()]).reshape(NBLK * PIECE, BLK)
     small, stack = pl.pallas_call(
         weights_kernel,
         out_shape=[jax.ShapeDtypeStruct((CH, 128), f32),
@@ -384,7 +430,9 @@
         out_shape=[jax.ShapeDtypeStruct((NBLK * CH, BLK), bf16),
                    jax.ShapeDtypeStruct(out_weight.shape, bf16)],
         in_specs=[pl.BlockSpec(memory_space=pltpu.VMEM)] * 3 + [far],
-        scratch_shapes=[pltpu.VMEM((NBLK * CH, BLK), f32)] * 3 + [pltpu.SemaphoreType.DMA],
+        scratch_shapes=[pltpu.VMEM((NBLK * CH, BLK), f32)] * 3
+        + [pltpu.VMEM(((NBLK + 1) * CH, BLK), f32), pltpu.VMEM((4 * NBLK + CH, BLK), f32),
+           pltpu.SemaphoreType.DMA],
         compiler_params=params,
         name="convolve",
     )(fields, wide, table, other_weight)

time: 67.4 us -> 66.5 us (0.987)
  blocking collectives: 30.3 us -> 28.8 us
    all_to_all x1, blocking collectives: 21.2 us -> 19.7 us  [per_device(): lax.all_to_all(gated.reshape(NBLK * cores, CH // cores, BLK), ('ctx', 'ch...]
where the time goes in v6:
time: 66.5 us; the launch traced here: 65.5 us
  blocking collectives  28.8 us (43%)
  starting transfers between devices  20 us (30%)
  Pallas kernels  9.78 us (15%)
  waiting for transfers between devices  5.3 us (8%)
  local copies, waits for them, and re-layouts  0.94 us (1%)
  other arithmetic  0.67 us (1%)
    all_to_all x1, blocking collectives, per_device(): lax.all_to_all(gated.reshape(NBLK * cores, CH // cores, BLK), ('ctx', 'ch...  19.7 us
    all_to_all x1, starting transfers between devices, per_device(): lax.all_to_all(parts.reshape(NBLK, PIECE // 4, 4, BLK), 'ctx', 0, 0, tile...  17.1 us
    all_to_all x1, blocking collectives, per_device(): lax.all_to_all(partial.reshape(chips, SHARE, dout), 'ch', 0, 0, tiled=Tru...  9.05 us
    all_to_all x1, waiting for transfers between devices, per_device(): lax.all_to_all(parts.reshape(NBLK, PIECE // 4, 4, BLK), 'ctx', 0, 0, tile...  5.29 us
    pallas_call x1, Pallas kernels, per_device(): pl.pallas_call(filter_kernel, out_shape=[jax.ShapeDtypeStruct((CH * NBLK...  4.29 us
    ppermute x1, starting transfers between devices, per_device(): lax.ppermute(own_weight, 'ch', [(d, d ^ 1) for d in range(groups)])  2.86 us
    pallas_call x1, Pallas kernels, per_device(): pl.pallas_call(prep_kernel, out_shape=[jax.ShapeDtypeStruct((NBLK * PIECE...  2.38 us
    pallas_call x1, Pallas kernels, per_device(): pl.pallas_call(conv_kernel, out_shape=[jax.ShapeDtypeStruct((NBLK * CH, B...  1.82 us
  transfers between devices with their start and end apart: 2, of which 1 were waited for; matrix products, arithmetic and copies ran while one was open for 0% of the time, Pallas kernels for 7%

profile of v6, /device:TPU:1, one launch (start us, length us, event | category | flops | bytes accessed | tf_op | source)
XLA Modules:
  0.0 65.5 jit_solution(15281706782107461342)
XLA Ops:
  0.0 2.4 %prep.1 = (bf16[1280,128]{1,0:T(8,128)(2,1)}, f32[120,512]{1,0:T(8,128)}) custom-call(bf16[128,512]{1,0:T(8,128)(2,1)} %query_hbm.1, bf16[128,512]{1,0:T(8,128)(2,1)} %key_hbm.1, bf16[128,512]{1,0:T(8,128)(2,1)} %value_hbm.1, f32[33,64]{1,0:T(8,128)} %w_in_hbm.1, f32[64,64]{1,0:T(8,128)} %w_mid_hbm.1, f32[64,512]{1,0:T(8,128)} %w_out_hbm.1, ...), custom_call_target="tpu_custom_call" | custom-call | tf_op jit(solution)/shard_map/prep/pallas_call | solution.py:396
  2.4 17.1 %all-to-all-start = ((bf16[64,5,4,128]{3,2,1,0:T(4,128)(2,1)}), bf16[64,5,4,128]{3,2,1,0:T(4,128)(2,1)S(1)}, u32[]{:S(2)}, u32[]{:S(2)}) async-start(bf16[64,5,4,128]{3,2,1,0:T(4,128)(2,1)} %bitcast.11), calls=%async_computation | async-start | bytes 655360 | tf_op jit(solution)/shard_map/all_to_all | solution.py:408
  19.5 0.0 copy-start.1
  19.6 0.9 %copy-done.1 = f32[120,512]{1,0:T(8,128)S(1)} copy-done((f32[120,512]{1,0:T(8,128)S(1)}, f32[120,512]{1,0:T(8,128)}, u32[]{:S(2)}) %copy-start.1) | copy-done | bytes 245784
  20.5 0.4 weights.1
  20.9 2.9 %collective-permute-start = (bf16[512,2048]{1,0:T(8,128)(2,1)}, bf16[512,2048]{1,0:T(8,128)(2,1)}, u32[]{:S(2)}, u32[]{:S(2)}) collective-permute-start(bf16[512,2048]{1,0:T(8,128)(2,1)} %own_ref), channel_id=1, source_target_pairs={{0,1},{1,0},{2,3},{3,2},{4,5},{5,4},{6,7},{7,6},{8,9},{9,8},{10,11... | collective-permute-start | bytes 6291464 | tf_op jit(solution)/shard_map/ppermute | solution.py:418
  23.7 4.3 %filter.1 = (f32[584,256]{1,0:T(8,128)S(1)}, bf16[768,256]{1,0:T(8,128)(2,1)S(1)}) custom-call(f32[8,128]{1,0:T(8,128)S(1)} %get-tuple-element.18.small_ref, bf16[144,256]{1,0:T(8,128)(2,1)S(1)} %get-tuple-element.19.stack_ref), custom_call_target="tpu_custom_call" | custom-call | flops 99999997952 | bytes 1000000000 | tf_op jit(solution)/shard_map/filter/pallas_call | solution.py:419
  28.0 0.0 copy-start
  28.1 5.3 %all-to-all-done = bf16[64,5,4,128]{3,2,1,0:T(4,128)(2,1)S(1)} async-done(((bf16[64,5,4,128]{3,2,1,0:T(4,128)(2,1)}), bf16[64,5,4,128]{3,2,1,0:T(4,128)(2,1)S(1)}, u32[]{:S(2)}, u32[]{:S(2)}) %all-to-all-start) | async-done | bytes 327712 | tf_op jit(solution)/shard_map/all_to_all | solution.py:408
  33.3 0.0 collective-permute-done.other_hbm
  33.3 1.8 %convolve.1 = (bf16[512,128]{1,0:T(8,128)(2,1)S(1)}, bf16[512,2048]{1,0:T(8,128)(2,1)S(1)}) custom-call(bf16[1280,128]{1,0:T(8,128)(2,1)S(1)} %bitcast.7, f32[584,256]{1,0:T(8,128)S(1)} %get-tuple-element.20.wide_ref, bf16[768,256]{1,0:T(8,128)(2,1)S(1)} %get-tuple-element.21.table_ref, bf16[512,2048]{1,0:T(8,128)(2,1)} %collective-permute-done.other_hbm), custom_call_target="tpu_custom_call" | custom-call | tf_op jit(solution)/shard_map/convolve/pallas_call | solution.py:428
  35.2 19.7 %all_to_all.15 = bf16[128,4,128]{2,1,0:T(4,128)(2,1)S(1)} all-to-all(bf16[128,4,128]{2,1,0:T(4,128)(2,1)S(1)} %bitcast.10), channel_id=1, replica_groups={{0,32,16,48,8,40,24,56,256,288,272,304,264,296,280,312,128,160,144,176,..., dimensions={0} | all-to-all | bytes 262144 | tf_op jit(solution)/shard_map/all_to_all | solution.py:440
  54.9 0.0 copy-done
  54.9 0.9 %project.1 = bf16[64,2048]{1,0:T(8,128)(2,1)S(1)} custom-call(bf16[512,128]{1,0:T(8,128)(2,1)S(1)} %bitcast.9, bf16[512,2048]{1,0:T(8,128)(2,1)S(1)} %copy-done, bf16[512,2048]{1,0:T(8,128)(2,1)S(1)} %get-tuple-element.24.other_ref), custom_call_target="tpu_custom_call" | custom-call | tf_op jit(solution)/shard_map/project/pallas_call | solution.py:442
  55.8 9.1 %all_to_all.16 = bf16[4,16,2048]{2,1,0:T(8,128)(2,1)S(1)} all-to-all(bf16[4,16,2048]{2,1,0:T(8,128)(2,1)S(1)} %bitcast.8), channel_id=1, replica_groups={{0,2,6,4},{1,3,7,5},{8,10,14,12},{9,11,15,13},{16,18,22,20},{17,19,23,2..., dimensions={0} | all-to-all | bytes 524288 | tf_op jit(solution)/shard_map/all_to_all | solution.py:449
  64.9 0.7 %reduce_sum.12 = bf16[16,2048]{1,0:T(8,128)(2,1)} reduce(bf16[4,16,2048]{2,1,0:T(8,128)(2,1)S(1)} %all_to_all.16, bf16[]{:T(256)} %constant.2.clone.1), dimensions={0}, to_apply=%region_0.0 | reduce | flops 98304 | bytes 327682 | tf_op jit(solution)/shard_map/reduce_sum | solution.py:451
Async XLA Ops:
  2.4 31.0 %all-to-all-start = ((bf16[64,5,4,128]{3,2,1,0:T(4,128)(2,1)}), bf16[64,5,4,128]{3,2,1,0:T(4,128)(2,1)S(1)}, u32[]{:S(2)}, u32[]{:S(2)}) async-start(bf16[64,5,4,128]{3,2,1,0:T(4,128)(2,1)} %bitcast.11), calls=%async_computation | async-start | bytes 655360 | tf_op jit(solution)/shard_map/all_to_all | solution.py:408
  19.5 0.9 %copy-start.1 = (f32[120,512]{1,0:T(8,128)S(1)}, f32[120,512]{1,0:T(8,128)}, u32[]{:S(2)}) copy-start(f32[120,512]{1,0:T(8,128)} %get-tuple-element.16.pack_ref) | copy-start | bytes 737284
  20.9 12.5 %collective-permute-start = (bf16[512,2048]{1,0:T(8,128)(2,1)}, bf16[512,2048]{1,0:T(8,128)(2,1)}, u32[]{:S(2)}, u32[]{:S(2)}) collective-permute-start(bf16[512,2048]{1,0:T(8,128)(2,1)} %own_ref), channel_id=1, source_target_pairs={{0,1},{1,0},{2,3},{3,2},{4,5},{5,4},{6,7},{7,6},{8,9},{9,8},{10,11... | collective-permute-start | bytes 6291464 | tf_op jit(solution)/shard_map/ppermute | solution.py:418
  28.0 26.9 %copy-start = (bf16[512,2048]{1,0:T(8,128)(2,1)S(1)}, bf16[512,2048]{1,0:T(8,128)(2,1)}, u32[]{:S(2)}) copy-start(bf16[512,2048]{1,0:T(8,128)(2,1)} %own_ref) | copy-start | bytes 6291460

commit v7 on v6

--- a/solution.py
+++ b/solution.py
@@ -20,8 +20,10 @@
 TAPS = 7
 EDGE = TAPS - 1
 PIECE = 20
+FIRST = 13
+SECOND = 11
 UNITS = 64
-CHUNK = 2048
+CHUNK = 4096
 PACK = (0, 64, 88, 96, 104, 112)
 PACK_ROWS = 120
 bf16 = jnp.bfloat16
@@ -29,16 +31,16 @@
 highest = lax.Precision.HIGHEST
 
 
+def first_order():
+    return [FIRST * n % NBLK for n in range(NBLK)]
+
+
 def second_order():
-    order = []
-    for n in range(NBLK):
-        turned = int(format(n, "06b")[::-1], 2)
-        order.append(turned % 8 * 8 + turned // 8)
-    return order
+    return [SECOND * n % NBLK for n in range(NBLK)]
 
 
 def second_place(ctx):
-    return sum((ctx // 2 ** src % 2) * 2 ** dst for src, dst in enumerate((2, 1, 0, 5, 4, 3)))
+    return pow(SECOND, -1, NBLK) * ctx % NBLK
 
 
 def sine_coefs():
@@ -70,11 +72,6 @@
 
 def mm(left, right):
     return jnp.dot(left, right, preferred_element_type=f32)
-
-
-def mm_split(value, top_mat, low_mat):
-    top = value.astype(bf16)
-    return mm(top, top_mat) + mm(top, low_mat)
 
 
 def prep_kernel(query_hbm, key_hbm, value_hbm, w_in_hbm, w_mid_hbm, w_out_hbm, taps_hbm, rate_hbm,
@@ -119,10 +116,15 @@
     copies[3].wait()
     query_even, query_odd = pairs(held[0].astype(f32))
     edges = edge_ref[...].T.reshape(NBLK // 2, CH, BLK)
-    rows = jnp.concatenate([prod_even, query_even, jnp.where(low_half, edges, prod_odd),
-                            jnp.where(low_half, prod_odd, query_odd),
-                            jnp.where(low_half, query_odd, edges)], 1)
-    out_ref[...] = rows.reshape(NBLK * PIECE, BLK).astype(bf16)
+    low = low_half[0]
+    places = [second_place(ctx) for ctx in first_order()]
+    for slot in range(0, NBLK, 4):
+        rows = []
+        for n in (slot, slot + 2):
+            even, odd = places[n] // 2, places[n + 1] // 2
+            rows += [prod_even[even], query_even[even], jnp.where(low, edges[even], prod_odd[odd]),
+                     jnp.where(low, prod_odd[odd], query_odd[odd]), jnp.where(low, query_odd[odd], edges[odd])]
+        out_ref[slot * PIECE:(slot + 4) * PIECE, :] = jnp.concatenate(rows, 0).astype(bf16)
     for copy in copies[4:]:
         copy.wait()
     chans = rate_ref.shape[1]
@@ -149,7 +151,7 @@
         lanes = slice(c * BLK, (c + 1) * BLK)
         re, im = outer[:NBLK, lanes], outer[NBLK:, lanes]
         out.append(jnp.concatenate([re * tw_re - im * tw_im, re * tw_im + im * tw_re], 1))
-    return mm_split(jnp.concatenate(out, 0), mats_ref[0][...], mats_ref[1][...])
+    return mm(jnp.concatenate(out, 0).astype(bf16), mats_ref[...])
 
 
 def views(wide_ref, table_ref):
@@ -157,9 +159,9 @@
     spec = wide_ref.at[0:CH * NBLK]
     tw = [wide_ref.at[CH * NBLK:CH * NBLK + NBLK, n * BLK:(n + 1) * BLK] for n in range(2)]
     par = wide_ref.at[CH * NBLK + NBLK:CH * NBLK + NBLK + CH, 0:BLK]
-    mats = [table_ref.at[n * half:(n + 1) * half] for n in range(2)]
-    first = table_ref.at[2 * half:2 * half + BLK, 0:3 * NBLK]
-    last = [table_ref.at[2 * half + BLK + n * NBLK:2 * half + BLK + (n + 1) * NBLK, 0:3 * NBLK]
+    mats = table_ref.at[0:half]
+    first = table_ref.at[half:half + BLK, 0:3 * NBLK]
+    last = [table_ref.at[half + BLK + n * NBLK:half + BLK + (n + 1) * NBLK, 0:3 * NBLK]
             for n in range(2)]
     return spec, tw, par, mats, first, last
 
@@ -187,7 +189,7 @@
     shape = (BLK, BLK)
     cos, sin = wave((grid(shape, 0) * grid(shape, 1)).astype(f32) / BLK)
     mats = jnp.concatenate([jnp.concatenate([cos, -sin], 1), jnp.concatenate([sin, cos], 1)], 0)
-    mats_ref[0][...], mats_ref[1][...] = split(mats)
+    mats_ref[...] = mats.astype(bf16)
 
 
 def weights_kernel(pack_ref, small_ref, stack_ref):
@@ -255,8 +257,9 @@
         one = sine_turns(mm(w_in, jnp.concatenate([top, low, top], 0)))
         top, low = split(one)
         two = sine_turns(mm(w_mid, jnp.concatenate([top, low, top], 0)))
-        top, low = split(two)
-        shape = mm(w_out, jnp.concatenate([top, low, top], 0))[:CH]
+        top = two.astype(bf16)
+        shape = mm(jnp.concatenate([w_out[:CH, :UNITS], w_out[CH:, 2 * UNITS:]], 0), top)
+        shape = shape[:CH] + shape[CH:]
         taper = gain * jnp.exp(-rate * (lane + float(chunk * CHUNK))) * shape
         for n in range(per_chunk):
             first_row = (chunk * per_chunk + n) * CH
@@ -273,7 +276,7 @@
     swap.start()
     spec_ref, tw_ref, par_ref, mats_ref, first_ref, last_ref = views(wide_ref, table_ref)
     par = par_ref[...]
-    order = second_order()
+    order = first_order()
     sub = lax.broadcasted_iota(jnp.int32, (CH, BLK), 0) < 4
     at_lane = lax.broadcasted_iota(jnp.int32, (CH, BLK), 1)
     raw_ref[0:CH, :] = jnp.zeros((CH, BLK), f32)
@@ -331,7 +334,7 @@
     s_re, s_im = spec[:, :BLK], spec[:, BLK:]
     h_re, h_im = spec_ref[:, :BLK], spec_ref[:, BLK:]
     both = jnp.concatenate([s_re * h_re - s_im * h_im, -(s_re * h_im + s_im * h_re)], 1)
-    back = mm_split(both, mats_ref[0][...], mats_ref[1][...])
+    back = mm(both.astype(bf16), mats_ref[...])
     tw_re, tw_im = tw_ref[0][...], tw_ref[1][...]
     cols = []
     for c in range(CH):
@@ -342,6 +345,7 @@
     conv = mm(last, jnp.concatenate([top, low, top], 0))
     for c in range(CH):
         conv_ref[pl.ds(c, NBLK, stride=CH), :] = conv[:, c * BLK:(c + 1) * BLK]
+    order = second_order()
     same = sub == (at_lane < HALF)
     lane = lax.broadcasted_iota(jnp.int32, (BLK, BLK), 1)
     slot = lane % HALF // SHARE
@@ -406,7 +410,7 @@
         name="prep",
     )(*operands)
     fields = lax.all_to_all(parts.reshape(NBLK, PIECE // 4, 4, BLK), "ctx", 0, 0, tiled=True,
-                            axis_index_groups=[second_order()]).reshape(NBLK * PIECE, BLK)
+                            axis_index_groups=[first_order()]).reshape(NBLK * PIECE, BLK)
     small, stack = pl.pallas_call(
         weights_kernel,
         out_shape=[jax.ShapeDtypeStruct((CH, 128), f32),
@@ -419,7 +423,7 @@
     wide, table = pl.pallas_call(
         filter_kernel,
         out_shape=[jax.ShapeDtypeStruct((CH * NBLK + NBLK + CH, 2 * BLK), f32),
-                   jax.ShapeDtypeStruct((4 * BLK + 2 * BLK, 2 * BLK), bf16)],
+                   jax.ShapeDtypeStruct((4 * BLK, 2 * BLK), bf16)],
         scratch_shapes=[pltpu.VMEM((NBLK * CH, BLK), f32)],
         compiler_params=params,
         cost_estimate=pl.CostEstimate(flops=10**11, bytes_accessed=10**9, transcendentals=10**6),

time: 66.5 us -> 65.9 us (level)
  blocking collectives: 28.8 us -> 29.9 us
  Pallas kernels: 9.78 us -> 9.02 us
  waiting for transfers between devices: 5.3 us -> 4.6 us
    all_to_all x1, blocking collectives: 19.7 us -> 20.9 us  [per_device(): lax.all_to_all(gated.reshape(NBLK * cores, CH // cores, BLK), ('ctx', 'ch...]
    all_to_all x1, waiting for transfers between devices: 5.29 us -> 4.59 us  [per_device(): lax.all_to_all(parts.reshape(NBLK, PIECE // 4, 4, BLK), 'ctx', 0, 0, tile...]
  transfers between devices with their start and end apart: 2 -> 2, of which waited for: 1 -> 1; matrix products, arithmetic and copies ran while one was open for 0% -> 0% of each run, Pallas kernels for 7% -> 6%
where the time goes in v7:
time: 65.9 us; the launch traced here: 65.2 us
  blocking collectives  29.9 us (45%)
  starting transfers between devices  20 us (30%)
  Pallas kernels  9.02 us (14%)
  waiting for transfers between devices  4.6 us (7%)
  local copies, waits for them, and re-layouts  0.94 us (1%)
  other arithmetic  0.67 us (1%)
    all_to_all x1, blocking collectives, per_device(): lax.all_to_all(gated.reshape(NBLK * cores, CH // cores, BLK), ('ctx', 'ch...  20.9 us
    all_to_all x1, starting transfers between devices, per_device(): lax.all_to_all(parts.reshape(NBLK, PIECE // 4, 4, BLK), 'ctx', 0, 0, tile...  17.1 us
    all_to_all x1, blocking collectives, per_device(): lax.all_to_all(partial.reshape(chips, SHARE, dout), 'ch', 0, 0, tiled=Tru...  9.05 us
    all_to_all x1, waiting for transfers between devices, per_device(): lax.all_to_all(parts.reshape(NBLK, PIECE // 4, 4, BLK), 'ctx', 0, 0, tile...  4.59 us
    pallas_call x1, Pallas kernels, per_device(): pl.pallas_call(filter_kernel, out_shape=[jax.ShapeDtypeStruct((CH * NBLK...  3.77 us
    ppermute x1, starting transfers between devices, per_device(): lax.ppermute(own_weight, 'ch', [(d, d ^ 1) for d in range(groups)])  2.86 us
    pallas_call x1, Pallas kernels, per_device(): pl.pallas_call(prep_kernel, out_shape=[jax.ShapeDtypeStruct((NBLK * PIECE...  2.38 us
    pallas_call x1, Pallas kernels, per_device(): pl.pallas_call(conv_kernel, out_shape=[jax.ShapeDtypeStruct((NBLK * CH, B...  1.61 us
  transfers between devices with their start and end apart: 2, of which 1 were waited for; matrix products, arithmetic and copies ran while one was open for 0% of the time, Pallas kernels for 6%

profile of v7, /device:TPU:1, one launch (start us, length us, event | category | flops | bytes accessed | tf_op | source)
XLA Modules:
  0.0 65.2 jit_solution(16755619303064349652)
XLA Ops:
  0.0 2.4 %prep.1 = (bf16[1280,128]{1,0:T(8,128)(2,1)}, f32[120,512]{1,0:T(8,128)}) custom-call(bf16[128,512]{1,0:T(8,128)(2,1)} %query_hbm.1, bf16[128,512]{1,0:T(8,128)(2,1)} %key_hbm.1, bf16[128,512]{1,0:T(8,128)(2,1)} %value_hbm.1, f32[33,64]{1,0:T(8,128)} %w_in_hbm.1, f32[64,64]{1,0:T(8,128)} %w_mid_hbm.1, f32[64,512]{1,0:T(8,128)} %w_out_hbm.1, ...), custom_call_target="tpu_custom_call" | custom-call | tf_op jit(solution)/shard_map/prep/pallas_call | solution.py:400
  2.4 17.1 %all-to-all-start = ((bf16[64,5,4,128]{3,2,1,0:T(4,128)(2,1)}), bf16[64,5,4,128]{3,2,1,0:T(4,128)(2,1)S(1)}, u32[]{:S(2)}, u32[]{:S(2)}) async-start(bf16[64,5,4,128]{3,2,1,0:T(4,128)(2,1)} %bitcast.11), calls=%async_computation | async-start | bytes 655360 | tf_op jit(solution)/shard_map/all_to_all | solution.py:412
  19.5 0.0 copy-start.1
  19.6 0.9 %copy-done.1 = f32[120,512]{1,0:T(8,128)S(1)} copy-done((f32[120,512]{1,0:T(8,128)S(1)}, f32[120,512]{1,0:T(8,128)}, u32[]{:S(2)}) %copy-start.1) | copy-done | bytes 245784
  20.5 0.3 weights.1
  20.8 2.9 %collective-permute-start = (bf16[512,2048]{1,0:T(8,128)(2,1)}, bf16[512,2048]{1,0:T(8,128)(2,1)}, u32[]{:S(2)}, u32[]{:S(2)}) collective-permute-start(bf16[512,2048]{1,0:T(8,128)(2,1)} %own_ref), channel_id=1, source_target_pairs={{0,1},{1,0},{2,3},{3,2},{4,5},{5,4},{6,7},{7,6},{8,9},{9,8},{10,11... | collective-permute-start | bytes 6291464 | tf_op jit(solution)/shard_map/ppermute | solution.py:422
  23.7 3.8 %filter.1 = (f32[584,256]{1,0:T(8,128)S(1)}, bf16[512,256]{1,0:T(8,128)(2,1)S(1)}) custom-call(f32[8,128]{1,0:T(8,128)S(1)} %get-tuple-element.18.small_ref, bf16[144,256]{1,0:T(8,128)(2,1)S(1)} %get-tuple-element.19.stack_ref), custom_call_target="tpu_custom_call" | custom-call | flops 99999997952 | bytes 1000000000 | tf_op jit(solution)/shard_map/filter/pallas_call | solution.py:423
  27.5 0.0 copy-start
  27.5 4.6 %all-to-all-done = bf16[64,5,4,128]{3,2,1,0:T(4,128)(2,1)S(1)} async-done(((bf16[64,5,4,128]{3,2,1,0:T(4,128)(2,1)}), bf16[64,5,4,128]{3,2,1,0:T(4,128)(2,1)S(1)}, u32[]{:S(2)}, u32[]{:S(2)}) %all-to-all-start) | async-done | bytes 327712 | tf_op jit(solution)/shard_map/all_to_all | solution.py:412
  32.1 0.0 collective-permute-done.other_hbm
  32.1 1.6 %convolve.1 = (bf16[512,128]{1,0:T(8,128)(2,1)S(1)}, bf16[512,2048]{1,0:T(8,128)(2,1)S(1)}) custom-call(bf16[1280,128]{1,0:T(8,128)(2,1)S(1)} %bitcast.7, f32[584,256]{1,0:T(8,128)S(1)} %get-tuple-element.20.wide_ref, bf16[512,256]{1,0:T(8,128)(2,1)S(1)} %get-tuple-element.21.table_ref, bf16[512,2048]{1,0:T(8,128)(2,1)} %collective-permute-done.other_hbm), custom_call_target="tpu_custom_call" | custom-call | tf_op jit(solution)/shard_map/convolve/pallas_call | solution.py:432
  33.7 20.9 %all_to_all.15 = bf16[128,4,128]{2,1,0:T(4,128)(2,1)S(1)} all-to-all(bf16[128,4,128]{2,1,0:T(4,128)(2,1)S(1)} %bitcast.10), channel_id=1, replica_groups={{0,88,176,264,352,440,16,104,192,280,368,456,32,120,208,296,384,472,48,..., dimensions={0} | all-to-all | bytes 262144 | tf_op jit(solution)/shard_map/all_to_all | solution.py:444
  54.6 0.0 copy-done
  54.6 0.9 %project.1 = bf16[64,2048]{1,0:T(8,128)(2,1)S(1)} custom-call(bf16[512,128]{1,0:T(8,128)(2,1)S(1)} %bitcast.9, bf16[512,2048]{1,0:T(8,128)(2,1)S(1)} %copy-done, bf16[512,2048]{1,0:T(8,128)(2,1)S(1)} %get-tuple-element.24.other_ref), custom_call_target="tpu_custom_call" | custom-call | tf_op jit(solution)/shard_map/project/pallas_call | solution.py:446
  55.5 9.1 %all_to_all.16 = bf16[4,16,2048]{2,1,0:T(8,128)(2,1)S(1)} all-to-all(bf16[4,16,2048]{2,1,0:T(8,128)(2,1)S(1)} %bitcast.8), channel_id=1, replica_groups={{0,2,6,4},{1,3,7,5},{8,10,14,12},{9,11,15,13},{16,18,22,20},{17,19,23,2..., dimensions={0} | all-to-all | bytes 524288 | tf_op jit(solution)/shard_map/all_to_all | solution.py:453
  64.6 0.7 %reduce_sum.12 = bf16[16,2048]{1,0:T(8,128)(2,1)} reduce(bf16[4,16,2048]{2,1,0:T(8,128)(2,1)S(1)} %all_to_all.16, bf16[]{:T(256)} %constant.2.clone.1), dimensions={0}, to_apply=%region_0.0 | reduce | flops 98304 | bytes 327682 | tf_op jit(solution)/shard_map/reduce_sum | solution.py:455
Async XLA Ops:
  2.4 29.7 %all-to-all-start = ((bf16[64,5,4,128]{3,2,1,0:T(4,128)(2,1)}), bf16[64,5,4,128]{3,2,1,0:T(4,128)(2,1)S(1)}, u32[]{:S(2)}, u32[]{:S(2)}) async-start(bf16[64,5,4,128]{3,2,1,0:T(4,128)(2,1)} %bitcast.11), calls=%async_computation | async-start | bytes 655360 | tf_op jit(solution)/shard_map/all_to_all | solution.py:412
  19.5 0.9 %copy-start.1 = (f32[120,512]{1,0:T(8,128)S(1)}, f32[120,512]{1,0:T(8,128)}, u32[]{:S(2)}) copy-start(f32[120,512]{1,0:T(8,128)} %get-tuple-element.16.pack_ref) | copy-start | bytes 737284
  20.8 11.3 %collective-permute-start = (bf16[512,2048]{1,0:T(8,128)(2,1)}, bf16[512,2048]{1,0:T(8,128)(2,1)}, u32[]{:S(2)}, u32[]{:S(2)}) collective-permute-start(bf16[512,2048]{1,0:T(8,128)(2,1)} %own_ref), channel_id=1, source_target_pairs={{0,1},{1,0},{2,3},{3,2},{4,5},{5,4},{6,7},{7,6},{8,9},{9,8},{10,11... | collective-permute-start | bytes 6291464 | tf_op jit(solution)/shard_map/ppermute | solution.py:422
  27.5 27.1 %copy-start = (bf16[512,2048]{1,0:T(8,128)(2,1)S(1)}, bf16[512,2048]{1,0:T(8,128)(2,1)}, u32[]{:S(2)}) copy-start(bf16[512,2048]{1,0:T(8,128)(2,1)} %own_ref) | copy-start | bytes 6291460

commit v8 on v7

--- a/solution.py
+++ b/solution.py
@@ -143,8 +143,8 @@
 
 def forward(rows_ref, first_ref, tw_ref, mats_ref):
     cols = jnp.concatenate([rows_ref[pl.ds(c, NBLK, stride=CH), :] for c in range(CH)], 1)
-    top, low = split(cols)
-    outer = mm(first_ref[...], jnp.concatenate([top, low, top], 0))
+    top = cols.astype(bf16)
+    outer = mm(first_ref[...], jnp.concatenate([top, top], 0))
     tw_re, tw_im = tw_ref[0][...], tw_ref[1][...]
     out = []
     for c in range(CH):
@@ -160,9 +160,8 @@
     tw = [wide_ref.at[CH * NBLK:CH * NBLK + NBLK, n * BLK:(n + 1) * BLK] for n in range(2)]
     par = wide_ref.at[CH * NBLK + NBLK:CH * NBLK + NBLK + CH, 0:BLK]
     mats = table_ref.at[0:half]
-    first = table_ref.at[half:half + BLK, 0:3 * NBLK]
-    last = [table_ref.at[half + BLK + n * NBLK:half + BLK + (n + 1) * NBLK, 0:3 * NBLK]
-            for n in range(2)]
+    first = table_ref.at[half:half + BLK, 0:2 * NBLK]
+    last = table_ref.at[half + BLK:half + BLK + NBLK, 0:4 * NBLK]
     return spec, tw, par, mats, first, last
 
 
@@ -177,11 +176,10 @@
     shape = (NBLK, NBLK)
     cos, sin = wave((grid(shape, 0).astype(f32) - 0.25) * grid(shape, 1).astype(f32) / NBLK)
     top, low = split(jnp.concatenate([cos, -sin], 0))
-    first_ref[...] = jnp.concatenate([top, top, low], 1)
+    first_ref[...] = jnp.concatenate([top, low], 1)
     cos, sin = wave((grid(shape, 1).astype(f32) - 0.25) * grid(shape, 0).astype(f32) / NBLK)
     top, low = split(jnp.concatenate([cos, -sin], 1) / TOKENS)
-    wide = jnp.concatenate([top, top, low], 1)
-    last_ref[0][...], last_ref[1][...] = wide[:, :3 * NBLK], wide[:, 3 * NBLK:]
+    last_ref[...] = jnp.concatenate([top, low], 1)
     shape = (NBLK, BLK)
     shifted = grid(shape, 0).astype(f32) - 0.25
     cos, sin = wave(shifted * grid(shape, 1).astype(f32) / TOKENS)
@@ -340,9 +338,8 @@
     for c in range(CH):
         re, im = back[c * NBLK:(c + 1) * NBLK, :BLK], back[c * NBLK:(c + 1) * NBLK, BLK:]
         cols.append(jnp.concatenate([re * tw_re - im * tw_im, -(re * tw_im + im * tw_re)], 0))
-    top, low = split(jnp.concatenate(cols, 1))
-    last = jnp.concatenate([last_ref[0][...], last_ref[1][...]], 1)
-    conv = mm(last, jnp.concatenate([top, low, top], 0))
+    top = jnp.concatenate(cols, 1).astype(bf16)
+    conv = mm(last_ref[...], jnp.concatenate([top, top], 0))
     for c in range(CH):
         conv_ref[pl.ds(c, NBLK, stride=CH), :] = conv[:, c * BLK:(c + 1) * BLK]
     order = second_order()

time: 65.9 us -> 65.9 us (level)
  no operation moved by 1% of the time
where the time goes in v8:
time: 65.9 us; the launch traced here: 65.2 us
  blocking collectives  29.9 us (45%)
  starting transfers between devices  20 us (30%)
  Pallas kernels  9.01 us (14%)
  waiting for transfers between devices  4.61 us (7%)
  local copies, waits for them, and re-layouts  0.94 us (1%)
  other arithmetic  0.67 us (1%)
    all_to_all x1, blocking collectives, per_device(): lax.all_to_all(gated.reshape(NBLK * cores, CH // cores, BLK), ('ctx', 'ch...  20.9 us
    all_to_all x1, starting transfers between devices, per_device(): lax.all_to_all(parts.reshape(NBLK, PIECE // 4, 4, BLK), 'ctx', 0, 0, tile...  17.1 us
    all_to_all x1, blocking collectives, per_device(): lax.all_to_all(partial.reshape(chips, SHARE, dout), 'ch', 0, 0, tiled=Tru...  9.05 us
    all_to_all x1, waiting for transfers between devices, per_device(): lax.all_to_all(parts.reshape(NBLK, PIECE // 4, 4, BLK), 'ctx', 0, 0, tile...  4.6 us
    pallas_call x1, Pallas kernels, per_device(): pl.pallas_call(filter_kernel, out_shape=[jax.ShapeDtypeStruct((CH * NBLK...  3.76 us
    ppermute x1, starting transfers between devices, per_device(): lax.ppermute(own_weight, 'ch', [(d, d ^ 1) for d in range(groups)])  2.86 us
    pallas_call x1, Pallas kernels, per_device(): pl.pallas_call(prep_kernel, out_shape=[jax.ShapeDtypeStruct((NBLK * PIECE...  2.38 us
    pallas_call x1, Pallas kernels, per_device(): pl.pallas_call(conv_kernel, out_shape=[jax.ShapeDtypeStruct((NBLK * CH, B...  1.61 us
  transfers between devices with their start and end apart: 2, of which 1 were waited for; matrix products, arithmetic and copies ran while one was open for 0% of the time, Pallas kernels for 6%

profile of v8, /device:TPU:1, one launch (start us, length us, event | category | flops | bytes accessed | tf_op | source)
XLA Modules:
  0.0 65.2 jit_solution(14709880083526883135)
XLA Ops:
  0.0 2.4 %prep.1 = (bf16[1280,128]{1,0:T(8,128)(2,1)}, f32[120,512]{1,0:T(8,128)}) custom-call(bf16[128,512]{1,0:T(8,128)(2,1)} %query_hbm.1, bf16[128,512]{1,0:T(8,128)(2,1)} %key_hbm.1, bf16[128,512]{1,0:T(8,128)(2,1)} %value_hbm.1, f32[33,64]{1,0:T(8,128)} %w_in_hbm.1, f32[64,64]{1,0:T(8,128)} %w_mid_hbm.1, f32[64,512]{1,0:T(8,128)} %w_out_hbm.1, ...), custom_call_target="tpu_custom_call" | custom-call | tf_op jit(solution)/shard_map/prep/pallas_call | solution.py:397
  2.4 17.1 %all-to-all-start = ((bf16[64,5,4,128]{3,2,1,0:T(4,128)(2,1)}), bf16[64,5,4,128]{3,2,1,0:T(4,128)(2,1)S(1)}, u32[]{:S(2)}, u32[]{:S(2)}) async-start(bf16[64,5,4,128]{3,2,1,0:T(4,128)(2,1)} %bitcast.11), calls=%async_computation | async-start | bytes 655360 | tf_op jit(solution)/shard_map/all_to_all | solution.py:409
  19.5 0.0 copy-start.1
  19.6 0.9 %copy-done.1 = f32[120,512]{1,0:T(8,128)S(1)} copy-done((f32[120,512]{1,0:T(8,128)S(1)}, f32[120,512]{1,0:T(8,128)}, u32[]{:S(2)}) %copy-start.1) | copy-done | bytes 245784
  20.5 0.3 weights.1
  20.8 2.9 %collective-permute-start = (bf16[512,2048]{1,0:T(8,128)(2,1)}, bf16[512,2048]{1,0:T(8,128)(2,1)}, u32[]{:S(2)}, u32[]{:S(2)}) collective-permute-start(bf16[512,2048]{1,0:T(8,128)(2,1)} %own_ref), channel_id=1, source_target_pairs={{0,1},{1,0},{2,3},{3,2},{4,5},{5,4},{6,7},{7,6},{8,9},{9,8},{10,11... | collective-permute-start | bytes 6291464 | tf_op jit(solution)/shard_map/ppermute | solution.py:419
  23.7 3.8 %filter.1 = (f32[584,256]{1,0:T(8,128)S(1)}, bf16[512,256]{1,0:T(8,128)(2,1)S(1)}) custom-call(f32[8,128]{1,0:T(8,128)S(1)} %get-tuple-element.18.small_ref, bf16[144,256]{1,0:T(8,128)(2,1)S(1)} %get-tuple-element.19.stack_ref), custom_call_target="tpu_custom_call" | custom-call | flops 99999997952 | bytes 1000000000 | tf_op jit(solution)/shard_map/filter/pallas_call | solution.py:420
  27.5 0.0 copy-start
  27.5 4.6 %all-to-all-done = bf16[64,5,4,128]{3,2,1,0:T(4,128)(2,1)S(1)} async-done(((bf16[64,5,4,128]{3,2,1,0:T(4,128)(2,1)}), bf16[64,5,4,128]{3,2,1,0:T(4,128)(2,1)S(1)}, u32[]{:S(2)}, u32[]{:S(2)}) %all-to-all-start) | async-done | bytes 327712 | tf_op jit(solution)/shard_map/all_to_all | solution.py:409
  32.1 0.0 collective-permute-done.other_hbm
  32.1 1.6 %convolve.1 = (bf16[512,128]{1,0:T(8,128)(2,1)S(1)}, bf16[512,2048]{1,0:T(8,128)(2,1)S(1)}) custom-call(bf16[1280,128]{1,0:T(8,128)(2,1)S(1)} %bitcast.7, f32[584,256]{1,0:T(8,128)S(1)} %get-tuple-element.20.wide_ref, bf16[512,256]{1,0:T(8,128)(2,1)S(1)} %get-tuple-element.21.table_ref, bf16[512,2048]{1,0:T(8,128)(2,1)} %collective-permute-done.other_hbm), custom_call_target="tpu_custom_call" | custom-call | tf_op jit(solution)/shard_map/convolve/pallas_call | solution.py:429
  33.7 20.9 %all_to_all.15 = bf16[128,4,128]{2,1,0:T(4,128)(2,1)S(1)} all-to-all(bf16[128,4,128]{2,1,0:T(4,128)(2,1)S(1)} %bitcast.10), channel_id=1, replica_groups={{0,88,176,264,352,440,16,104,192,280,368,456,32,120,208,296,384,472,48,..., dimensions={0} | all-to-all | bytes 262144 | tf_op jit(solution)/shard_map/all_to_all | solution.py:441
  54.6 0.0 copy-done
  54.6 0.9 %project.1 = bf16[64,2048]{1,0:T(8,128)(2,1)S(1)} custom-call(bf16[512,128]{1,0:T(8,128)(2,1)S(1)} %bitcast.9, bf16[512,2048]{1,0:T(8,128)(2,1)S(1)} %copy-done, bf16[512,2048]{1,0:T(8,128)(2,1)S(1)} %get-tuple-element.24.other_ref), custom_call_target="tpu_custom_call" | custom-call | tf_op jit(solution)/shard_map/project/pallas_call | solution.py:443
  55.5 9.1 %all_to_all.16 = bf16[4,16,2048]{2,1,0:T(8,128)(2,1)S(1)} all-to-all(bf16[4,16,2048]{2,1,0:T(8,128)(2,1)S(1)} %bitcast.8), channel_id=1, replica_groups={{0,2,6,4},{1,3,7,5},{8,10,14,12},{9,11,15,13},{16,18,22,20},{17,19,23,2..., dimensions={0} | all-to-all | bytes 524288 | tf_op jit(solution)/shard_map/all_to_all | solution.py:450
  64.6 0.7 %reduce_sum.12 = bf16[16,2048]{1,0:T(8,128)(2,1)} reduce(bf16[4,16,2048]{2,1,0:T(8,128)(2,1)S(1)} %all_to_all.16, bf16[]{:T(256)} %constant.2.clone.1), dimensions={0}, to_apply=%region_0.0 | reduce | flops 98304 | bytes 327682 | tf_op jit(solution)/shard_map/reduce_sum | solution.py:452
Async XLA Ops:
  2.4 29.7 %all-to-all-start = ((bf16[64,5,4,128]{3,2,1,0:T(4,128)(2,1)}), bf16[64,5,4,128]{3,2,1,0:T(4,128)(2,1)S(1)}, u32[]{:S(2)}, u32[]{:S(2)}) async-start(bf16[64,5,4,128]{3,2,1,0:T(4,128)(2,1)} %bitcast.11), calls=%async_computation | async-start | bytes 655360 | tf_op jit(solution)/shard_map/all_to_all | solution.py:409
  19.5 0.9 %copy-start.1 = (f32[120,512]{1,0:T(8,128)S(1)}, f32[120,512]{1,0:T(8,128)}, u32[]{:S(2)}) copy-start(f32[120,512]{1,0:T(8,128)} %get-tuple-element.16.pack_ref) | copy-start | bytes 737284
  20.8 11.3 %collective-permute-start = (bf16[512,2048]{1,0:T(8,128)(2,1)}, bf16[512,2048]{1,0:T(8,128)(2,1)}, u32[]{:S(2)}, u32[]{:S(2)}) collective-permute-start(bf16[512,2048]{1,0:T(8,128)(2,1)} %own_ref), channel_id=1, source_target_pairs={{0,1},{1,0},{2,3},{3,2},{4,5},{5,4},{6,7},{7,6},{8,9},{9,8},{10,11... | collective-permute-start | bytes 6291464 | tf_op jit(solution)/shard_map/ppermute | solution.py:419
  27.5 27.1 %copy-start = (bf16[512,2048]{1,0:T(8,128)(2,1)S(1)}, bf16[512,2048]{1,0:T(8,128)(2,1)}, u32[]{:S(2)}) copy-start(bf16[512,2048]{1,0:T(8,128)(2,1)} %own_ref) | copy-start | bytes 6291460

commit v9 on v7

--- a/solution.py
+++ b/solution.py
@@ -21,7 +21,7 @@
 EDGE = TAPS - 1
 PIECE = 20
 FIRST = 13
-SECOND = 11
+SECOND = 43
 UNITS = 64
 CHUNK = 4096
 PACK = (0, 64, 88, 96, 104, 112)

time: 65.9 us -> 66.1 us (level)
  no operation moved by 1% of the time
where the time goes in v9:
time: 66.1 us; the launch traced here: 65.3 us
  blocking collectives  29.9 us (45%)
  starting transfers between devices  20 us (30%)
  Pallas kernels  9.02 us (14%)
  waiting for transfers between devices  4.6 us (7%)
  local copies, waits for them, and re-layouts  0.94 us (1%)
  other arithmetic  0.67 us (1%)
    all_to_all x1, blocking collectives, per_device(): lax.all_to_all(gated.reshape(NBLK * cores, CH // cores, BLK), ('ctx', 'ch...  20.9 us
    all_to_all x1, starting transfers between devices, per_device(): lax.all_to_all(parts.reshape(NBLK, PIECE // 4, 4, BLK), 'ctx', 0, 0, tile...  17.1 us
    all_to_all x1, blocking collectives, per_device(): lax.all_to_all(partial.reshape(chips, SHARE, dout), 'ch', 0, 0, tiled=Tru...  9.05 us
    all_to_all x1, waiting for transfers between devices, per_device(): lax.all_to_all(parts.reshape(NBLK, PIECE // 4, 4, BLK), 'ctx', 0, 0, tile...  4.59 us
    pallas_call x1, Pallas kernels, per_device(): pl.pallas_call(filter_kernel, out_shape=[jax.ShapeDtypeStruct((CH * NBLK...  3.77 us
    ppermute x1, starting transfers between devices, per_device(): lax.ppermute(own_weight, 'ch', [(d, d ^ 1) for d in range(groups)])  2.86 us
    pallas_call x1, Pallas kernels, per_device(): pl.pallas_call(prep_kernel, out_shape=[jax.ShapeDtypeStruct((NBLK * PIECE...  2.38 us
    pallas_call x1, Pallas kernels, per_device(): pl.pallas_call(conv_kernel, out_shape=[jax.ShapeDtypeStruct((NBLK * CH, B...  1.61 us
  transfers between devices with their start and end apart: 2, of which 1 were waited for; matrix products, arithmetic and copies ran while one was open for 0% of the time, Pallas kernels for 6%

profile of v9, /device:TPU:1, one launch (start us, length us, event | category | flops | bytes accessed | tf_op | source)
XLA Modules:
  0.0 65.3 jit_solution(16719603921359745969)
XLA Ops:
  0.0 2.4 %prep.1 = (bf16[1280,128]{1,0:T(8,128)(2,1)}, f32[120,512]{1,0:T(8,128)}) custom-call(bf16[128,512]{1,0:T(8,128)(2,1)} %query_hbm.1, bf16[128,512]{1,0:T(8,128)(2,1)} %key_hbm.1, bf16[128,512]{1,0:T(8,128)(2,1)} %value_hbm.1, f32[33,64]{1,0:T(8,128)} %w_in_hbm.1, f32[64,64]{1,0:T(8,128)} %w_mid_hbm.1, f32[64,512]{1,0:T(8,128)} %w_out_hbm.1, ...), custom_call_target="tpu_custom_call" | custom-call | tf_op jit(solution)/shard_map/prep/pallas_call | solution.py:400
  2.4 17.1 %all-to-all-start = ((bf16[64,5,4,128]{3,2,1,0:T(4,128)(2,1)}), bf16[64,5,4,128]{3,2,1,0:T(4,128)(2,1)S(1)}, u32[]{:S(2)}, u32[]{:S(2)}) async-start(bf16[64,5,4,128]{3,2,1,0:T(4,128)(2,1)} %bitcast.11), calls=%async_computation | async-start | bytes 655360 | tf_op jit(solution)/shard_map/all_to_all | solution.py:412
  19.5 0.0 copy-start.1
  19.6 0.9 %copy-done.1 = f32[120,512]{1,0:T(8,128)S(1)} copy-done((f32[120,512]{1,0:T(8,128)S(1)}, f32[120,512]{1,0:T(8,128)}, u32[]{:S(2)}) %copy-start.1) | copy-done | bytes 245784
  20.5 0.3 weights.1
  20.8 2.9 %collective-permute-start = (bf16[512,2048]{1,0:T(8,128)(2,1)}, bf16[512,2048]{1,0:T(8,128)(2,1)}, u32[]{:S(2)}, u32[]{:S(2)}) collective-permute-start(bf16[512,2048]{1,0:T(8,128)(2,1)} %own_ref), channel_id=1, source_target_pairs={{0,1},{1,0},{2,3},{3,2},{4,5},{5,4},{6,7},{7,6},{8,9},{9,8},{10,11... | collective-permute-start | bytes 6291464 | tf_op jit(solution)/shard_map/ppermute | solution.py:422
  23.7 3.8 %filter.1 = (f32[584,256]{1,0:T(8,128)S(1)}, bf16[512,256]{1,0:T(8,128)(2,1)S(1)}) custom-call(f32[8,128]{1,0:T(8,128)S(1)} %get-tuple-element.18.small_ref, bf16[144,256]{1,0:T(8,128)(2,1)S(1)} %get-tuple-element.19.stack_ref), custom_call_target="tpu_custom_call" | custom-call | flops 99999997952 | bytes 1000000000 | tf_op jit(solution)/shard_map/filter/pallas_call | solution.py:423
  27.5 0.0 copy-start
  27.5 4.6 %all-to-all-done = bf16[64,5,4,128]{3,2,1,0:T(4,128)(2,1)S(1)} async-done(((bf16[64,5,4,128]{3,2,1,0:T(4,128)(2,1)}), bf16[64,5,4,128]{3,2,1,0:T(4,128)(2,1)S(1)}, u32[]{:S(2)}, u32[]{:S(2)}) %all-to-all-start) | async-done | bytes 327712 | tf_op jit(solution)/shard_map/all_to_all | solution.py:412
  32.1 0.0 collective-permute-done.other_hbm
  32.1 1.6 %convolve.1 = (bf16[512,128]{1,0:T(8,128)(2,1)S(1)}, bf16[512,2048]{1,0:T(8,128)(2,1)S(1)}) custom-call(bf16[1280,128]{1,0:T(8,128)(2,1)S(1)} %bitcast.7, f32[584,256]{1,0:T(8,128)S(1)} %get-tuple-element.20.wide_ref, bf16[512,256]{1,0:T(8,128)(2,1)S(1)} %get-tuple-element.21.table_ref, bf16[512,2048]{1,0:T(8,128)(2,1)} %collective-permute-done.other_hbm), custom_call_target="tpu_custom_call" | custom-call | tf_op jit(solution)/shard_map/convolve/pallas_call | solution.py:432
  33.7 20.9 %all_to_all.15 = bf16[128,4,128]{2,1,0:T(4,128)(2,1)S(1)} all-to-all(bf16[128,4,128]{2,1,0:T(4,128)(2,1)S(1)} %bitcast.10), channel_id=1, replica_groups={{0,344,176,8,352,184,16,360,192,24,368,200,32,376,208,40,384,216,48,392..., dimensions={0} | all-to-all | bytes 262144 | tf_op jit(solution)/shard_map/all_to_all | solution.py:444
  54.6 0.0 copy-done
  54.6 0.9 %project.1 = bf16[64,2048]{1,0:T(8,128)(2,1)S(1)} custom-call(bf16[512,128]{1,0:T(8,128)(2,1)S(1)} %bitcast.9, bf16[512,2048]{1,0:T(8,128)(2,1)S(1)} %copy-done, bf16[512,2048]{1,0:T(8,128)(2,1)S(1)} %get-tuple-element.24.other_ref), custom_call_target="tpu_custom_call" | custom-call | tf_op jit(solution)/shard_map/project/pallas_call | solution.py:446
  55.5 9.0 %all_to_all.16 = bf16[4,16,2048]{2,1,0:T(8,128)(2,1)S(1)} all-to-all(bf16[4,16,2048]{2,1,0:T(8,128)(2,1)S(1)} %bitcast.8), channel_id=1, replica_groups={{0,2,6,4},{1,3,7,5},{8,10,14,12},{9,11,15,13},{16,18,22,20},{17,19,23,2..., dimensions={0} | all-to-all | bytes 524288 | tf_op jit(solution)/shard_map/all_to_all | solution.py:453
  64.6 0.7 %reduce_sum.12 = bf16[16,2048]{1,0:T(8,128)(2,1)} reduce(bf16[4,16,2048]{2,1,0:T(8,128)(2,1)S(1)} %all_to_all.16, bf16[]{:T(256)} %constant.2.clone.1), dimensions={0}, to_apply=%region_0.0 | reduce | flops 98304 | bytes 327682 | tf_op jit(solution)/shard_map/reduce_sum | solution.py:455
Async XLA Ops:
  2.4 29.7 %all-to-all-start = ((bf16[64,5,4,128]{3,2,1,0:T(4,128)(2,1)}), bf16[64,5,4,128]{3,2,1,0:T(4,128)(2,1)S(1)}, u32[]{:S(2)}, u32[]{:S(2)}) async-start(bf16[64,5,4,128]{3,2,1,0:T(4,128)(2,1)} %bitcast.11), calls=%async_computation | async-start | bytes 655360 | tf_op jit(solution)/shard_map/all_to_all | solution.py:412
  19.5 0.9 %copy-start.1 = (f32[120,512]{1,0:T(8,128)S(1)}, f32[120,512]{1,0:T(8,128)}, u32[]{:S(2)}) copy-start(f32[120,512]{1,0:T(8,128)} %get-tuple-element.16.pack_ref) | copy-start | bytes 737284
  20.8 11.3 %collective-permute-start = (bf16[512,2048]{1,0:T(8,128)(2,1)}, bf16[512,2048]{1,0:T(8,128)(2,1)}, u32[]{:S(2)}, u32[]{:S(2)}) collective-permute-start(bf16[512,2048]{1,0:T(8,128)(2,1)} %own_ref), channel_id=1, source_target_pairs={{0,1},{1,0},{2,3},{3,2},{4,5},{5,4},{6,7},{7,6},{8,9},{9,8},{10,11... | collective-permute-start | bytes 6291464 | tf_op jit(solution)/shard_map/ppermute | solution.py:422
  27.5 27.1 %copy-start = (bf16[512,2048]{1,0:T(8,128)(2,1)S(1)}, bf16[512,2048]{1,0:T(8,128)(2,1)}, u32[]{:S(2)}) copy-start(bf16[512,2048]{1,0:T(8,128)(2,1)} %own_ref) | copy-start | bytes 6291460
